TPU v7x, 32 devices: a whole 2x2x4 slice. The times are simulated.
32 devices in a mesh: gx: 4 (over y, core), gy: 8 (over z, x).
Axes of the slice: x: 2, y: 2, z: 4, core: 2. Of those that a mesh axis runs over, the one named last changes fastest.
Arguments:
- first_lame: float32 [256, 4096], P('gx', 'gy'), may hold values from 1 to 10
- shear_modulus: float32 [256, 4096], P('gx', 'gy'), may hold values from 1 to 10
- applied_load: float32 [2, 256, 4096], P(None, 'gx', 'gy'), may hold values from -12 to 12
- plastic_owner: int32 [16384, 1], P(('gx', 'gy')), may hold values from 0 to 31; in each aligned block of 512 rows (0 to 511, 512 to 1023, ...) at most 32 rows name the same one
- plastic_cell: int32 [16384], P(('gx', 'gy')), may hold values from 0 to 32767
- plastic_code: int32 [16384], P(('gx', 'gy')), may hold values from 0 to 3
Outputs:
- displacement: float32 [2, 256, 4096], P(None, 'gx', 'gy')
Inputs may be any that keep to these rules, and one draw needn't show every extreme that they name: `plastic_owner`: owners are numbered row-major over (gx, gy). In each aligned block of 512 entries (the list of one device) no owner is named more than 32 times, a bound that some block reaches. `plastic_cell`: Row-major position within the owner's 64 x 512 block; a cell may be listed several times. `plastic_code`: code 0 marks a padding entry. An entry's owner, cell and code may travel together as one number, ((owner * 64 * 512) + cell) * 4 + code.
All inputs are finite; a program needn't handle non-finite values.
Results may differ from a plain program's by a relative error of at most 0.00011.
Values sent between devices are 32-bit elements; how exact they have to be, the bound alone decides.
No kernel may reach another device: no remote copies, remote signals or barrier semaphores. Data moves between devices by JAX's collectives and lax.ppermute only.
A program may use at most 128 MiB of HBM per device.

v0:
```python
import functools
import math

import jax
import jax.numpy as jnp
import numpy as np
from jax import lax
from jax.sharding import PartitionSpec as P

LEVELS = 3
SWEEPS = 2
COARSE_SWEEPS = 6


DAMPING = 0.5
YIELD_DROP = 0.6
HIGHEST = lax.Precision.HIGHEST
ELEMENT_NODES = ((0, 0), (1, 0), (0, 1), (1, 1))


def passed_along(array, axis, by):
    devices = lax.axis_size(axis)
    pairs = [(i, i + by) for i in range(devices) if 0 <= i + by < devices]
    return lax.ppermute(array, axis, pairs)


def element_tables():
    gauss_points = (0.5 - 0.5 / math.sqrt(3.0), 0.5 + 0.5 / math.sqrt(3.0))
    scale_rows = np.array([2.0, 2.0, 1.0])
    volumetric = np.zeros((8, 8))
    deviatoric = np.zeros((8, 8))
    for coord_row in gauss_points:
        for coord_col in gauss_points:
            strain = np.zeros((3, 8))
            for corner, (row_step, col_step) in enumerate(ELEMENT_NODES):
                shape_row = coord_row if row_step else 1.0 - coord_row
                shape_col = coord_col if col_step else 1.0 - coord_col
                slope_row = (1.0 if row_step else -1.0) * shape_col
                slope_col = (1.0 if col_step else -1.0) * shape_row
                strain[0, 2 * corner] = slope_row
                strain[1, 2 * corner + 1] = slope_col
                strain[2, 2 * corner] = slope_col
                strain[2, 2 * corner + 1] = slope_row
            trace_row = strain[0] + strain[1]
            volumetric = volumetric + 0.25 * np.outer(trace_row, trace_row)
            deviatoric = deviatoric + 0.25 * np.dot(strain.T, scale_rows[:, None] * strain)
    first_map = np.zeros((64, 8))
    second_map = np.zeros((64, 256))
    for sub_row in (0, 1):
        for sub_col in (0, 1):
            interp = np.zeros((8, 8))
            for corner, (row_step, col_step) in enumerate(ELEMENT_NODES):
                place_row = 0.5 * (sub_row + row_step)
                place_col = 0.5 * (sub_col + col_step)
                for source_corner, (src_row, src_col) in enumerate(ELEMENT_NODES):
                    weight = (place_row if src_row else 1.0 - place_row) * (
                        place_col if src_col else 1.0 - place_col
                    )
                    interp[2 * corner, 2 * source_corner] = weight
                    interp[2 * corner + 1, 2 * source_corner + 1] = weight
            subcell = sub_row * 2 + sub_col
            first_map[:, 2 * subcell] = np.dot(interp.T, np.dot(volumetric, interp)).reshape(64)
            first_map[:, 2 * subcell + 1] = np.dot(interp.T, np.dot(deviatoric, interp)).reshape(64)
            paired = np.outer(interp.T, interp.T).reshape(8, 8, 8, 8).transpose(0, 2, 1, 3)
            second_map[:, 64 * subcell : 64 * subcell + 64] = paired.reshape(64, 64)
    return (
        jnp.asarray(volumetric, jnp.float32),
        jnp.asarray(deviatoric, jnp.float32),
        jnp.asarray(first_map, jnp.float32),
        jnp.asarray(second_map, jnp.float32),
    )


def element_dofs(extended):
    row_count = extended.shape[1] - 1
    column_count = extended.shape[2] - 1
    return jnp.stack(
        [
            extended[component, row_step : row_step + row_count, col_step : col_step + column_count]
            for row_step, col_step in ELEMENT_NODES
            for component in (0, 1)
        ]
    )


def element_scatter(values):
    padded = None
    for corner, (row_step, col_step) in enumerate(ELEMENT_NODES):
        placed = jnp.pad(
            values[2 * corner : 2 * corner + 2],
            ((0, 0), (row_step, 1 - row_step), (col_step, 1 - col_step)),
        )
        padded = placed if padded is None else padded + placed
    return padded


def extend(field):
    column = passed_along(field[:, :, :1], "gy", -1)
    wider = jnp.concatenate([field, column], axis=2)
    upper_row = passed_along(wider[:, :1, :], "gx", -1)
    return jnp.concatenate([wider, upper_row], axis=1)


def assemble(padded):
    spill_row = passed_along(padded[:, -1:, :], "gx", 1)
    folded = jnp.concatenate([padded[:, :1, :] + spill_row, padded[:, 1:-1, :]], axis=1)
    spill_column = passed_along(folded[:, :, -1:], "gy", 1)
    return jnp.concatenate([folded[:, :, :1] + spill_column, folded[:, :, 1:-1]], axis=2)


def fine_terms(degrees, moduli, tables):
    row_count, column_count = (degrees.shape[1], degrees.shape[2])
    flat = degrees.reshape(8, row_count * column_count)
    values = moduli[0].reshape(1, -1) * jnp.dot(tables[0], flat, precision=HIGHEST) + moduli[
        1
    ].reshape(1, -1) * jnp.dot(tables[1], flat, precision=HIGHEST)
    return values.reshape(8, row_count, column_count)


def matrix_terms(degrees, element_matrix):
    row_count, column_count = (element_matrix.shape[1], element_matrix.shape[2])
    return jnp.sum(element_matrix.reshape(8, 8, row_count, column_count) * degrees[None], axis=1)


def fine_apply(field, first_eff, shear_eff, tables):
    degrees = element_dofs(extend(field))
    moduli = jnp.stack([first_eff, shear_eff])
    return assemble(element_scatter(fine_terms(degrees, moduli, tables)))


def matrix_apply(field, element_matrix):
    degrees = element_dofs(extend(field))
    return assemble(element_scatter(matrix_terms(degrees, element_matrix)))


def matrix_diagonal(element_matrix):
    return assemble(element_scatter(element_matrix[0::9]))


def level_operator(element_matrix):
    return (
        functools.partial(matrix_apply, element_matrix=element_matrix),
        matrix_diagonal(element_matrix),
    )


def first_coarse(first_eff, shear_eff, first_map):
    row_count, column_count = first_eff.shape
    half_rows, half_cols = (row_count // 2, column_count // 2)

    def by_subcell(values):
        return (
            values.reshape(half_rows, 2, half_cols, 2)
            .transpose(1, 3, 0, 2)
            .reshape(4, half_rows * half_cols)
        )

    coefficients = jnp.stack([by_subcell(first_eff), by_subcell(shear_eff)], axis=1).reshape(
        8, half_rows * half_cols
    )
    return jnp.dot(first_map, coefficients, precision=HIGHEST).reshape(64, half_rows, half_cols)


def next_coarse(element_matrix, second_map):
    row_count, column_count = (element_matrix.shape[1], element_matrix.shape[2])
    half_rows, half_cols = (row_count // 2, column_count // 2)
    sub_blocks = (
        element_matrix.reshape(64, half_rows, 2, half_cols, 2)
        .transpose(2, 4, 0, 1, 3)
        .reshape(256, half_rows * half_cols)
    )
    return jnp.dot(second_map, sub_blocks, precision=HIGHEST).reshape(64, half_rows, half_cols)


def restrict_terms(residual):
    component_count, row_count, column_count = residual.shape
    paired = residual.reshape(component_count, row_count // 2, 2, column_count)
    even_part, odd_part = (paired[:, :, 0], paired[:, :, 1])
    row_terms = jnp.pad(even_part + 0.5 * odd_part, ((0, 0), (0, 1), (0, 0))) + jnp.pad(
        0.5 * odd_part, ((0, 0), (1, 0), (0, 0))
    )
    paired = row_terms.reshape(component_count, row_count // 2 + 1, column_count // 2, 2)
    even_part, odd_part = (paired[..., 0], paired[..., 1])
    return jnp.pad(even_part + 0.5 * odd_part, ((0, 0), (0, 0), (0, 1))) + jnp.pad(
        0.5 * odd_part, ((0, 0), (0, 0), (1, 0))
    )


def prolong(extended):
    component_count, outer_rows, outer_cols = extended.shape
    half_rows, half_cols = (outer_rows - 1, outer_cols - 1)
    row_terms = jnp.stack(
        [extended[:, :half_rows], 0.5 * (extended[:, :half_rows] + extended[:, 1:])], axis=2
    )
    row_terms = row_terms.reshape(component_count, 2 * half_rows, outer_cols)
    both_terms = jnp.stack(
        [row_terms[:, :, :half_cols], 0.5 * (row_terms[:, :, :half_cols] + row_terms[:, :, 1:])],
        axis=3,
    )
    return both_terms.reshape(component_count, 2 * half_rows, 2 * half_cols)


def relax(source, apply_level, diagonal):
    field = DAMPING * source / diagonal
    for sweep_index in range(COARSE_SWEEPS - 1):
        field = field + DAMPING * (source - apply_level(field)) / diagonal
    return field


def coarsest(source, element_matrix):
    apply_level, diagonal = level_operator(element_matrix)
    return relax(source, apply_level, diagonal)


def cycle(level, source, operators, matrices):
    if level == LEVELS:
        return coarsest(source, matrices[LEVELS - 1])
    apply_level, diagonal = operators[level]
    field = DAMPING * source / diagonal
    field = field + DAMPING * (source - apply_level(field)) / diagonal
    residual = source - apply_level(field)
    coarse_source = assemble(restrict_terms(residual))
    correction = cycle(level + 1, coarse_source, operators, matrices)
    field = field + prolong(extend(correction))
    for sweep_index in range(SWEEPS):
        field = field + DAMPING * (source - apply_level(field)) / diagonal
    return field


def plastic_totals(plastic_owner, plastic_cell, plastic_code, cell_count):
    owner_list = plastic_owner[:, 0]
    entry_word = (owner_list * cell_count + plastic_cell) * 4 + plastic_code
    all_words = lax.all_gather(entry_word, ("gx", "gy"), axis=0, tiled=True)
    my_index = lax.axis_index("gx") * lax.axis_size("gy") + lax.axis_index("gy")
    all_owner = all_words // (4 * cell_count)
    arrived_cell = all_words // 4 % cell_count
    arrived_code = jnp.where(all_owner == my_index, all_words % 4, 0)
    return jnp.zeros((cell_count,), jnp.int32).at[arrived_cell].add(arrived_code)


def body(first_lame, shear_modulus, applied_load, plastic_owner, plastic_cell, plastic_code):
    row_count, column_count = first_lame.shape
    code_total = plastic_totals(plastic_owner, plastic_cell, plastic_code, row_count * column_count)
    factor = jnp.power(YIELD_DROP, code_total.reshape(row_count, column_count).astype(jnp.float32))
    first_eff = first_lame * factor
    shear_eff = shear_modulus * factor
    tables = element_tables()
    diag_first = jnp.diagonal(tables[0])[:, None, None]
    diag_shear = jnp.diagonal(tables[1])[:, None, None]
    fine_level = functools.partial(
        fine_apply, first_eff=first_eff, shear_eff=shear_eff, tables=tables
    )
    fine_diagonal = assemble(
        element_scatter(first_eff[None] * diag_first + shear_eff[None] * diag_shear)
    )
    matrices = [first_coarse(first_eff, shear_eff, tables[2])]
    for level in range(1, LEVELS):
        matrices.append(next_coarse(matrices[-1], tables[3]))
    operators = [(fine_level, fine_diagonal)]
    for level in range(1, LEVELS):
        operators.append(level_operator(matrices[level - 1]))
    return cycle(0, applied_load, operators, matrices)


def solution(mesh):
    return jax.shard_map(
        body,
        mesh=mesh,
        in_specs=(
            P("gx", "gy"),
            P("gx", "gy"),
            P(None, "gx", "gy"),
            P(("gx", "gy"), None),
            P(("gx", "gy")),
            P(("gx", "gy")),
        ),
        out_specs=P(None, "gx", "gy"),
        check_vma=False,
    )
```

profile of v0, /device:TPU:1, one launch (start us, length us, event | category | flops | bytes accessed | tf_op | source)
XLA Modules:
  0.0 782.8 jit_solution(11188335611763160524)
XLA Ops:
  1.4 62.4 %all-gather = s32[32,1,512]{2,1,0:T(1,128)S(1)} all-gather(s32[1,1,512]{2,1,0:T(1,128)S(1)} %bitcast.325), channel_id=1, replica_groups=mesh['gx'=4,'gy'=8] {'gx','gy'}, dimensions={0}, use_global_device_ids=true | all-gather | bytes 67584 | tf_op jit(solution)/shard_map/all_gather | solution.py:233
  63.9 85.9 %scatter_custom_fusion = s32[32768]{0:T(1024)S(1)} fusion(s32[16384]{0:T(1024)S(1)} %get-tuple-element.112, s32[16384]{0:T(1024)S(1)} %get-tuple-element.111, s32[]{:T(128)} %constant.89.clone.1), kind=kCustom, calls=%fused_computation.275 | custom fusion | flops 16384 | bytes 131076 | tf_op jit(solution)/shard_map/scatter-add | solution.py:238
  153.6 9.7 %collective-permute-start = (f32[2,1,513]{2,0,1:T(2,128)S(1)}, f32[2,1,513]{2,0,1:T(2,128)S(1)}, u32[]{:S(2)}, u32[]{:S(2)}) collective-permute-start(f32[2,1,513]{2,0,1:T(2,128)S(1)} %copy.804), channel_id=1, source_target_pairs={{0,8},{8,16},{16,24},{1,9},{9,17},{17,25},{2,10},{10,18},{18,26},{... | collective-permute-start | bytes 12320 | tf_op jit(solution)/shard_map/ppermute | solution.py:24
  163.3 9.7 %reshape.137 = f32[32,2,256,2]{3,2,1,0:T(8,128)} reshape(f32[64,512]{1,0:T(8,128)S(1)} %get-tuple-element.77) | data formatting | bytes 262144 | tf_op jit(solution)/shard_map/reshape | solution.py:153
  173.1 9.8 %reshape.138 = f32[32,2,256,2]{3,2,1,0:T(8,128)} reshape(f32[64,512]{1,0:T(8,128)S(1)} %get-tuple-element.78) | data formatting | bytes 262144 | tf_op jit(solution)/shard_map/reshape | solution.py:153
  182.8 5.2 copy.824
  188.1 5.2 copy.825
  208.3 5.0 copy.840
  223.5 3.5 collective-permute-start.3
  270.3 3.5 collective-permute-start.5
  288.9 4.4 collective-permute-start.7
  293.9 5.0 collective-permute-start.13
  327.2 4.5 collective-permute-start.10
  339.2 4.0 collective-permute-start.11
  363.3 4.1 collective-permute-start.16
  368.2 4.5 collective-permute-start.17
  375.2 4.3 collective-permute-start.25
  383.2 3.3 collective-permute-done.19
  392.3 4.5 collective-permute-start.21
  402.3 5.2 collective-permute-start.22
  413.3 4.3 collective-permute-start.23
  422.0 3.9 collective-permute-done.26
  427.9 5.8 collective-permute-start.36
  437.3 4.8 collective-permute-start.29
  444.4 3.4 collective-permute-done.30
  447.8 4.0 collective-permute-start.31
  452.4 5.1 collective-permute-start.37
  458.0 4.4 collective-permute-start.32
  468.2 5.0 collective-permute-start.34
  476.0 3.9 collective-permute-start.35
  491.3 4.0 collective-permute-done.39
  499.4 4.5 collective-permute-start.41
  506.8 3.4 collective-permute-done.42
  510.2 4.1 collective-permute-start.43
  521.0 4.5 collective-permute-start.45
  528.3 3.4 collective-permute-done.46
  531.7 4.1 collective-permute-start.47
  542.2 4.5 collective-permute-start.49
  548.9 3.4 collective-permute-done.50
  552.3 4.1 collective-permute-start.51
  562.8 4.5 collective-permute-start.53
  569.4 3.4 collective-permute-done.54
  572.8 4.1 collective-permute-start.55
  583.3 4.5 collective-permute-start.57
  589.9 3.4 collective-permute-done.58
  593.4 4.1 collective-permute-start.59
  602.8 4.4 collective-permute-done.60
  615.6 4.3 collective-permute-start.63
  622.8 3.5 collective-permute-done.64
  626.3 4.1 collective-permute-start.65
  636.8 4.5 collective-permute-start.67
  644.3 3.5 collective-permute-done.68
  647.8 4.1 collective-permute-start.69
  656.7 4.5 collective-permute-done.70
  670.5 4.3 collective-permute-start.73
  677.2 3.6 collective-permute-done.74
  680.9 4.1 collective-permute-start.75
  692.3 4.5 collective-permute-start.77
  699.3 3.6 collective-permute-done.78
  702.9 4.1 collective-permute-start.79
  712.1 4.2 collective-permute-done.80
  738.2 4.2 collective-permute-start.83
  749.3 4.1 collective-permute-start.85
  774.8 4.5 collective-permute-start.87
  (670 shorter events, 353.2 us)
Async XLA Ops:
  153.6 43.9 %collective-permute-start = (f32[2,1,513]{2,0,1:T(2,128)S(1)}, f32[2,1,513]{2,0,1:T(2,128)S(1)}, u32[]{:S(2)}, u32[]{:S(2)}) collective-permute-start(f32[2,1,513]{2,0,1:T(2,128)S(1)} %copy.804), channel_id=1, source_target_pairs={{0,8},{8,16},{16,24},{1,9},{9,17},{17,25},{2,10},{10,18},{18,26},{... | collective-permute-start | bytes 12320 | tf_op jit(solution)/shard_map/ppermute | solution.py:24
  201.3 12.1 %collective-permute-start.1 = (f32[2,64,1]{1,2,0:T(1,128)S(1)}, f32[2,64,1]{1,2,0:T(1,128)S(1)}, u32[]{:S(2)}, u32[]{:S(2)}) collective-permute-start(f32[2,64,1]{1,2,0:T(1,128)S(1)} %pad_maximum_fusion.85), channel_id=1, source_target_pairs={{0,1},{1,2},{2,3},{3,4},{4,5},{5,6},{6,7},{8,9},{9,10},{10,11},{11... | collective-permute-start | bytes 1544 | tf_op jit(solution)/shard_map/ppermute | solution.py:24
  203.2 80.5 %collective-permute-start.12 = (f32[2,1,257]{2,1,0:T(1,128)}, f32[2,1,257]{2,1,0:T(1,128)S(1)}, u32[]{:S(2)}, u32[]{:S(2)}) collective-permute-start(f32[2,1,257]{2,1,0:T(1,128)} %pad_add_fusion.66), channel_id=1, source_target_pairs={{0,8},{8,16},{16,24},{1,9},{9,17},{17,25},{2,10},{10,18},{18,26},{... | collective-permute-start | bytes 6176 | tf_op jit(solution)/shard_map/ppermute | solution.py:24
  223.5 5.2 collective-permute-start.3
  259.7 6.8 collective-permute-start.4
  262.3 110.4 %collective-permute-start.24 = (f32[2,1,129]{2,1,0:T(1,128)}, f32[2,1,129]{2,1,0:T(1,128)}, u32[]{:S(2)}, u32[]{:S(2)}) collective-permute-start(f32[2,1,129]{2,1,0:T(1,128)} %pad_add_fusion.71), channel_id=1, source_target_pairs={{0,8},{8,16},{16,24},{1,9},{9,17},{17,25},{2,10},{10,18},{18,26},{... | collective-permute-start | bytes 3104 | tf_op jit(solution)/shard_map/ppermute | solution.py:24
  270.3 9.5 %collective-permute-start.5 = (f32[2,64,1]{1,2,0:T(1,128)S(1)}, f32[2,64,1]{1,2,0:T(1,128)S(1)}, u32[]{:S(2)}, u32[]{:S(2)}) collective-permute-start(f32[2,64,1]{1,2,0:T(1,128)S(1)} %pad_maximum_fusion.84), channel_id=1, source_target_pairs={{0,1},{1,2},{2,3},{3,4},{4,5},{5,6},{6,7},{8,9},{9,10},{10,11},{11... | collective-permute-start | bytes 1544 | tf_op jit(solution)/shard_map/ppermute | solution.py:24
  288.9 10.0 %collective-permute-start.7 = (f32[2,1,513]{2,0,1:T(2,128)S(1)}, f32[2,1,513]{2,0,1:T(2,128)S(1)}, u32[]{:S(2)}, u32[]{:S(2)}) collective-permute-start(f32[2,1,513]{2,0,1:T(2,128)S(1)} %copy.816), channel_id=1, source_target_pairs={{8,0},{16,8},{24,16},{9,1},{17,9},{25,17},{10,2},{18,10},{26,18},{... | collective-permute-start | bytes 12320 | tf_op jit(solution)/shard_map/ppermute | solution.py:24
  293.9 21.4 %collective-permute-start.13 = (f32[2,32,1]{2,1,0:T(8,128)}, f32[2,32,1]{2,1,0:T(8,128)}, u32[]{:S(2)}, u32[]{:S(2)}) collective-permute-start(f32[2,32,1]{2,1,0:T(8,128)} %fusion.100), channel_id=1, source_target_pairs={{0,1},{1,2},{2,3},{3,4},{4,5},{5,6},{6,7},{8,9},{9,10},{10,11},{11... | collective-permute-start | bytes 776 | tf_op jit(solution)/shard_map/ppermute | solution.py:24
  327.2 8.3 %collective-permute-start.10 = (f32[2,1,257]{1,2,0:T(8,128)}, f32[2,1,257]{1,2,0:T(8,128)}, u32[]{:S(2)}, u32[]{:S(2)}) collective-permute-start(f32[2,1,257]{1,2,0:T(8,128)} %slice_add_fusion.4), channel_id=1, source_target_pairs={{0,8},{8,16},{16,24},{1,9},{9,17},{17,25},{2,10},{10,18},{18,26},{... | collective-permute-start | bytes 6176 | tf_op jit(solution)/shard_map/ppermute | solution.py:24
  339.2 5.0 collective-permute-start.11
  346.5 4.9 collective-permute-start.14
  352.6 7.9 %collective-permute-start.15 = (f32[2,1,257]{2,1,0:T(1,128)}, f32[2,1,257]{2,1,0:T(1,128)S(1)}, u32[]{:S(2)}, u32[]{:S(2)}) collective-permute-start(f32[2,1,257]{2,1,0:T(1,128)} %pad_maximum_fusion.77), channel_id=1, source_target_pairs={{8,0},{16,8},{24,16},{9,1},{17,9},{25,17},{10,2},{18,10},{26,18},{... | collective-permute-start | bytes 6176 | tf_op jit(solution)/shard_map/ppermute | solution.py:24
  363.3 4.8 collective-permute-start.16
  368.2 5.6 collective-permute-start.17
  373.9 5.6 collective-permute-start.18
  375.2 6.2 collective-permute-start.25
  379.5 6.9 collective-permute-start.19
  392.3 5.6 collective-permute-start.21
  402.3 7.7 collective-permute-start.22
  413.3 5.1 collective-permute-start.23
  419.9 6.0 collective-permute-start.26
  425.9 7.8 collective-permute-start.27
  427.9 16.4 %collective-permute-start.36 = (f32[2,1,65]{2,1,0:T(1,128)S(1)}, f32[2,1,65]{2,1,0:T(1,128)S(1)}, u32[]{:S(2)}, u32[]{:S(2)}) collective-permute-start(f32[2,1,65]{2,1,0:T(1,128)S(1)} %pad_add_fusion.77), channel_id=1, source_target_pairs={{0,8},{8,16},{16,24},{1,9},{9,17},{17,25},{2,10},{10,18},{18,26},{... | collective-permute-start | bytes 1568 | tf_op jit(solution)/shard_map/ppermute | solution.py:24
  437.3 5.7 collective-permute-start.29
  443.0 4.8 collective-permute-start.30
  447.8 9.8 %collective-permute-start.31 = (f32[2,1,129]{2,1,0:T(1,128)S(1)}, f32[2,1,129]{2,1,0:T(1,128)S(1)}, u32[]{:S(2)}, u32[]{:S(2)}) collective-permute-start(f32[2,1,129]{2,1,0:T(1,128)S(1)} %pad_maximum_fusion.80), channel_id=1, source_target_pairs={{8,0},{16,8},{24,16},{9,1},{17,9},{25,17},{10,2},{18,10},{26,18},{... | collective-permute-start | bytes 3104 | tf_op jit(solution)/shard_map/ppermute | solution.py:24
  452.4 27.5 %collective-permute-start.37 = (f32[2,8,1]{2,1,0:T(8,128)}, f32[2,8,1]{2,1,0:T(8,128)}, u32[]{:S(2)}, u32[]{:S(2)}) collective-permute-start(f32[2,8,1]{2,1,0:T(8,128)} %fusion.170), channel_id=1, source_target_pairs={{0,1},{1,2},{2,3},{3,4},{4,5},{5,6},{6,7},{8,9},{9,10},{10,11},{11... | collective-permute-start | bytes 200 | tf_op jit(solution)/shard_map/ppermute | solution.py:24
  458.0 5.1 collective-permute-start.32
  468.2 6.7 collective-permute-start.34
  476.0 4.7 collective-permute-start.35
  482.1 5.0 collective-permute-start.38
  487.8 7.5 collective-permute-start.39
  499.4 5.3 collective-permute-start.41
  510.2 7.4 collective-permute-start.43
  521.0 5.3 collective-permute-start.45
  531.7 7.1 collective-permute-start.47
  542.2 5.3 collective-permute-start.49
  552.3 7.1 collective-permute-start.51
  562.8 5.3 collective-permute-start.53
  572.8 7.1 collective-permute-start.55
  583.3 5.3 collective-permute-start.57
  593.4 7.1 collective-permute-start.59
  601.6 5.7 collective-permute-start.60
  607.2 4.9 collective-permute-start.61
  615.6 5.1 collective-permute-start.63
  621.5 4.8 collective-permute-start.64
  626.3 7.1 collective-permute-start.65
  636.8 5.4 collective-permute-start.67
  643.0 4.8 collective-permute-start.68
  647.8 7.1 collective-permute-start.69
  655.4 5.8 collective-permute-start.70
  661.2 4.9 collective-permute-start.71
  670.5 5.3 collective-permute-start.73
  675.9 4.9 collective-permute-start.74
  680.9 7.1 collective-permute-start.75
  692.3 5.6 collective-permute-start.77
  698.0 4.9 collective-permute-start.78
  702.9 7.1 collective-permute-start.79
  710.8 5.5 collective-permute-start.80
  716.5 4.9 collective-permute-start.81
  738.2 5.0 collective-permute-start.83
  749.3 7.1 collective-permute-start.85
  774.8 5.2 collective-permute-start.87
  (82 other events, 1130.3 us)
where the time goes:
time: 797 us; the launch traced here: 783 us
  starting transfers between devices  265 us (33%)
  other arithmetic  170 us (21%)
  waiting for transfers between devices  139 us (17%)
  local copies, waits for them, and re-layouts  130 us (16%)
  blocking collectives  62.4 us (8%)
  matrix products  13.5 us (2%)
    ppermute x88, starting transfers between devices, passed_along(): return lax.ppermute(array, axis, pairs)  265 us
    ppermute x88, waiting for transfers between devices, passed_along(): return lax.ppermute(array, axis, pairs)  139 us
    scatter-add x1, other arithmetic, plastic_totals(): jnp.zeros((cell_count,), jnp.int32).at[arrived_cell].add(arrived_code)  85.9 us
    all_gather x1, blocking collectives, plastic_totals(): all_words = lax.all_gather(entry_word, ('gx', 'gy'), axis=0, tiled=True)  62.4 us
    unnamed x139, local copies, waits for them, and re-layouts  22.7 us
    reshape x2, local copies, waits for them, and re-layouts, by_subcell(): values.reshape(half_rows, 2, half_cols, 2).transpose(1, 3, 0, 2)  19.5 us
    slice x35, local copies, waits for them, and re-layouts, element_scatter(): values[2 * corner:2 * corner + 2]  16.5 us
  transfers between devices with their start and end apart: 88, of which 70 were waited for; matrix products, arithmetic and copies ran while one was open for 20% of the time, Pallas kernels for 0%

commit v1 on v0

v1 whole, which is shorter than its diff:
```python
import functools
import math

import jax
import jax.numpy as jnp
import numpy as np
from jax import lax
from jax.experimental import pallas as pl
from jax.experimental.pallas import tpu as pltpu
from jax.sharding import PartitionSpec as P

LEVELS = 3
SWEEPS = 2
COARSE_SWEEPS = 6
YIELD_DROP = 0.6
GROUP = 1 << LEVELS
HALO_ROWS = 32
HALO_COLS = 128
LANES = 128
VMEM_LIMIT = 56 * 1024 * 1024
F32 = jnp.float32
BF16 = jnp.bfloat16

FIRST = ("11", "12", "33", "1r", "2r", "3r", "1c", "2c", "3c", "rr", "rc")
FULL = FIRST + ("cc",)
FIRST_AT = {name: FIRST.index(name) for name in FIRST} | {"22": 0, "cc": FIRST.index("rr")}
FULL_AT = {name: FULL.index(name) for name in FULL} | {"22": 0}


def passed_along(array, axis, by):
    devices = lax.axis_size(axis)
    pairs = [(i, i + by) for i in range(devices) if 0 <= i + by < devices]
    return lax.ppermute(array, axis, pairs)


def log2(number):
    power = number.bit_length() - 1
    assert 1 << power == number
    return power


def from_before(value, axis):
    return pltpu.roll(value, 1, axis)


def from_after(value, axis):
    return pltpu.roll(value, value.shape[axis] - 1, axis)


def plus(*terms):
    total = None
    for term in terms:
        if term is not None:
            total = term if total is None else total + term
    return total


def times(weight, term):
    return None if term is None else weight * term


def factor_kernel(place, words, factor, rows_of, cols_of, codes, counts, *, rows, cols, gy):
    word = words[...]
    cell_bits = log2(rows * cols)
    owner = word >> (cell_bits + 2)
    cell = (word >> 2) & (rows * cols - 1)
    row = (owner >> log2(gy)) * rows + (cell >> log2(cols)) - place[0] * rows + HALO_ROWS
    col = (owner & (gy - 1)) * cols + (cell & (cols - 1)) - place[1] * cols
    inside = (row >= 0) & (row < rows + 2 * HALO_ROWS) & (col >= -HALO_COLS) & (col < cols + HALO_COLS)
    at = jnp.where(col < 0, col + cols + HALO_COLS, jnp.where(col >= cols, col + HALO_COLS, col))
    half = (cols + 2 * HALO_COLS) // 2
    tall = rows + 2 * HALO_ROWS
    upper = at >= half
    rows_of[...] = jnp.where(inside, jnp.where(upper, row + tall, row), -1)
    cols_of[...] = jnp.where(upper, at - half, at)
    codes[...] = (word & 3).astype(F32)
    counts[...] = jnp.zeros_like(counts)
    length = words.shape[1]

    @pl.loop(0, words.shape[0])
    def _(i):
        line = pl.ds(i, 1)
        row_id = lax.broadcasted_iota(jnp.int32, (2 * tall, length), 0)
        col_id = lax.broadcasted_iota(jnp.int32, (half, length), 0)
        by_row = jnp.where(row_id == rows_of[line, :], codes[line, :], 0.0).astype(BF16)
        by_col = jnp.where(col_id == cols_of[line, :], 1.0, 0.0).astype(BF16)
        counts[...] += lax.dot_general(
            by_row, by_col, (((1,), (1,)), ((), ())), preferred_element_type=F32
        )

    per_half = half // LANES
    for tile in range(2 * per_half):
        side, lane = tile // per_half, tile % per_half
        count = counts[side * tall : (side + 1) * tall, lane * LANES : (lane + 1) * LANES]
        factor[tile] = jnp.exp(count * math.log(YIELD_DROP))


def yield_factor(place, words, rows, cols, gy):
    tall, wide = rows + 2 * HALO_ROWS, cols + 2 * HALO_COLS
    return pl.pallas_call(
        functools.partial(factor_kernel, rows=rows, cols=cols, gy=gy),
        out_shape=jax.ShapeDtypeStruct((wide // LANES, tall, LANES), F32),
        in_specs=[
            pl.BlockSpec(memory_space=pltpu.SMEM),
            pl.BlockSpec(memory_space=pltpu.VMEM),
        ],
        out_specs=pl.BlockSpec(memory_space=pltpu.VMEM),
        scratch_shapes=[
            pltpu.VMEM(words.shape, jnp.int32),
            pltpu.VMEM(words.shape, jnp.int32),
            pltpu.VMEM(words.shape, F32),
            pltpu.VMEM((2 * tall, wide // 2), F32),
        ],
        compiler_params=pltpu.CompilerParams(vmem_limit_bytes=VMEM_LIMIT),
        cost_estimate=pl.CostEstimate(flops=10**9, bytes_accessed=10**6, transcendentals=0),
        name="yield_factor",
    )(place, words)


class Level:
    def __init__(self, matrix, names_at, inverse, spill):
        self.matrix, self.names_at, self.inverse, self.spill = matrix, names_at, inverse, spill
        self.count = matrix.shape[1]

    def entry(self, name, m, k):
        at = self.names_at.get(name)
        return None if at is None else self.matrix[at, m, k]

    def stress(self, m, k, modes):
        names = "123rc"
        known = {}
        result = []
        for i in range(5):
            terms = []
            for j in range(5):
                name = names[min(i, j)] + names[max(i, j)]
                if name not in known:
                    known[name] = self.entry(name, m, k)
                if known[name] is not None:
                    terms.append(known[name] * modes[j])
            result.append(plus(*terms))
        return result

    def halves(self, component, m, k):
        if component == 0:
            names = ("11", "33", "rr", "13", "1r", "3r")
        else:
            names = ("22", "33", "cc", "23", "3c", "2c")
        first, second, third, cross, by_col, by_row = [self.entry(name, m, k) for name in names]
        base = first + second + third
        by_row, by_col, cross = 2.0 * by_row, 2.0 * by_col, times(2.0, cross)
        if cross is None:
            return base - by_row, base + by_row, by_col, by_col
        return base - by_row, base + by_row, by_col - cross, by_col + cross

    def components(self):
        return (0, 1)

    def make_inverse(self, row_ok, col_ok):
        count = self.count
        for component in self.components():
            kept = {}
            for k in range(count):
                parts = [self.halves(component, m, k) for m in range(count)]
                for m in range(count):
                    above = parts[m - 1] if m else parts[count - 1]
                    lower = [above[1], above[3]]
                    if m == 0:
                        lower = [from_before(value, 0) for value in lower]
                    even, odd = parts[m][0] + lower[0], parts[m][2] + lower[1]
                    kept[m, k] = (even - odd, even + odd)
            for k in range(count):
                for m in range(count):
                    left = kept[m, k - 1][1] if k else from_before(kept[m, count - 1][1], 1)
                    diagonal = kept[m, k][0] + left
                    value = jnp.where(diagonal > 0.0, 0.5 / diagonal, 0.0)
                    if m == 0:
                        value = value * row_ok
                    if k == 0:
                        value = value * col_ok
                    self.inverse[component, m, k] = value


class FineLevel(Level):
    def stress(self, m, k, modes):
        lame, shear, mixed = self.matrix[0, m, k], self.matrix[1, m, k], self.matrix[2, m, k]
        first, second, third, bend_row, bend_col = modes
        twice, mean = shear + shear, lame * (first + second)
        return [
            mean + twice * first,
            mean + twice * second,
            shear * third,
            mixed * bend_row,
            mixed * bend_col,
        ]

    def components(self):
        return (0,)

    def make_inverse(self, row_ok, col_ok):
        count = self.count

        @pl.loop(0, count)
        def _(k):
            parts = [self.matrix[2, m, k] for m in range(count)]
            for m in range(count):
                above = parts[m - 1] if m else from_before(parts[count - 1], 0)
                self.inverse[0, m, k] = parts[m] + above

        for m in range(count):
            left = from_before(self.inverse[0, m, count - 1], 1)
            for k in range(count):
                here = self.inverse[0, m, k]
                diagonal = 4.0 * (here + left)
                left = here
                value = jnp.where(diagonal > 0.0, 0.5 / diagonal, 0.0)
                if m == 0:
                    value = value * row_ok
                if k == 0:
                    value = value * col_ok
                self.inverse[0, m, k] = value


def inverse_of(level, component, m, k):
    return level.inverse[min(component, len(level.components()) - 1), m, k]


def close_columns(level, x):
    count = level.count
    for component in (0, 1):
        for m in range(count):
            x[component, m, count] = from_after(x[component, m, 0], 1)


def start(level, x, source):
    count = level.count

    def column(k):
        for component in (0, 1):
            for m in range(count):
                x[component, m, k] = source[component, m, k] * inverse_of(level, component, m, k)

    over_columns(count, column)
    close_columns(level, x)


def over_columns(count, column):
    if count > 2:
        pl.loop(0, count)(column)
    else:
        for k in range(count):
            column(k)


def apply(level, x, source, out, residual):
    count, spill = level.count, level.spill
    spill[...] = jnp.zeros_like(spill)

    def column(k):
        sums, steps = [], []
        for m in range(count):
            here = [x[component, m, k] for component in (0, 1)]
            after = [x[component, m, k + 1] for component in (0, 1)]
            sums.append([here[c] + after[c] for c in (0, 1)])
            steps.append([after[c] - here[c] for c in (0, 1)])
        sums.append([from_after(value, 0) for value in sums[0]])
        steps.append([from_after(value, 0) for value in steps[0]])
        own, passed = [], []
        for m in range(count):
            modes = (
                sums[m + 1][0] - sums[m][0],
                steps[m][1] + steps[m + 1][1],
                (steps[m][0] + steps[m + 1][0]) + (sums[m + 1][1] - sums[m][1]),
                steps[m + 1][0] - steps[m][0],
                steps[m + 1][1] - steps[m][1],
            )
            first, second, third, bend_row, bend_col = level.stress(m, k, modes)
            own.append((first, third - bend_row, third, second - bend_col))
            passed.append((first, third + bend_row, third, second + bend_col))
        for m in range(count):
            above = passed[m - 1] if m else [from_before(value, 0) for value in passed[count - 1]]
            for component in (0, 1):
                at = 2 * component
                even = above[at] - own[m][at]
                odd = above[at + 1] + own[m][at + 1]
                left = spill[component, m]
                spill[component, m] = even + odd
                rest = source[component, m, k] - ((even - odd) + left)
                if not residual:
                    rest = x[component, m, k] + inverse_of(level, component, m, k) * rest
                out[component, m, k] = rest

    over_columns(count, column)
    for component in (0, 1):
        for m in range(count):
            left = from_before(spill[component, m], 1)
            if not residual:
                left = left * inverse_of(level, component, m, 0)
            out[component, m, 0] = out[component, m, 0] - left
    if not residual:
        close_columns(level, out)


def restrict(residual, target, count):
    half = count // 2
    for component in (0, 1):
        for k in range(half):
            lines = []
            for m in range(count):
                odd = residual[component, m, 2 * k + 1]
                if k:
                    before = residual[component, m, 2 * k - 1]
                else:
                    before = from_before(residual[component, m, count - 1], 1)
                lines.append(residual[component, m, 2 * k] + 0.5 * (odd + before))
            for m in range(half):
                before = lines[2 * m - 1] if m else from_before(lines[count - 1], 0)
                target[component, m, k] = lines[2 * m] + 0.5 * (lines[2 * m + 1] + before)


def prolong(coarse, before, x, count):
    half = count // 2
    for component in (0, 1):
        planes = {(m, k): coarse(component, m, k) for m in range(half) for k in range(half)}
        for m in range(half):
            planes[m, half] = from_after(planes[m, 0], 1)
        for k in range(half + 1):
            planes[half, k] = from_after(planes[0, k], 0)
        for m in range(half):
            for k in range(half):
                a, b, c, d = planes[m, k], planes[m + 1, k], planes[m, k + 1], planes[m + 1, k + 1]
                x[component, 2 * m, 2 * k] = before[component, 2 * m, 2 * k] + a
                x[component, 2 * m + 1, 2 * k] = before[component, 2 * m + 1, 2 * k] + 0.5 * (a + b)
                x[component, 2 * m, 2 * k + 1] = before[component, 2 * m, 2 * k + 1] + 0.5 * (a + c)
                x[component, 2 * m + 1, 2 * k + 1] = before[component, 2 * m + 1, 2 * k + 1] + 0.25 * ((a + b) + (c + d))


def haar(level, names_at, m, k):
    def signed(name, row, col):
        if name not in names_at:
            return None
        value = {
            (a, b): level.matrix[names_at[name], 2 * m + a, 2 * k + b] for a in (0, 1) for b in (0, 1)
        }
        low = value[0, 1] - value[0, 0] if col else value[0, 1] + value[0, 0]
        high = value[1, 1] - value[1, 0] if col else value[1, 1] + value[1, 0]
        return high - low if row else high + low

    return signed


def coarsen_fine(fine, coarse):
    count = coarse.count

    def column(k):
        for m in range(count):
            signed = haar(fine, {"l": 0, "s": 1}, m, k)
            lame, shear = signed("l", 0, 0), signed("s", 0, 0)
            lame_row, shear_row = signed("l", 1, 0), signed("s", 1, 0)
            lame_col, shear_col = signed("l", 0, 1), signed("s", 0, 1)
            lame_both, shear_both = signed("l", 1, 1), signed("s", 1, 1)
            values = {
                "11": 0.25 * (lame + 2.0 * shear),
                "12": 0.25 * lame,
                "33": 0.25 * shear,
                "1r": 0.125 * (lame_col + 2.0 * shear_col),
                "2r": 0.125 * lame_col,
                "3r": 0.125 * shear_row,
                "1c": 0.125 * lame_row,
                "2c": 0.125 * (lame_row + 2.0 * shear_row),
                "3c": 0.125 * shear_col,
                "rr": (lame + 3.0 * shear) * (1.0 / 12.0),
                "rc": 0.0625 * (lame_both + shear_both),
            }
            for name, value in values.items():
                coarse.matrix[FIRST_AT[name], m, k] = value

    over_columns(count, column)


def coarsen(fine, write, count):
    for k in range(count):
        for m in range(count):
            signed = haar(fine, fine.names_at, m, k)

            def total(name):
                return signed(name, 0, 0)

            def by_row(name):
                return signed(name, 1, 0)

            def by_col(name):
                return signed(name, 0, 1)

            def by_both(name):
                return signed(name, 1, 1)

            values = {}
            for name in ("11", "12", "33"):
                values[name] = times(0.25, total(name))
            for i in "123":
                one, two, three = ["".join(sorted(i + j)) for j in "123"]
                values[i + "r"] = 0.125 * plus(by_col(one), by_row(three), total(i + "r"))
                values[i + "c"] = 0.125 * plus(by_row(two), by_col(three), total(i + "c"))
            values["rr"] = 0.0625 * plus(
                total("11"),
                total("33"),
                times(2.0, by_both("13")),
                2.0 * (by_col("1r") + by_row("3r")),
                total("rr"),
            )
            values["cc"] = 0.0625 * plus(
                total("22"),
                total("33"),
                times(2.0, by_both("23")),
                2.0 * (by_row("2c") + by_col("3c")),
                total("cc"),
            )
            values["rc"] = 0.0625 * plus(
                by_both("12"),
                total("13"),
                total("23"),
                by_both("33"),
                by_col("1c"),
                by_row("3c"),
                by_row("2r"),
                by_col("3r"),
                total("rc"),
            )
            for name in FULL:
                write(FULL_AT[name], m, k, values[name])


def edge_masks(place, shape, rows, cols, first_row, grid_rows, grid_cols):
    row = lax.broadcasted_iota(jnp.int32, shape, 0) * GROUP + (place[0] * rows + first_row)
    col = lax.broadcasted_iota(jnp.int32, shape, 1) * GROUP + (place[1] * cols - HALO_COLS)
    return (
        jnp.where(row < grid_rows, 1.0, 0.0).astype(F32),
        jnp.where(col < grid_cols, 1.0, 0.0).astype(F32),
    )


def three_parts(value):
    high = value.astype(BF16)
    rest = value - high.astype(F32)
    middle = rest.astype(BF16)
    low = (rest - middle.astype(F32)).astype(BF16)
    return high, middle, low


def down_kernel(
    place, first_lame, shear_modulus, applied_load, left, right, upper, lower, factor,
    matrix0, inverse0, source0, x0, matrix1, inverse1, source1, x1, matrix2, inverse2, source2, x2, coarsest,
    tiles, stacked, spread, other0, other1, other2, spill0, spill1, spill2, matrix3,
    *, rows, cols, gx, gy,
):
    tall, wide = rows + 2 * HALO_ROWS, cols + 2 * HALO_COLS
    side = tall // GROUP
    row_ok, col_ok = edge_masks(place, (side, LANES), rows, cols, -HALO_ROWS, gx * rows, gy * cols)

    for tile in range(wide // LANES):
        at = lax.broadcasted_iota(jnp.int32, (LANES, GROUP * LANES), 0) + tile * LANES
        if tile < cols // LANES:
            at = at + HALO_COLS
        elif tile == cols // LANES:
            at = at - cols
        target = (at & (GROUP - 1)) * LANES + (at >> LEVELS)
        lane = lax.broadcasted_iota(jnp.int32, (LANES, GROUP * LANES), 1)
        spread[tile * LANES : (tile + 1) * LANES, :] = jnp.where(lane == target, 1.0, 0.0).astype(BF16)

    own = (first_lame, shear_modulus, applied_load.at[0], applied_load.at[1])
    for field in range(4):
        for tile in range(wide // LANES):
            lanes = slice(tile * LANES, (tile + 1) * LANES)
            if tile < cols // LANES:
                middle = own[field][:, lanes]
            else:
                middle = (left if tile == cols // LANES else right)[field]
            parts = [
                (slice(0, HALO_ROWS), upper[field, :, lanes]),
                (slice(HALO_ROWS, HALO_ROWS + rows), middle),
                (slice(HALO_ROWS + rows, tall), lower[field, :, lanes]),
            ]
            for span, value in parts:
                if field < 2:
                    value = value * (0.25 * factor[tile, span, :])
                tiles[tile, span, :] = value
        for m in range(GROUP):
            for tile in range(wide // LANES):
                lanes = slice(tile * LANES, (tile + 1) * LANES)
                for part, value in enumerate(three_parts(tiles[tile, pl.ds(m, side, stride=GROUP), :])):
                    stacked[part * tall + m * side : part * tall + (m + 1) * side, lanes] = value
        for pair in range(GROUP // 2):
            lanes = slice(pair * 2 * LANES, (pair + 1) * 2 * LANES)
            product = jnp.dot(stacked[...], spread[:, lanes], preferred_element_type=F32)
            product = product[:tall] + product[tall : 2 * tall] + product[2 * tall :]
            for m in range(GROUP):
                for half in (0, 1):
                    plane = product[m * side : (m + 1) * side, half * LANES : (half + 1) * LANES]
                    if field < 2:
                        matrix0[field, m, 2 * pair + half] = plane
                    else:
                        source0[field - 2, m, 2 * pair + half] = plane

    def mix(k):
        for m in range(GROUP):
            matrix0[2, m, k] = matrix0[0, m, k] * (1.0 / 3.0) + matrix0[1, m, k]

    over_columns(GROUP, mix)

    level0 = FineLevel(matrix0, {}, inverse0, spill0)
    level1 = Level(matrix1, FIRST_AT, inverse1, spill1)
    level2 = Level(matrix2, FULL_AT, inverse2, spill2)

    coarsen_fine(level0, level1)

    def write2(at, m, k, value):
        matrix2[at, m, k] = value

    coarsen(level1, write2, level2.count)

    def write3(at, m, k, value):
        matrix3[at] = value

    coarsen(level2, write3, 1)
    for level in (level0, level1, level2):
        level.make_inverse(row_ok, col_ok)

    source3 = matrix3.at[pl.ds(len(FULL), 2)]
    chain = (
        (level0, source0, x0, other0, source1),
        (level1, source1, x1, other1, source2),
        (level2, source2, x2, other2, None),
    )
    for level, source, x, other, target in chain:
        start(level, other, source)
        apply(level, other, source, x, residual=False)
        apply(level, x, source, other, residual=True)
        if target is not None:
            restrict(other, target, level.count)
        else:
            restrict_last(other, source3)
    first = HALO_ROWS // GROUP
    for at in range(len(FULL) + 2):
        coarsest[at] = matrix3[at, first : first + rows // GROUP, :]


def restrict_last(residual, target):
    class Planes:
        def __setitem__(self, where, value):
            target[where[0]] = value

    restrict(residual, Planes(), 2)


def up_kernel(
    place, coarse, coarse_before, coarse_after,
    matrix0, inverse0, source0, x0_in, matrix1, inverse1, source1, x1_in, matrix2, inverse2, source2, x2_in,
    displacement,
    x0, other0, x1, other1, x2, other2, spill0, spill1, spill2, spill3, matrix3, inverse3, source3, x3, other3,
    stacked, gathered, tiles,
    *, rows, cols, gx, gy,
):
    block = rows // GROUP
    for at in range(len(FULL) + 2):
        for piece, part in enumerate((coarse_before, coarse, coarse_after)):
            if at < len(FULL):
                matrix3[at, 0, 0, piece * block : (piece + 1) * block, :] = part[at]
            else:
                source3[at - len(FULL), 0, 0, piece * block : (piece + 1) * block, :] = part[at]
    level3 = Level(matrix3, FULL_AT, inverse3, spill3)
    level3.make_inverse(*edge_masks(place, (3 * block, LANES), rows, cols, -rows, gx * rows, gy * cols))
    start(level3, x3, source3)
    now, then = x3, other3
    for _ in range(COARSE_SWEEPS - 1):
        apply(level3, now, source3, then, residual=False)
        now, then = then, now
    offset = block - HALO_ROWS // GROUP
    side = (rows + 2 * HALO_ROWS) // GROUP
    coarse_plane = functools.partial(cut_plane, now, offset, side)

    level0 = FineLevel(matrix0, {}, inverse0, spill0)
    level1 = Level(matrix1, FIRST_AT, inverse1, spill1)
    level2 = Level(matrix2, FULL_AT, inverse2, spill2)
    for level, source, before, x, other in (
        (level2, source2, x2_in, x2, other2),
        (level1, source1, x1_in, x1, other1),
        (level0, source0, x0_in, x0, other0),
    ):
        prolong(coarse_plane, before, x, level.count)
        close_columns(level, x)
        apply(level, x, source, other, residual=False)
        apply(level, other, source, x, residual=False)
        coarse_plane = functools.partial(whole_plane, x)

    for tile in range(cols // LANES):
        at = lax.broadcasted_iota(jnp.int32, (GROUP * LANES, LANES), 1) + tile * LANES + HALO_COLS
        target = (at & (GROUP - 1)) * LANES + (at >> LEVELS)
        line = lax.broadcasted_iota(jnp.int32, (GROUP * LANES, LANES), 0)
        gathered[:, tile * LANES : (tile + 1) * LANES] = jnp.where(line == target, 1.0, 0.0).astype(BF16)
    first = HALO_ROWS // GROUP
    for component in (0, 1):
        for pair in range(GROUP // 2):
            for k in range(GROUP):
                value = jnp.concatenate(
                    [x0[component, 2 * pair + h, k, first : first + block, :] for h in (0, 1)], axis=0
                )
                for part, piece in enumerate(three_parts(value)):
                    line = part * 2 * rows + component * rows + pair * 2 * block
                    stacked[line : line + 2 * block, k * LANES : (k + 1) * LANES] = piece
    product = jnp.dot(stacked[...], gathered[...], preferred_element_type=F32)
    product = product[: 2 * rows] + product[2 * rows : 4 * rows] + product[4 * rows :]
    for component in (0, 1):
        for tile in range(cols // LANES):
            lanes = slice(tile * LANES, (tile + 1) * LANES)
            for m in range(GROUP):
                line = component * rows + m * block
                tiles[component, tile, pl.ds(m, block, stride=GROUP), :] = product[line : line + block, lanes]
            displacement[component, :, lanes] = tiles[component, tile]


def cut_plane(x, offset, side, component, m, k):
    return x[component, 0, 0, offset : offset + side, :]


def whole_plane(x, component, m, k):
    return x[component, m, k]


def body(first_lame, shear_modulus, applied_load, plastic_owner, plastic_cell, plastic_code):
    rows, cols = first_lame.shape
    gx, gy = lax.axis_size("gx"), lax.axis_size("gy")
    devices = gx * gy
    place = jnp.stack([lax.axis_index("gx"), lax.axis_index("gy")]).astype(jnp.int32)

    word = (plastic_owner[:, 0] * (rows * cols) + plastic_cell) * 4 + plastic_code
    fields = [first_lame, shear_modulus, applied_load[0], applied_load[1]]
    first_cols = jnp.stack([field[:, :HALO_COLS] for field in fields])
    last_cols = jnp.stack([field[:, -HALO_COLS:] for field in fields])
    left = passed_along(last_cols, "gy", 1)
    right = passed_along(first_cols, "gy", -1)

    words = lax.all_to_all(
        jnp.broadcast_to(word[None], (devices, word.shape[0])), ("gx", "gy"), 0, 0, tiled=True
    )
    words, left, right = lax.optimization_barrier((words, left, right))

    def whole_rows(span):
        return jnp.concatenate(
            [jnp.stack([field[span] for field in fields]), left[:, span], right[:, span]], axis=2
        )

    upper = passed_along(whole_rows(slice(rows - HALO_ROWS, rows)), "gx", 1)
    lower = passed_along(whole_rows(slice(0, HALO_ROWS)), "gx", -1)
    factor = yield_factor(place, words, rows, cols, gy)

    tall, wide = rows + 2 * HALO_ROWS, cols + 2 * HALO_COLS
    side = tall // GROUP
    vmem, smem = pl.BlockSpec(memory_space=pltpu.VMEM), pl.BlockSpec(memory_space=pltpu.SMEM)

    def planes(fields, count, extra=0, lines=side):
        return (fields, count, count + extra, lines, LANES)

    state = []
    for count, entries, inverses in ((GROUP, 3, 1), (GROUP // 2, len(FIRST), 2), (GROUP // 4, len(FULL), 2)):
        state += [planes(entries, count), planes(inverses, count), planes(2, count), planes(2, count, 1)]
    held = len(FULL) + 2
    counts = (GROUP, GROUP // 2, GROUP // 4)
    *state, coarse = pl.pallas_call(
        functools.partial(down_kernel, rows=rows, cols=cols, gx=gx, gy=gy),
        out_shape=[jax.ShapeDtypeStruct(shape, F32) for shape in state]
        + [jax.ShapeDtypeStruct((held, rows // GROUP, LANES), F32)],
        in_specs=[smem] + [vmem] * 8,
        out_specs=[vmem] * (len(state) + 1),
        scratch_shapes=[
            pltpu.VMEM((wide // LANES, tall, LANES), F32),
            pltpu.VMEM((3 * tall, wide), BF16),
            pltpu.VMEM((wide, GROUP * LANES), BF16),
        ]
        + [pltpu.VMEM(planes(2, count, 1), F32) for count in counts]
        + [pltpu.VMEM((2, count, side, LANES), F32) for count in counts]
        + [pltpu.VMEM((held, side, LANES), F32)],
        compiler_params=pltpu.CompilerParams(vmem_limit_bytes=VMEM_LIMIT),
        name="descent",
    )(place, first_lame, shear_modulus, applied_load, left, right, upper, lower, factor)

    coarse_before = passed_along(coarse, "gx", 1)
    coarse_after = passed_along(coarse, "gx", -1)
    lines = 3 * (rows // GROUP)
    return pl.pallas_call(
        functools.partial(up_kernel, rows=rows, cols=cols, gx=gx, gy=gy),
        out_shape=jax.ShapeDtypeStruct((2, rows, cols), F32),
        in_specs=[smem] + [vmem] * (3 + len(state)),
        out_specs=vmem,
        scratch_shapes=[
            shape
            for count in counts
            for shape in (pltpu.VMEM(planes(2, count, 1), F32),) * 2
        ]
        + [pltpu.VMEM((2, count, side, LANES), F32) for count in counts]
        + [
            pltpu.VMEM((2, 1, lines, LANES), F32),
            pltpu.VMEM(planes(len(FULL), 1, 0, lines), F32),
            pltpu.VMEM(planes(2, 1, 0, lines), F32),
            pltpu.VMEM(planes(2, 1, 0, lines), F32),
            pltpu.VMEM(planes(2, 1, 1, lines), F32),
            pltpu.VMEM(planes(2, 1, 1, lines), F32),
            pltpu.VMEM((6 * rows, GROUP * LANES), BF16),
            pltpu.VMEM((GROUP * LANES, cols), BF16),
            pltpu.VMEM((2, cols // LANES, rows, LANES), F32),
        ],
        compiler_params=pltpu.CompilerParams(vmem_limit_bytes=VMEM_LIMIT),
        name="ascent",
    )(place, coarse, coarse_before, coarse_after, *state)


def solution(mesh):
    return jax.shard_map(
        body,
        mesh=mesh,
        in_specs=(
            P("gx", "gy"),
            P("gx", "gy"),
            P(None, "gx", "gy"),
            P(("gx", "gy"), None),
            P(("gx", "gy")),
            P(("gx", "gy")),
        ),
        out_specs=P(None, "gx", "gy"),
        check_vma=False,
    )
```

time: 797 us -> 71.1 us (0.09); the launches traced: 783 us -> 70.2 us
  starting transfers between devices: 265 us -> 23.6 us
  other arithmetic: 170 us -> 2.15 us
  waiting for transfers between devices: 139 us -> 5.82 us
  local copies, waits for them, and re-layouts: 130 us -> 5.32 us
  blocking collectives: 62.4 us -> 0 us
  Pallas kernels: 0 us -> 33.1 us
  matrix products: 13.5 us -> 0 us
    ppermute x88 -> x6, starting transfers between devices: 265 us -> 16.5 us  [passed_along(): return lax.ppermute(array, axis, pairs)]
    ppermute x88 -> x6, waiting for transfers between devices: 139 us -> 5.25 us  [passed_along(): return lax.ppermute(array, axis, pairs)]
    scatter-add x1 -> x0, other arithmetic: 85.9 us -> none  [plastic_totals(): jnp.zeros((cell_count,), jnp.int32).at[arrived_cell].add(arrived_code)]
    all_gather x1 -> x0, blocking collectives: 62.4 us -> none  [plastic_totals(): all_words = lax.all_gather(entry_word, ('gx', 'gy'), axis=0, tiled=True)]
    add x103 -> x1, other arithmetic: 40.8 us -> 0.7 us  [body(): (plastic_owner[:, 0] * (rows * cols) + plastic_cell) * 4 + plastic_code]
    slice x88 -> x3, local copies, waits for them, and re-layouts: 34.9 us -> 0.04 us  [the longest x1 0.02 us: whole_rows(): field[span]]
    pallas_call x0 -> x3, Pallas kernels: none -> 33.1 us  [the longest x1 12.5 us: yield_factor(): pl.pallas_call(functools.partial(factor_kernel, rows=rows, cols=cols, gy=...]
    reshape x8 -> x0, local copies, waits for them, and re-layouts: 24.1 us -> none  [the longest x2 19.5 us: by_subcell(): values.reshape(half_rows, 2, half_cols, 2).transpose(1, 3, 0, 2)]
  transfers between devices with their start and end apart: 88 -> 7, of which waited for: 70 -> 4; matrix products, arithmetic and copies ran while one was open for 20% -> 5% of each run, Pallas kernels for 0% -> 18%
where the time goes in v1:
time: 71.1 us; the launch traced here: 70.2 us
  Pallas kernels  33.1 us (47%)
  starting transfers between devices  23.6 us (33%)
  waiting for transfers between devices  5.82 us (8%)
  local copies, waits for them, and re-layouts  5.32 us (7%)
  other arithmetic  2.15 us (3%)
    ppermute x6, starting transfers between devices, passed_along(): return lax.ppermute(array, axis, pairs)  16.5 us
    pallas_call x1, Pallas kernels, yield_factor(): pl.pallas_call(functools.partial(factor_kernel, rows=rows, cols=cols, gy=...  12.5 us
    pallas_call x1, Pallas kernels, body(): pl.pallas_call(functools.partial(down_kernel, rows=rows, cols=cols, gx=gx...  11.6 us
    pallas_call x1, Pallas kernels, body(): pl.pallas_call(functools.partial(up_kernel, rows=rows, cols=cols, gx=gx,...  8.91 us
    all_to_all x1, starting transfers between devices, body(): lax.all_to_all(jnp.broadcast_to(word[None], (devices, word.shape[0])), ('...  7.1 us
    ppermute x6, waiting for transfers between devices, passed_along(): return lax.ppermute(array, axis, pairs)  5.25 us
    unnamed x19, local copies, waits for them, and re-layouts  2.77 us
  transfers between devices with their start and end apart: 7, of which 4 were waited for; matrix products, arithmetic and copies ran while one was open for 5% of the time, Pallas kernels for 18%

profile of v1, /device:TPU:1, one launch (start us, length us, event | category | flops | bytes accessed | tf_op | source)
XLA Modules:
  0.0 70.2 jit_solution(8036845790646124069)
XLA Ops:
  0.0 0.0 copy-start
  0.0 0.0 copy-start.2
  0.0 0.0 copy-start.1
  0.0 0.7 %broadcast_multiply_fusion = s32[512,1]{0,1:T(1,128)S(1)} fusion(s32[512,1]{0,1:T(1,128)} %param.9), kind=kLoop, calls=%fused_computation.20 | loop fusion | flops 512 | bytes 4096 | tf_op jit(solution)/shard_map/mul | solution.py:636
  0.8 0.7 %multiply_add_fusion = s32[512]{0:T(512)S(1)} fusion(s32[512]{0:T(512)} %param.11, s32[512]{0:T(512)S(1)} %bitcast.35, s32[512]{0:T(512)} %param.10), kind=kLoop, calls=%fused_computation.19 | loop fusion | flops 1536 | bytes 8192 | tf_op jit(solution)/shard_map/add | solution.py:636
  1.5 0.7 broadcast_in_dim.2
  2.1 7.1 %all-to-all-start = ((s32[32,1,512]{2,1,0:T(1,128)}), s32[32,1,512]{2,1,0:T(1,128)S(1)}, u32[]{:S(2)}, u32[]{:S(2)}) async-start(s32[32,1,512]{2,1,0:T(1,128)} %broadcast_in_dim.2), calls=%async_computation | async-start | bytes 131072 | tf_op jit(solution)/shard_map/all_to_all | solution.py:643
  9.2 1.0 %slice_bitcast_fusion.1 = (f32[64,512]{1,0:T(8,128)S(1)}, f32[64,512]{1,0:T(8,128)S(1)}) fusion(f32[2,64,512]{2,1,0:T(8,128)} %applied_load.1), kind=kLoop, calls=%fused_computation.5 | loop fusion | bytes 524288 | tf_op jit(solution)/shard_map/squeeze | solution.py:637
  10.2 0.8 %slice_bitcast_fusion.10 = (f32[1,64,128]{2,1,0:T(8,128)S(1)}, f32[1,64,128]{2,1,0:T(8,128)S(1)}, f32[1,64,128]{2,1,0:T(8,128)S(1)}, f32[1,64,128]{2,1,0:T(8,128)S(1)}) fusion(f32[64,512]{1,0:T(8,128)} %shear_modulus.1, f32[64,512]{1,0:T(8,128)} %first_lame.1), kind=kLoop, calls=%fused_computation.15 | loop fusion | bytes 262144 | tf_op jit(solution)/shard_map/stack | solution.py:638
  11.1 3.3 %collective-permute-start = (f32[4,64,128]{2,1,0:T(8,128)S(1)}, f32[4,64,128]{2,1,0:T(8,128)S(1)}, u32[]{:S(2)}, u32[]{:S(2)}) collective-permute-start(f32[4,64,128]{2,1,0:T(8,128)S(1)} %pad_maximum_fusion.2), channel_id=1, source_target_pairs={{0,1},{1,2},{2,3},{3,4},{4,5},{5,6},{6,7},{8,9},{9,10},{10,11},{11... | collective-permute-start | bytes 393224 | tf_op jit(solution)/shard_map/ppermute | solution.py:33
  14.4 1.3 %collective-permute-start.1 = (f32[4,64,128]{2,1,0:T(8,128)S(1)}, f32[4,64,128]{2,1,0:T(8,128)S(1)}, u32[]{:S(2)}, u32[]{:S(2)}) collective-permute-start(f32[4,64,128]{2,1,0:T(8,128)S(1)} %pad_maximum_fusion.3), channel_id=1, source_target_pairs={{1,0},{2,1},{3,2},{4,3},{5,4},{6,5},{7,6},{9,8},{10,9},{11,10},{12... | collective-permute-start | bytes 393224 | tf_op jit(solution)/shard_map/ppermute | solution.py:33
  15.7 0.0 copy-done.2
  15.7 0.0 copy-done.1
  15.8 0.0 copy-done
  15.8 0.6 all-to-all-done
  16.4 0.6 copy.9
  17.0 0.0 collective-permute-done.left
  17.0 0.0 copy-start.3
  17.0 3.7 %collective-permute-done.1.right = f32[4,64,128]{2,1,0:T(8,128)S(1)} collective-permute-done((f32[4,64,128]{2,1,0:T(8,128)S(1)}, f32[4,64,128]{2,1,0:T(8,128)S(1)}, u32[]{:S(2)}, u32[]{:S(2)}) %collective-permute-start.1) | collective-permute-done | bytes 131104 | tf_op jit(solution)/shard_map/ppermute | solution.py:33
  20.7 0.0 copy-start.4
  20.8 4.5 %collective-permute-start.2 = (f32[4,32,768]{2,1,0:T(8,128)S(1)}, f32[4,32,768]{2,1,0:T(8,128)S(1)}, u32[]{:S(2)}, u32[]{:S(2)}) collective-permute-start(f32[4,32,768]{2,1,0:T(8,128)S(1)} %pad_maximum_fusion), channel_id=1, source_target_pairs={{0,8},{8,16},{16,24},{1,9},{9,17},{17,25},{2,10},{10,18},{18,26},{... | collective-permute-start | bytes 1179656 | tf_op jit(solution)/shard_map/ppermute | solution.py:33
  25.3 1.9 %collective-permute-start.3 = (f32[4,32,768]{2,1,0:T(8,128)S(1)}, f32[4,32,768]{2,1,0:T(8,128)S(1)}, u32[]{:S(2)}, u32[]{:S(2)}) collective-permute-start(f32[4,32,768]{2,1,0:T(8,128)S(1)} %pad_maximum_fusion.1), channel_id=1, source_target_pairs={{8,0},{16,8},{24,16},{9,1},{17,9},{25,17},{10,2},{18,10},{26,18},{... | collective-permute-start | bytes 1179656 | tf_op jit(solution)/shard_map/ppermute | solution.py:33
  27.2 0.6 pad_add_fusion.place
  27.9 12.5 %yield_factor.1.factor = f32[6,128,128]{2,1,0:T(8,128)} custom-call(s32[2]{0:T(128)} %pad_add_fusion.place, s32[32,512]{1,0:T(8,128)} %bitcast.34), custom_call_target="tpu_custom_call" | custom-call | flops 1000000000 | bytes 1000000 | tf_op jit(solution)/shard_map/yield_factor/pallas_call | solution.py:100
  40.4 0.0 copy-done.3
  40.4 0.0 copy-done.4
  40.4 0.0 collective-permute-done.2.upper
  40.4 0.0 copy-start.5
  40.4 0.0 collective-permute-done.3.lower
  40.4 0.7 %copy-done.5 = f32[4,32,768]{2,1,0:T(8,128)} copy-done((f32[4,32,768]{2,1,0:T(8,128)}, f32[4,32,768]{2,1,0:T(8,128)S(1)}, u32[]{:S(2)}) %copy-start.5) | copy-done | bytes 393240
  41.2 0.0 copy-start.6
  41.2 0.7 %copy-done.6 = f32[4,32,768]{2,1,0:T(8,128)} copy-done((f32[4,32,768]{2,1,0:T(8,128)}, f32[4,32,768]{2,1,0:T(8,128)S(1)}, u32[]{:S(2)}) %copy-start.6) | copy-done | bytes 393240
  41.9 11.6 %descent.1 = (f32[3,8,8,16,128]{4,3,2,1,0:T(8,128)}, f32[1,8,8,16,128]{4,3,2,1,0:T(8,128)}, f32[2,8,8,16,128]{4,3,2,1,0:T(8,128)}, f32[2,8,9,16,128]{4,3,2,1,0:T...) custom-call(s32[2]{0:T(128)} %pad_add_fusion.place, ...), custom_call_target="tpu_custom_call" | custom-call | tf_op jit(solution)/shard_map/descent/pallas_call | solution.py:669
  53.5 1.9 %collective-permute-start.5 = (f32[14,8,128]{2,1,0:T(8,128)}, f32[14,8,128]{2,1,0:T(8,128)S(1)}, u32[]{:S(2)}, u32[]{:S(2)}) collective-permute-start(f32[14,8,128]{2,1,0:T(8,128)} %get-tuple-element.24.coarse), channel_id=1, source_target_pairs={{8,0},{16,8},{24,16},{9,1},{17,9},{25,17},{10,2},{18,10},{26,18},{... | collective-permute-start | bytes 172040 | tf_op jit(solution)/shard_map/ppermute | solution.py:33
  55.4 3.6 %collective-permute-start.4 = (f32[14,8,128]{2,1,0:T(8,128)}, f32[14,8,128]{2,1,0:T(8,128)S(1)}, u32[]{:S(2)}, u32[]{:S(2)}) collective-permute-start(f32[14,8,128]{2,1,0:T(8,128)} %get-tuple-element.24.coarse), channel_id=1, source_target_pairs={{0,8},{8,16},{16,24},{1,9},{9,17},{17,25},{2,10},{10,18},{18,26},{... | collective-permute-start | bytes 172040 | tf_op jit(solution)/shard_map/ppermute | solution.py:33
  59.1 0.1 collective-permute-done.5.coarse_after
  59.2 0.0 copy-start.7
  59.2 1.4 %collective-permute-done.4.coarse_before = f32[14,8,128]{2,1,0:T(8,128)S(1)} collective-permute-done((f32[14,8,128]{2,1,0:T(8,128)}, f32[14,8,128]{2,1,0:T(8,128)S(1)}, u32[]{:S(2)}, u32[]{:S(2)}) %collective-permute-start.4) | collective-permute-done | bytes 57376 | tf_op jit(solution)/shard_map/ppermute | solution.py:33
  60.6 0.0 copy-start.8
  60.6 0.0 copy-done.7
  60.7 0.6 copy-done.8
  61.3 8.9 %ascent.1 = f32[2,64,512]{2,1,0:T(8,128)} custom-call(s32[2]{0:T(128)} %pad_add_fusion.place, f32[14,8,128]{2,1,0:T(8,128)} %get-tuple-element.24.coarse, f32[14,8,128]{2,1,0:T(8,128)} %copy-done.8, f32[14,8,128]{2,1,0:T(8,128)} %copy-done.7, f32[3,8,8,16,128]{4,3,2,1,0:T(8,128)} %get-tuple-element.25.matrix0, ...), custom_call_target="tpu_custom_call" | custom-call | tf_op jit(solution)/shard_map/ascent/pallas_call | solution.py:690
  (9 shorter events, 0.2 us)
Async XLA Ops:
  0.0 15.8 %copy-start = (f32[2,64,512]{2,1,0:T(8,128)S(1)}, f32[2,64,512]{2,1,0:T(8,128)}, u32[]{:S(2)}) copy-start(f32[2,64,512]{2,1,0:T(8,128)} %applied_load.1) | copy-start | bytes 786436
  0.0 15.7 %copy-start.2 = (f32[64,512]{1,0:T(8,128)S(1)}, f32[64,512]{1,0:T(8,128)}, u32[]{:S(2)}) copy-start(f32[64,512]{1,0:T(8,128)} %shear_modulus.1) | copy-start | bytes 393220
  0.0 15.7 %copy-start.1 = (f32[64,512]{1,0:T(8,128)S(1)}, f32[64,512]{1,0:T(8,128)}, u32[]{:S(2)}) copy-start(f32[64,512]{1,0:T(8,128)} %first_lame.1) | copy-start | bytes 393220
  2.1 14.2 %all-to-all-start = ((s32[32,1,512]{2,1,0:T(1,128)}), s32[32,1,512]{2,1,0:T(1,128)S(1)}, u32[]{:S(2)}, u32[]{:S(2)}) async-start(s32[32,1,512]{2,1,0:T(1,128)} %broadcast_in_dim.2), calls=%async_computation | async-start | bytes 131072 | tf_op jit(solution)/shard_map/all_to_all | solution.py:643
  11.1 5.9 %collective-permute-start = (f32[4,64,128]{2,1,0:T(8,128)S(1)}, f32[4,64,128]{2,1,0:T(8,128)S(1)}, u32[]{:S(2)}, u32[]{:S(2)}) collective-permute-start(f32[4,64,128]{2,1,0:T(8,128)S(1)} %pad_maximum_fusion.2), channel_id=1, source_target_pairs={{0,1},{1,2},{2,3},{3,4},{4,5},{5,6},{6,7},{8,9},{9,10},{10,11},{11... | collective-permute-start | bytes 393224 | tf_op jit(solution)/shard_map/ppermute | solution.py:33
  14.4 6.3 %collective-permute-start.1 = (f32[4,64,128]{2,1,0:T(8,128)S(1)}, f32[4,64,128]{2,1,0:T(8,128)S(1)}, u32[]{:S(2)}, u32[]{:S(2)}) collective-permute-start(f32[4,64,128]{2,1,0:T(8,128)S(1)} %pad_maximum_fusion.3), channel_id=1, source_target_pairs={{1,0},{2,1},{3,2},{4,3},{5,4},{6,5},{7,6},{9,8},{10,9},{11,10},{12... | collective-permute-start | bytes 393224 | tf_op jit(solution)/shard_map/ppermute | solution.py:33
  17.0 23.4 %copy-start.3 = (f32[4,64,128]{2,1,0:T(8,128)}, f32[4,64,128]{2,1,0:T(8,128)S(1)}, u32[]{:S(2)}) copy-start(f32[4,64,128]{2,1,0:T(8,128)S(1)} %collective-permute-done.left) | copy-start | bytes 393220
  20.7 19.7 %copy-start.4 = (f32[4,64,128]{2,1,0:T(8,128)}, f32[4,64,128]{2,1,0:T(8,128)S(1)}, u32[]{:S(2)}) copy-start(f32[4,64,128]{2,1,0:T(8,128)S(1)} %collective-permute-done.1.right) | copy-start | bytes 393220
  20.8 19.6 %collective-permute-start.2 = (f32[4,32,768]{2,1,0:T(8,128)S(1)}, f32[4,32,768]{2,1,0:T(8,128)S(1)}, u32[]{:S(2)}, u32[]{:S(2)}) collective-permute-start(f32[4,32,768]{2,1,0:T(8,128)S(1)} %pad_maximum_fusion), channel_id=1, source_target_pairs={{0,8},{8,16},{16,24},{1,9},{9,17},{17,25},{2,10},{10,18},{18,26},{... | collective-permute-start | bytes 1179656 | tf_op jit(solution)/shard_map/ppermute | solution.py:33
  25.3 15.1 %collective-permute-start.3 = (f32[4,32,768]{2,1,0:T(8,128)S(1)}, f32[4,32,768]{2,1,0:T(8,128)S(1)}, u32[]{:S(2)}, u32[]{:S(2)}) collective-permute-start(f32[4,32,768]{2,1,0:T(8,128)S(1)} %pad_maximum_fusion.1), channel_id=1, source_target_pairs={{8,0},{16,8},{24,16},{9,1},{17,9},{25,17},{10,2},{18,10},{26,18},{... | collective-permute-start | bytes 1179656 | tf_op jit(solution)/shard_map/ppermute | solution.py:33
  40.4 0.8 %copy-start.5 = (f32[4,32,768]{2,1,0:T(8,128)}, f32[4,32,768]{2,1,0:T(8,128)S(1)}, u32[]{:S(2)}) copy-start(f32[4,32,768]{2,1,0:T(8,128)S(1)} %collective-permute-done.2.upper) | copy-start | bytes 1179652
  41.2 0.7 %copy-start.6 = (f32[4,32,768]{2,1,0:T(8,128)}, f32[4,32,768]{2,1,0:T(8,128)S(1)}, u32[]{:S(2)}) copy-start(f32[4,32,768]{2,1,0:T(8,128)S(1)} %collective-permute-done.3.lower) | copy-start | bytes 1179652
  53.5 5.7 %collective-permute-start.5 = (f32[14,8,128]{2,1,0:T(8,128)}, f32[14,8,128]{2,1,0:T(8,128)S(1)}, u32[]{:S(2)}, u32[]{:S(2)}) collective-permute-start(f32[14,8,128]{2,1,0:T(8,128)} %get-tuple-element.24.coarse), channel_id=1, source_target_pairs={{8,0},{16,8},{24,16},{9,1},{17,9},{25,17},{10,2},{18,10},{26,18},{... | collective-permute-start | bytes 172040 | tf_op jit(solution)/shard_map/ppermute | solution.py:33
  55.4 5.2 %collective-permute-start.4 = (f32[14,8,128]{2,1,0:T(8,128)}, f32[14,8,128]{2,1,0:T(8,128)S(1)}, u32[]{:S(2)}, u32[]{:S(2)}) collective-permute-start(f32[14,8,128]{2,1,0:T(8,128)} %get-tuple-element.24.coarse), channel_id=1, source_target_pairs={{0,8},{8,16},{16,24},{1,9},{9,17},{17,25},{2,10},{10,18},{18,26},{... | collective-permute-start | bytes 172040 | tf_op jit(solution)/shard_map/ppermute | solution.py:33
  59.2 1.4 %copy-start.7 = (f32[14,8,128]{2,1,0:T(8,128)}, f32[14,8,128]{2,1,0:T(8,128)S(1)}, u32[]{:S(2)}) copy-start(f32[14,8,128]{2,1,0:T(8,128)S(1)} %collective-permute-done.5.coarse_after) | copy-start | bytes 172036
  60.6 0.6 copy-start.8

commit v2 on v1

--- a/solution.py
+++ b/solution.py
@@ -17,7 +17,7 @@
 HALO_ROWS = 32
 HALO_COLS = 128
 LANES = 128
-VMEM_LIMIT = 56 * 1024 * 1024
+VMEM_LIMIT = 30 * 1024 * 1024
 F32 = jnp.float32
 BF16 = jnp.bfloat16
 

time: 71.1 us -> 61 us (0.86)
  Pallas kernels: 33.1 us -> 25.9 us
  local copies, waits for them, and re-layouts: 5.32 us -> 2.56 us
    pallas_call x1, Pallas kernels: 11.6 us -> 7.96 us  [body(): pl.pallas_call(functools.partial(down_kernel, rows=rows, cols=cols, gx=gx...]
    unnamed x19 -> x7, local copies, waits for them, and re-layouts: 2.77 us -> 0.02 us
    pallas_call x1, Pallas kernels: 8.91 us -> 6.44 us  [body(): pl.pallas_call(functools.partial(up_kernel, rows=rows, cols=cols, gx=gx,...]
    pallas_call x1, Pallas kernels: 12.5 us -> 11.5 us  [yield_factor(): pl.pallas_call(functools.partial(factor_kernel, rows=rows, cols=cols, gy=...]
  transfers between devices with their start and end apart: 7 -> 7, of which waited for: 4 -> 4; matrix products, arithmetic and copies ran while one was open for 5% -> 3% of each run, Pallas kernels for 18% -> 19%
where the time goes in v2:
time: 61 us; the launch traced here: 60 us
  Pallas kernels  25.9 us (42%)
  starting transfers between devices  23.7 us (39%)
  waiting for transfers between devices  6.14 us (10%)
  local copies, waits for them, and re-layouts  2.56 us (4%)
  other arithmetic  1.61 us (3%)
    ppermute x6, starting transfers between devices, passed_along(): return lax.ppermute(array, axis, pairs)  16.6 us
    pallas_call x1, Pallas kernels, yield_factor(): pl.pallas_call(functools.partial(factor_kernel, rows=rows, cols=cols, gy=...  11.5 us
    pallas_call x1, Pallas kernels, body(): pl.pallas_call(functools.partial(down_kernel, rows=rows, cols=cols, gx=gx...  7.96 us
    all_to_all x1, starting transfers between devices, body(): lax.all_to_all(jnp.broadcast_to(word[None], (devices, word.shape[0])), ('...  7.1 us
    pallas_call x1, Pallas kernels, body(): pl.pallas_call(functools.partial(up_kernel, rows=rows, cols=cols, gx=gx,...  6.44 us
    ppermute x6, waiting for transfers between devices, passed_along(): return lax.ppermute(array, axis, pairs)  5.56 us
  transfers between devices with their start and end apart: 7, of which 4 were waited for; matrix products, arithmetic and copies ran while one was open for 3% of the time, Pallas kernels for 19%

profile of v2, /device:TPU:1, one launch (start us, length us, event | category | flops | bytes accessed | tf_op | source)
XLA Modules:
  0.0 60.0 jit_solution(11586954551336792579)
XLA Ops:
  0.0 0.0 copy-start
  0.0 0.0 copy-start.2
  0.0 0.0 copy-start.1
  0.0 0.7 %broadcast_multiply_fusion = s32[512,1]{0,1:T(1,128)S(1)} fusion(s32[512,1]{0,1:T(1,128)} %param.9), kind=kLoop, calls=%fused_computation.20 | loop fusion | flops 512 | bytes 4096 | tf_op jit(solution)/shard_map/mul | solution.py:636
  0.8 0.7 %multiply_add_fusion = s32[512]{0:T(512)S(1)} fusion(s32[512]{0:T(512)} %param.11, s32[512]{0:T(512)S(1)} %bitcast.35, s32[512]{0:T(512)} %param.10), kind=kLoop, calls=%fused_computation.19 | loop fusion | flops 1536 | bytes 8192 | tf_op jit(solution)/shard_map/add | solution.py:636
  1.5 0.7 %broadcast_in_dim.2 = s32[32,1,512]{2,1,0:T(1,128)} broadcast(s32[512]{0:T(512)S(1)} %multiply_add_fusion), dimensions={2} | broadcast | bytes 67584 | tf_op jit(solution)/shard_map/broadcast_in_dim | solution.py:644
  2.1 7.1 %all-to-all-start = ((s32[32,1,512]{2,1,0:T(1,128)}), s32[32,1,512]{2,1,0:T(1,128)S(1)}, u32[]{:S(2)}, u32[]{:S(2)}) async-start(s32[32,1,512]{2,1,0:T(1,128)} %broadcast_in_dim.2), calls=%async_computation | async-start | bytes 131072 | tf_op jit(solution)/shard_map/all_to_all | solution.py:643
  9.2 1.0 %slice_bitcast_fusion.1 = (f32[64,512]{1,0:T(8,128)S(1)}, f32[64,512]{1,0:T(8,128)S(1)}) fusion(f32[2,64,512]{2,1,0:T(8,128)} %applied_load.1), kind=kLoop, calls=%fused_computation.5 | loop fusion | bytes 524288 | tf_op jit(solution)/shard_map/squeeze | solution.py:637
  10.2 0.8 %slice_bitcast_fusion.10 = (f32[1,64,128]{2,1,0:T(8,128)S(1)}, f32[1,64,128]{2,1,0:T(8,128)S(1)}, f32[1,64,128]{2,1,0:T(8,128)S(1)}, f32[1,64,128]{2,1,0:T(8,128)S(1)}) fusion(f32[64,512]{1,0:T(8,128)} %shear_modulus.1, f32[64,512]{1,0:T(8,128)} %first_lame.1), kind=kLoop, calls=%fused_computation.15 | loop fusion | bytes 262144 | tf_op jit(solution)/shard_map/stack | solution.py:638
  11.1 3.3 %collective-permute-start = (f32[4,64,128]{2,1,0:T(8,128)S(1)}, f32[4,64,128]{2,1,0:T(8,128)S(1)}, u32[]{:S(2)}, u32[]{:S(2)}) collective-permute-start(f32[4,64,128]{2,1,0:T(8,128)S(1)} %pad_maximum_fusion.2), channel_id=1, source_target_pairs={{0,1},{1,2},{2,3},{3,4},{4,5},{5,6},{6,7},{8,9},{9,10},{10,11},{11... | collective-permute-start | bytes 393224 | tf_op jit(solution)/shard_map/ppermute | solution.py:33
  14.4 1.3 %collective-permute-start.1 = (f32[4,64,128]{2,1,0:T(8,128)S(1)}, f32[4,64,128]{2,1,0:T(8,128)S(1)}, u32[]{:S(2)}, u32[]{:S(2)}) collective-permute-start(f32[4,64,128]{2,1,0:T(8,128)S(1)} %pad_maximum_fusion.3), channel_id=1, source_target_pairs={{1,0},{2,1},{3,2},{4,3},{5,4},{6,5},{7,6},{9,8},{10,9},{11,10},{12... | collective-permute-start | bytes 393224 | tf_op jit(solution)/shard_map/ppermute | solution.py:33
  15.7 0.0 copy-done.2
  15.7 0.0 copy-done.1
  15.8 0.0 copy-done
  15.8 0.6 all-to-all-done
  16.4 0.5 collective-permute-done.left
  16.9 3.8 %collective-permute-done.1.right = f32[4,64,128]{2,1,0:T(8,128)S(1)} collective-permute-done((f32[4,64,128]{2,1,0:T(8,128)S(1)}, f32[4,64,128]{2,1,0:T(8,128)S(1)}, u32[]{:S(2)}, u32[]{:S(2)}) %collective-permute-start.1) | collective-permute-done | bytes 131104 | tf_op jit(solution)/shard_map/ppermute | solution.py:33
  20.8 4.5 %collective-permute-start.2 = (f32[4,32,768]{2,1,0:T(8,128)S(1)}, f32[4,32,768]{2,1,0:T(8,128)S(1)}, u32[]{:S(2)}, u32[]{:S(2)}) collective-permute-start(f32[4,32,768]{2,1,0:T(8,128)S(1)} %pad_maximum_fusion), channel_id=1, source_target_pairs={{0,8},{8,16},{16,24},{1,9},{9,17},{17,25},{2,10},{10,18},{18,26},{... | collective-permute-start | bytes 1179656 | tf_op jit(solution)/shard_map/ppermute | solution.py:33
  25.3 1.9 %collective-permute-start.3 = (f32[4,32,768]{2,1,0:T(8,128)S(1)}, f32[4,32,768]{2,1,0:T(8,128)S(1)}, u32[]{:S(2)}, u32[]{:S(2)}) collective-permute-start(f32[4,32,768]{2,1,0:T(8,128)S(1)} %pad_maximum_fusion.1), channel_id=1, source_target_pairs={{8,0},{16,8},{24,16},{9,1},{17,9},{25,17},{10,2},{18,10},{26,18},{... | collective-permute-start | bytes 1179656 | tf_op jit(solution)/shard_map/ppermute | solution.py:33
  27.2 0.1 pad_add_fusion.place
  27.3 11.5 %yield_factor.1.factor = f32[6,128,128]{2,1,0:T(8,128)S(1)} custom-call(s32[2]{0:T(128)S(1)} %pad_add_fusion.place, s32[32,512]{1,0:T(8,128)S(1)} %bitcast.34), custom_call_target="tpu_custom_call" | custom-call | flops 1000000000 | bytes 1000000 | tf_op jit(solution)/shard_map/yield_factor/pallas_call | solution.py:100
  38.8 0.0 collective-permute-done.2.upper
  38.8 0.0 collective-permute-done.3.lower
  38.8 8.0 %descent.1 = (f32[3,8,8,16,128]{4,3,2,1,0:T(8,128)S(1)}, f32[1,8,8,16,128]{4,3,2,1,0:T(8,128)S(1)}, f32[2,8,8,16,128]{4,3,2,1,0:T(8,128)S(1)}, f32[2,8,9,16,128]...) custom-call(s32[2]{0:T(128)S(1)} %pad_add_fusion.place, ...), custom_call_target="tpu_custom_call" | custom-call | tf_op jit(solution)/shard_map/descent/pallas_call | solution.py:669
  46.8 1.9 %collective-permute-start.5 = (f32[14,8,128]{2,1,0:T(8,128)S(1)}, f32[14,8,128]{2,1,0:T(8,128)S(1)}, u32[]{:S(2)}, u32[]{:S(2)}) collective-permute-start(f32[14,8,128]{2,1,0:T(8,128)S(1)} %get-tuple-element.24.coarse), channel_id=1, source_target_pairs={{8,0},{16,8},{24,16},{9,1},{17,9},{25,17},{10,2},{18,10},{26,18},{... | collective-permute-start | bytes 172040 | tf_op jit(solution)/shard_map/ppermute | solution.py:33
  48.7 3.6 %collective-permute-start.4 = (f32[14,8,128]{2,1,0:T(8,128)S(1)}, f32[14,8,128]{2,1,0:T(8,128)S(1)}, u32[]{:S(2)}, u32[]{:S(2)}) collective-permute-start(f32[14,8,128]{2,1,0:T(8,128)S(1)} %get-tuple-element.24.coarse), channel_id=1, source_target_pairs={{0,8},{8,16},{16,24},{1,9},{9,17},{17,25},{2,10},{10,18},{18,26},{... | collective-permute-start | bytes 172040 | tf_op jit(solution)/shard_map/ppermute | solution.py:33
  52.4 0.0 collective-permute-done.5.coarse_after
  52.4 1.2 %collective-permute-done.4.coarse_before = f32[14,8,128]{2,1,0:T(8,128)S(1)} collective-permute-done((f32[14,8,128]{2,1,0:T(8,128)S(1)}, f32[14,8,128]{2,1,0:T(8,128)S(1)}, u32[]{:S(2)}, u32[]{:S(2)}) %collective-permute-start.4) | collective-permute-done | bytes 57376 | tf_op jit(solution)/shard_map/ppermute | solution.py:33
  53.6 6.4 %ascent.1 = f32[2,64,512]{2,1,0:T(8,128)} custom-call(s32[2]{0:T(128)S(1)} %pad_add_fusion.place, f32[14,8,128]{2,1,0:T(8,128)S(1)} %get-tuple-element.24.coarse, f32[14,8,128]{2,1,0:T(8,128)S(1)} %collective-permute-done.4.coarse_before, f32[14,8,128]{2,1,0:T(8,128)S(1)} %collective-permute-done.5.coarse_after, ...), custom_call_target="tpu_custom_call" | custom-call | tf_op jit(solution)/shard_map/ascent/pallas_call | solution.py:690
  (10 shorter events, 0.2 us)
Async XLA Ops:
  0.0 15.8 %copy-start = (f32[2,64,512]{2,1,0:T(8,128)S(1)}, f32[2,64,512]{2,1,0:T(8,128)}, u32[]{:S(2)}) copy-start(f32[2,64,512]{2,1,0:T(8,128)} %applied_load.1) | copy-start | bytes 786436
  0.0 15.7 %copy-start.2 = (f32[64,512]{1,0:T(8,128)S(1)}, f32[64,512]{1,0:T(8,128)}, u32[]{:S(2)}) copy-start(f32[64,512]{1,0:T(8,128)} %shear_modulus.1) | copy-start | bytes 393220
  0.0 15.7 %copy-start.1 = (f32[64,512]{1,0:T(8,128)S(1)}, f32[64,512]{1,0:T(8,128)}, u32[]{:S(2)}) copy-start(f32[64,512]{1,0:T(8,128)} %first_lame.1) | copy-start | bytes 393220
  2.1 14.2 %all-to-all-start = ((s32[32,1,512]{2,1,0:T(1,128)}), s32[32,1,512]{2,1,0:T(1,128)S(1)}, u32[]{:S(2)}, u32[]{:S(2)}) async-start(s32[32,1,512]{2,1,0:T(1,128)} %broadcast_in_dim.2), calls=%async_computation | async-start | bytes 131072 | tf_op jit(solution)/shard_map/all_to_all | solution.py:643
  11.1 5.8 %collective-permute-start = (f32[4,64,128]{2,1,0:T(8,128)S(1)}, f32[4,64,128]{2,1,0:T(8,128)S(1)}, u32[]{:S(2)}, u32[]{:S(2)}) collective-permute-start(f32[4,64,128]{2,1,0:T(8,128)S(1)} %pad_maximum_fusion.2), channel_id=1, source_target_pairs={{0,1},{1,2},{2,3},{3,4},{4,5},{5,6},{6,7},{8,9},{9,10},{10,11},{11... | collective-permute-start | bytes 393224 | tf_op jit(solution)/shard_map/ppermute | solution.py:33
  14.4 6.3 %collective-permute-start.1 = (f32[4,64,128]{2,1,0:T(8,128)S(1)}, f32[4,64,128]{2,1,0:T(8,128)S(1)}, u32[]{:S(2)}, u32[]{:S(2)}) collective-permute-start(f32[4,64,128]{2,1,0:T(8,128)S(1)} %pad_maximum_fusion.3), channel_id=1, source_target_pairs={{1,0},{2,1},{3,2},{4,3},{5,4},{6,5},{7,6},{9,8},{10,9},{11,10},{12... | collective-permute-start | bytes 393224 | tf_op jit(solution)/shard_map/ppermute | solution.py:33
  20.8 18.0 %collective-permute-start.2 = (f32[4,32,768]{2,1,0:T(8,128)S(1)}, f32[4,32,768]{2,1,0:T(8,128)S(1)}, u32[]{:S(2)}, u32[]{:S(2)}) collective-permute-start(f32[4,32,768]{2,1,0:T(8,128)S(1)} %pad_maximum_fusion), channel_id=1, source_target_pairs={{0,8},{8,16},{16,24},{1,9},{9,17},{17,25},{2,10},{10,18},{18,26},{... | collective-permute-start | bytes 1179656 | tf_op jit(solution)/shard_map/ppermute | solution.py:33
  25.3 13.5 %collective-permute-start.3 = (f32[4,32,768]{2,1,0:T(8,128)S(1)}, f32[4,32,768]{2,1,0:T(8,128)S(1)}, u32[]{:S(2)}, u32[]{:S(2)}) collective-permute-start(f32[4,32,768]{2,1,0:T(8,128)S(1)} %pad_maximum_fusion.1), channel_id=1, source_target_pairs={{8,0},{16,8},{24,16},{9,1},{17,9},{25,17},{10,2},{18,10},{26,18},{... | collective-permute-start | bytes 1179656 | tf_op jit(solution)/shard_map/ppermute | solution.py:33
  46.8 5.6 %collective-permute-start.5 = (f32[14,8,128]{2,1,0:T(8,128)S(1)}, f32[14,8,128]{2,1,0:T(8,128)S(1)}, u32[]{:S(2)}, u32[]{:S(2)}) collective-permute-start(f32[14,8,128]{2,1,0:T(8,128)S(1)} %get-tuple-element.24.coarse), channel_id=1, source_target_pairs={{8,0},{16,8},{24,16},{9,1},{17,9},{25,17},{10,2},{18,10},{26,18},{... | collective-permute-start | bytes 172040 | tf_op jit(solution)/shard_map/ppermute | solution.py:33
  48.7 4.9 %collective-permute-start.4 = (f32[14,8,128]{2,1,0:T(8,128)S(1)}, f32[14,8,128]{2,1,0:T(8,128)S(1)}, u32[]{:S(2)}, u32[]{:S(2)}) collective-permute-start(f32[14,8,128]{2,1,0:T(8,128)S(1)} %get-tuple-element.24.coarse), channel_id=1, source_target_pairs={{0,8},{8,16},{16,24},{1,9},{9,17},{17,25},{2,10},{10,18},{18,26},{... | collective-permute-start | bytes 172040 | tf_op jit(solution)/shard_map/ppermute | solution.py:33

commit v3 on v2

--- a/solution.py
+++ b/solution.py
@@ -17,6 +17,7 @@
 HALO_ROWS = 32
 HALO_COLS = 128
 LANES = 128
+LISTS_AT_ONCE = 16
 VMEM_LIMIT = 30 * 1024 * 1024
 F32 = jnp.float32
 BF16 = jnp.bfloat16
@@ -59,39 +60,42 @@
     return None if term is None else weight * term
 
 
-def factor_kernel(place, words, factor, rows_of, cols_of, codes, counts, *, rows, cols, gy):
+def factor_kernel(place, words, factor, tall_of, lane_of, codes, counts, *, rows, cols, gy):
     word = words[...]
     cell_bits = log2(rows * cols)
     owner = word >> (cell_bits + 2)
     cell = (word >> 2) & (rows * cols - 1)
     row = (owner >> log2(gy)) * rows + (cell >> log2(cols)) - place[0] * rows + HALO_ROWS
     col = (owner & (gy - 1)) * cols + (cell & (cols - 1)) - place[1] * cols
-    inside = (row >= 0) & (row < rows + 2 * HALO_ROWS) & (col >= -HALO_COLS) & (col < cols + HALO_COLS)
+    tall = rows + 2 * HALO_ROWS
+    inside = (row >= 0) & (row < tall) & (col >= -HALO_COLS) & (col < cols + HALO_COLS)
     at = jnp.where(col < 0, col + cols + HALO_COLS, jnp.where(col >= cols, col + HALO_COLS, col))
-    half = (cols + 2 * HALO_COLS) // 2
-    tall = rows + 2 * HALO_ROWS
-    upper = at >= half
-    rows_of[...] = jnp.where(inside, jnp.where(upper, row + tall, row), -1)
-    cols_of[...] = jnp.where(upper, at - half, at)
+    tall_of[...] = jnp.where(inside, row + tall * (at >> log2(2 * LANES)), -1)
+    lane_of[...] = at & (2 * LANES - 1)
     codes[...] = (word & 3).astype(F32)
     counts[...] = jnp.zeros_like(counts)
     length = words.shape[1]
-
-    @pl.loop(0, words.shape[0])
+    group = min(LISTS_AT_ONCE, words.shape[0])
+
+    @pl.loop(0, words.shape[0] // group)
     def _(i):
-        line = pl.ds(i, 1)
-        row_id = lax.broadcasted_iota(jnp.int32, (2 * tall, length), 0)
-        col_id = lax.broadcasted_iota(jnp.int32, (half, length), 0)
-        by_row = jnp.where(row_id == rows_of[line, :], codes[line, :], 0.0).astype(BF16)
-        by_col = jnp.where(col_id == cols_of[line, :], 1.0, 0.0).astype(BF16)
+        tall_id = lax.broadcasted_iota(jnp.int32, (counts.shape[0], length), 0)
+        lane_id = lax.broadcasted_iota(jnp.int32, (2 * LANES, length), 0)
+        by_tall, by_lane = [], []
+        for j in range(group):
+            line = pl.ds(i * group + j, 1)
+            by_tall.append(jnp.where(tall_id == tall_of[line, :], codes[line, :], 0.0).astype(BF16))
+            by_lane.append(jnp.where(lane_id == lane_of[line, :], 1.0, 0.0).astype(BF16))
         counts[...] += lax.dot_general(
-            by_row, by_col, (((1,), (1,)), ((), ())), preferred_element_type=F32
+            jnp.concatenate(by_tall, axis=1),
+            jnp.concatenate(by_lane, axis=1),
+            (((1,), (1,)), ((), ())),
+            preferred_element_type=F32,
         )
 
-    per_half = half // LANES
-    for tile in range(2 * per_half):
-        side, lane = tile // per_half, tile % per_half
-        count = counts[side * tall : (side + 1) * tall, lane * LANES : (lane + 1) * LANES]
+    for tile in range(counts.shape[0] // tall * 2):
+        lines, lanes = tile // 2 * tall, tile % 2 * LANES
+        count = counts[lines : lines + tall, lanes : lanes + LANES]
         factor[tile] = jnp.exp(count * math.log(YIELD_DROP))
 
 
@@ -109,12 +113,89 @@
             pltpu.VMEM(words.shape, jnp.int32),
             pltpu.VMEM(words.shape, jnp.int32),
             pltpu.VMEM(words.shape, F32),
-            pltpu.VMEM((2 * tall, wide // 2), F32),
+            pltpu.VMEM((tall * wide // (2 * LANES), 2 * LANES), F32),
         ],
         compiler_params=pltpu.CompilerParams(vmem_limit_bytes=VMEM_LIMIT),
-        cost_estimate=pl.CostEstimate(flops=10**9, bytes_accessed=10**6, transcendentals=0),
+        cost_estimate=pl.CostEstimate(
+            flops=2 * tall * wide * words.size, bytes_accessed=4 * words.size, transcendentals=tall * wide
+        ),
         name="yield_factor",
     )(place, words)
+
+
+def pack_kernel(
+    first_lame, shear_modulus, applied_load, owner, cell, code,
+    fields, first_cols, last_cols, words, lists, arrived,
+    *, cells,
+):
+    copies = [
+        pltpu.make_async_copy(source, target, arrived.at[at])
+        for at, (source, target) in enumerate(
+            (
+                (owner, lists.at[0]),
+                (cell, lists.at[1]),
+                (code, lists.at[2]),
+                (first_lame, fields.at[0]),
+                (shear_modulus, fields.at[1]),
+                (applied_load, fields.at[pl.ds(2, 2)]),
+            )
+        )
+    ]
+    for copy in copies:
+        copy.start()
+    for copy in copies[:3]:
+        copy.wait()
+    word = (lists[0] * cells + lists[1]) * 4 + lists[2]
+    for device in range(words.shape[0]):
+        words[device] = word
+    for copy in copies[3:]:
+        copy.wait()
+    first_cols[...] = fields[:, :, :HALO_COLS]
+    last_cols[...] = fields[:, :, fields.shape[2] - HALO_COLS :]
+
+
+def pack(first_lame, shear_modulus, applied_load, owner, cell, code, devices):
+    rows, cols = first_lame.shape
+    edge = jax.ShapeDtypeStruct((4, rows, HALO_COLS), F32)
+    length = cell.shape[0]
+    arrays = [first_lame, shear_modulus, applied_load] + [part.reshape(1, -1) for part in (owner, cell, code)]
+    hbm, vmem = pl.BlockSpec(memory_space=pltpu.HBM), pl.BlockSpec(memory_space=pltpu.VMEM)
+    return pl.pallas_call(
+        functools.partial(pack_kernel, cells=rows * cols),
+        out_shape=[
+            jax.ShapeDtypeStruct((4, rows, cols), F32),
+            edge,
+            edge,
+            jax.ShapeDtypeStruct((devices, 1, length), jnp.int32),
+        ],
+        in_specs=[hbm] * 6,
+        out_specs=[vmem] * 4,
+        scratch_shapes=[pltpu.VMEM((3, 1, length), jnp.int32), pltpu.SemaphoreType.DMA((6,))],
+        compiler_params=pltpu.CompilerParams(vmem_limit_bytes=8 * 1024 * 1024),
+        name="pack",
+    )(*[pltpu.with_memory_space_constraint(array, pltpu.HBM) for array in arrays])
+
+
+def rows_kernel(fields, left, right, last_rows, first_rows):
+    cols = fields.shape[2]
+    for out, start in ((last_rows, fields.shape[1] - HALO_ROWS), (first_rows, 0)):
+        span = slice(start, start + HALO_ROWS)
+        out[:, :, :cols] = fields[:, span, :]
+        out[:, :, cols : cols + HALO_COLS] = left[:, span, :]
+        out[:, :, cols + HALO_COLS :] = right[:, span, :]
+
+
+def pack_rows(fields, left, right):
+    edge = jax.ShapeDtypeStruct((4, HALO_ROWS, fields.shape[2] + 2 * HALO_COLS), F32)
+    vmem = pl.BlockSpec(memory_space=pltpu.VMEM)
+    return pl.pallas_call(
+        rows_kernel,
+        out_shape=[edge, edge],
+        in_specs=[vmem] * 3,
+        out_specs=[vmem] * 2,
+        compiler_params=pltpu.CompilerParams(vmem_limit_bytes=8 * 1024 * 1024),
+        name="pack_rows",
+    )(fields, left, right)
 
 
 class Level:
@@ -449,7 +530,7 @@
 
 
 def down_kernel(
-    place, first_lame, shear_modulus, applied_load, left, right, upper, lower, factor,
+    place, fields, left, right, upper, lower, factor,
     matrix0, inverse0, source0, x0, matrix1, inverse1, source1, x1, matrix2, inverse2, source2, x2, coarsest,
     tiles, stacked, spread, other0, other1, other2, spill0, spill1, spill2, matrix3,
     *, rows, cols, gx, gy,
@@ -468,12 +549,11 @@
         lane = lax.broadcasted_iota(jnp.int32, (LANES, GROUP * LANES), 1)
         spread[tile * LANES : (tile + 1) * LANES, :] = jnp.where(lane == target, 1.0, 0.0).astype(BF16)
 
-    own = (first_lame, shear_modulus, applied_load.at[0], applied_load.at[1])
     for field in range(4):
         for tile in range(wide // LANES):
             lanes = slice(tile * LANES, (tile + 1) * LANES)
             if tile < cols // LANES:
-                middle = own[field][:, lanes]
+                middle = fields[field, :, lanes]
             else:
                 middle = (left if tile == cols // LANES else right)[field]
             parts = [
@@ -633,25 +713,16 @@
     devices = gx * gy
     place = jnp.stack([lax.axis_index("gx"), lax.axis_index("gy")]).astype(jnp.int32)
 
-    word = (plastic_owner[:, 0] * (rows * cols) + plastic_cell) * 4 + plastic_code
-    fields = [first_lame, shear_modulus, applied_load[0], applied_load[1]]
-    first_cols = jnp.stack([field[:, :HALO_COLS] for field in fields])
-    last_cols = jnp.stack([field[:, -HALO_COLS:] for field in fields])
+    fields, first_cols, last_cols, words = pack(
+        first_lame, shear_modulus, applied_load, plastic_owner, plastic_cell, plastic_code, devices
+    )
     left = passed_along(last_cols, "gy", 1)
     right = passed_along(first_cols, "gy", -1)
-
-    words = lax.all_to_all(
-        jnp.broadcast_to(word[None], (devices, word.shape[0])), ("gx", "gy"), 0, 0, tiled=True
-    )
-    words, left, right = lax.optimization_barrier((words, left, right))
-
-    def whole_rows(span):
-        return jnp.concatenate(
-            [jnp.stack([field[span] for field in fields]), left[:, span], right[:, span]], axis=2
-        )
-
-    upper = passed_along(whole_rows(slice(rows - HALO_ROWS, rows)), "gx", 1)
-    lower = passed_along(whole_rows(slice(0, HALO_ROWS)), "gx", -1)
+    words = lax.all_to_all(words, ("gx", "gy"), 0, 0, tiled=True).reshape(devices, -1)
+
+    last_rows, first_rows = pack_rows(fields, left, right)
+    upper = passed_along(last_rows, "gx", 1)
+    lower = passed_along(first_rows, "gx", -1)
     factor = yield_factor(place, words, rows, cols, gy)
 
     tall, wide = rows + 2 * HALO_ROWS, cols + 2 * HALO_COLS
@@ -670,7 +741,7 @@
         functools.partial(down_kernel, rows=rows, cols=cols, gx=gx, gy=gy),
         out_shape=[jax.ShapeDtypeStruct(shape, F32) for shape in state]
         + [jax.ShapeDtypeStruct((held, rows // GROUP, LANES), F32)],
-        in_specs=[smem] + [vmem] * 8,
+        in_specs=[smem] + [vmem] * 6,
         out_specs=[vmem] * (len(state) + 1),
         scratch_shapes=[
             pltpu.VMEM((wide // LANES, tall, LANES), F32),
@@ -682,7 +753,7 @@
         + [pltpu.VMEM((held, side, LANES), F32)],
         compiler_params=pltpu.CompilerParams(vmem_limit_bytes=VMEM_LIMIT),
         name="descent",
-    )(place, first_lame, shear_modulus, applied_load, left, right, upper, lower, factor)
+    )(place, fields, left, right, upper, lower, factor)
 
     coarse_before = passed_along(coarse, "gx", 1)
     coarse_after = passed_along(coarse, "gx", -1)

time: 61 us -> 49 us (0.80); the launches traced: 60 us -> 48.7 us
  Pallas kernels: 25.9 us -> 20.6 us
  local copies, waits for them, and re-layouts: 2.56 us -> 0.01 us
  waiting for transfers between devices: 6.14 us -> 3.91 us
  other arithmetic: 1.61 us -> 0.08 us
    pallas_call x1, Pallas kernels: 11.5 us -> 4.38 us  [yield_factor(): pl.pallas_call(functools.partial(factor_kernel, rows=rows, cols=cols, gy=...]
    ppermute x6, waiting for transfers between devices: 5.56 us -> 2.42 us  [passed_along(): return lax.ppermute(array, axis, pairs)]
    pallas_call x0 -> x2, Pallas kernels: none -> 1.86 us  [the longest x1 1.8 us: pack(): pl.pallas_call(functools.partial(pack_kernel, cells=rows * cols), out_sha...]
    squeeze x1 -> x0, local copies, waits for them, and re-layouts: 0.99 us -> none  [body(): fields = [first_lame, shear_modulus, applied_load[0], applied_load[1]]]
    all_to_all x1, waiting for transfers between devices: 0.58 us -> 1.5 us  [body(): lax.all_to_all(words, ('gx', 'gy'), 0, 0, tiled=True).reshape(devices, -1)]
    another operation x3 -> x0, local copies, waits for them, and re-layouts: 0.85 us -> none  [the longest x2 0.83 us: body(): first_cols = jnp.stack([field[:, :HALO_COLS] for field in fields])]
    mul x1 -> x0, other arithmetic: 0.74 us -> none  [body(): plastic_owner[:, 0] * (rows * cols) + plastic_cell]
    add x1 -> x0, other arithmetic: 0.7 us -> none  [body(): (plastic_owner[:, 0] * (rows * cols) + plastic_cell) * 4 + plastic_code]
  transfers between devices with their start and end apart: 7 -> 7, of which waited for: 4 -> 3; matrix products, arithmetic and copies ran while one was open for 3% -> 0% of each run, Pallas kernels for 19% -> 9%
where the time goes in v3:
time: 49 us; the launch traced here: 48.7 us
  starting transfers between devices  24 us (49%)
  Pallas kernels  20.6 us (42%)
  waiting for transfers between devices  3.91 us (8%)
    ppermute x6, starting transfers between devices, passed_along(): return lax.ppermute(array, axis, pairs)  16.3 us
    pallas_call x1, Pallas kernels, body(): pl.pallas_call(functools.partial(down_kernel, rows=rows, cols=cols, gx=gx...  7.95 us
    all_to_all x1, starting transfers between devices, body(): lax.all_to_all(words, ('gx', 'gy'), 0, 0, tiled=True).reshape(devices, -1)  7.7 us
    pallas_call x1, Pallas kernels, body(): pl.pallas_call(functools.partial(up_kernel, rows=rows, cols=cols, gx=gx,...  6.44 us
    pallas_call x1, Pallas kernels, yield_factor(): pl.pallas_call(functools.partial(factor_kernel, rows=rows, cols=cols, gy=...  4.38 us
    ppermute x6, waiting for transfers between devices, passed_along(): return lax.ppermute(array, axis, pairs)  2.42 us
    pallas_call x1, Pallas kernels, pack(): pl.pallas_call(functools.partial(pack_kernel, cells=rows * cols), out_sha...  1.8 us
    all_to_all x1, waiting for transfers between devices, body(): lax.all_to_all(words, ('gx', 'gy'), 0, 0, tiled=True).reshape(devices, -1)  1.5 us
  transfers between devices with their start and end apart: 7, of which 3 were waited for; matrix products, arithmetic and copies ran while one was open for 0% of the time, Pallas kernels for 9%

profile of v3, /device:TPU:1, one launch (start us, length us, event | category | flops | bytes accessed | tf_op | source)
XLA Modules:
  0.0 48.7 jit_solution(10819879538502490035)
XLA Ops:
  0.0 1.8 %pack.1 = (f32[4,64,512]{2,1,0:T(8,128)S(1)}, f32[4,64,128]{2,1,0:T(8,128)S(1)}, f32[4,64,128]{2,1,0:T(8,128)S(1)}, s32[32,1,512]{2,1,0:T(1,128)}) custom-call(f32[64,512]{1,0:T(8,128)} %first_lame.1, f32[64,512]{1,0:T(8,128)} %shear_modulus.1, f32[2,64,512]{2,1,0:T(8,128)} %applied_load.1, s32[1,512]{1,0:T(1,128)} %bitcast.9, s32[1,512]{1,0:T(1,128)} %bitcast.10, ...), custom_call_target="tpu_custom_call" | custom-call | tf_op jit(solution)/shard_map/pack/pallas_call | solution.py:163
  1.8 4.0 %collective-permute-start = (f32[4,64,128]{2,1,0:T(8,128)S(1)}, f32[4,64,128]{2,1,0:T(8,128)S(1)}, u32[]{:S(2)}, u32[]{:S(2)}) collective-permute-start(f32[4,64,128]{2,1,0:T(8,128)S(1)} %get-tuple-element.25), channel_id=1, source_target_pairs={{0,1},{1,2},{2,3},{3,4},{4,5},{5,6},{6,7},{8,9},{9,10},{10,11},{11... | collective-permute-start | bytes 393224 | tf_op jit(solution)/shard_map/ppermute | solution.py:34
  5.8 1.3 %collective-permute-start.1 = (f32[4,64,128]{2,1,0:T(8,128)S(1)}, f32[4,64,128]{2,1,0:T(8,128)S(1)}, u32[]{:S(2)}, u32[]{:S(2)}) collective-permute-start(f32[4,64,128]{2,1,0:T(8,128)S(1)} %get-tuple-element.26), channel_id=1, source_target_pairs={{1,0},{2,1},{3,2},{4,3},{5,4},{6,5},{7,6},{9,8},{10,9},{11,10},{12... | collective-permute-start | bytes 393224 | tf_op jit(solution)/shard_map/ppermute | solution.py:34
  7.1 7.7 %all-to-all-start = ((s32[32,1,512]{2,1,0:T(1,128)}), s32[32,1,512]{2,1,0:T(1,128)S(1)}, u32[]{:S(2)}, u32[]{:S(2)}) async-start(s32[32,1,512]{2,1,0:T(1,128)} %get-tuple-element.29), calls=%async_computation | async-start | bytes 131072 | tf_op jit(solution)/shard_map/all_to_all | solution.py:721
  14.8 0.0 collective-permute-done.left
  14.8 0.0 collective-permute-done.1.right
  14.8 0.1 pack_rows.1
  14.9 3.5 %collective-permute-start.2 = (f32[4,32,768]{2,1,0:T(8,128)S(1)}, f32[4,32,768]{2,1,0:T(8,128)S(1)}, u32[]{:S(2)}, u32[]{:S(2)}) collective-permute-start(f32[4,32,768]{2,1,0:T(8,128)S(1)} %get-tuple-element.27), channel_id=1, source_target_pairs={{0,8},{8,16},{16,24},{1,9},{9,17},{17,25},{2,10},{10,18},{18,26},{... | collective-permute-start | bytes 1179656 | tf_op jit(solution)/shard_map/ppermute | solution.py:34
  18.4 1.9 %collective-permute-start.3 = (f32[4,32,768]{2,1,0:T(8,128)S(1)}, f32[4,32,768]{2,1,0:T(8,128)S(1)}, u32[]{:S(2)}, u32[]{:S(2)}) collective-permute-start(f32[4,32,768]{2,1,0:T(8,128)S(1)} %get-tuple-element.28), channel_id=1, source_target_pairs={{8,0},{16,8},{24,16},{9,1},{17,9},{25,17},{10,2},{18,10},{26,18},{... | collective-permute-start | bytes 1179656 | tf_op jit(solution)/shard_map/ppermute | solution.py:34
  20.3 0.1 pad_add_fusion.place
  20.4 1.5 %all-to-all-done = s32[32,1,512]{2,1,0:T(1,128)S(1)} async-done(((s32[32,1,512]{2,1,0:T(1,128)}), s32[32,1,512]{2,1,0:T(1,128)S(1)}, u32[]{:S(2)}, u32[]{:S(2)}) %all-to-all-start) | async-done | bytes 65568 | tf_op jit(solution)/shard_map/all_to_all | solution.py:721
  21.9 4.4 %yield_factor.1.factor = f32[6,128,128]{2,1,0:T(8,128)S(1)} custom-call(s32[2]{0:T(128)S(1)} %pad_add_fusion.place, s32[32,512]{1,0:T(8,128)S(1)} %bitcast.8), custom_call_target="tpu_custom_call" | custom-call | flops 3221225472 | bytes 65536 | tf_op jit(solution)/shard_map/yield_factor/pallas_call | solution.py:104
  26.3 0.0 collective-permute-done.2.upper
  26.3 1.2 %collective-permute-done.3.lower = f32[4,32,768]{2,1,0:T(8,128)S(1)} collective-permute-done((f32[4,32,768]{2,1,0:T(8,128)S(1)}, f32[4,32,768]{2,1,0:T(8,128)S(1)}, u32[]{:S(2)}, u32[]{:S(2)}) %collective-permute-start.3) | collective-permute-done | bytes 393248 | tf_op jit(solution)/shard_map/ppermute | solution.py:34
  27.5 7.9 %descent.1 = (f32[3,8,8,16,128]{4,3,2,1,0:T(8,128)S(1)}, f32[1,8,8,16,128]{4,3,2,1,0:T(8,128)S(1)}, f32[2,8,8,16,128]{4,3,2,1,0:T(8,128)S(1)}, f32[2,8,9,16,128]...) custom-call(s32[2]{0:T(128)S(1)} %pad_add_fusion.place, ...), custom_call_target="tpu_custom_call" | custom-call | tf_op jit(solution)/shard_map/descent/pallas_call | solution.py:740
  35.5 1.9 %collective-permute-start.5 = (f32[14,8,128]{2,1,0:T(8,128)S(1)}, f32[14,8,128]{2,1,0:T(8,128)S(1)}, u32[]{:S(2)}, u32[]{:S(2)}) collective-permute-start(f32[14,8,128]{2,1,0:T(8,128)S(1)} %get-tuple-element.30.coarse), channel_id=1, source_target_pairs={{8,0},{16,8},{24,16},{9,1},{17,9},{25,17},{10,2},{18,10},{26,18},{... | collective-permute-start | bytes 172040 | tf_op jit(solution)/shard_map/ppermute | solution.py:34
  37.4 3.6 %collective-permute-start.4 = (f32[14,8,128]{2,1,0:T(8,128)S(1)}, f32[14,8,128]{2,1,0:T(8,128)S(1)}, u32[]{:S(2)}, u32[]{:S(2)}) collective-permute-start(f32[14,8,128]{2,1,0:T(8,128)S(1)} %get-tuple-element.30.coarse), channel_id=1, source_target_pairs={{0,8},{8,16},{16,24},{1,9},{9,17},{17,25},{2,10},{10,18},{18,26},{... | collective-permute-start | bytes 172040 | tf_op jit(solution)/shard_map/ppermute | solution.py:34
  41.0 0.0 collective-permute-done.5.coarse_after
  41.1 1.2 %collective-permute-done.4.coarse_before = f32[14,8,128]{2,1,0:T(8,128)S(1)} collective-permute-done((f32[14,8,128]{2,1,0:T(8,128)S(1)}, f32[14,8,128]{2,1,0:T(8,128)S(1)}, u32[]{:S(2)}, u32[]{:S(2)}) %collective-permute-start.4) | collective-permute-done | bytes 57376 | tf_op jit(solution)/shard_map/ppermute | solution.py:34
  42.3 6.4 %ascent.1 = f32[2,64,512]{2,1,0:T(8,128)} custom-call(s32[2]{0:T(128)S(1)} %pad_add_fusion.place, f32[14,8,128]{2,1,0:T(8,128)S(1)} %get-tuple-element.30.coarse, f32[14,8,128]{2,1,0:T(8,128)S(1)} %collective-permute-done.4.coarse_before, f32[14,8,128]{2,1,0:T(8,128)S(1)} %collective-permute-done.5.coarse_after, ...), custom_call_target="tpu_custom_call" | custom-call | tf_op jit(solution)/shard_map/ascent/pallas_call | solution.py:761
  (1 shorter events, 0.0 us)
Async XLA Ops:
  1.8 13.0 %collective-permute-start = (f32[4,64,128]{2,1,0:T(8,128)S(1)}, f32[4,64,128]{2,1,0:T(8,128)S(1)}, u32[]{:S(2)}, u32[]{:S(2)}) collective-permute-start(f32[4,64,128]{2,1,0:T(8,128)S(1)} %get-tuple-element.25), channel_id=1, source_target_pairs={{0,1},{1,2},{2,3},{3,4},{4,5},{5,6},{6,7},{8,9},{9,10},{10,11},{11... | collective-permute-start | bytes 393224 | tf_op jit(solution)/shard_map/ppermute | solution.py:34
  5.8 9.0 %collective-permute-start.1 = (f32[4,64,128]{2,1,0:T(8,128)S(1)}, f32[4,64,128]{2,1,0:T(8,128)S(1)}, u32[]{:S(2)}, u32[]{:S(2)}) collective-permute-start(f32[4,64,128]{2,1,0:T(8,128)S(1)} %get-tuple-element.26), channel_id=1, source_target_pairs={{1,0},{2,1},{3,2},{4,3},{5,4},{6,5},{7,6},{9,8},{10,9},{11,10},{12... | collective-permute-start | bytes 393224 | tf_op jit(solution)/shard_map/ppermute | solution.py:34
  7.1 14.9 %all-to-all-start = ((s32[32,1,512]{2,1,0:T(1,128)}), s32[32,1,512]{2,1,0:T(1,128)S(1)}, u32[]{:S(2)}, u32[]{:S(2)}) async-start(s32[32,1,512]{2,1,0:T(1,128)} %get-tuple-element.29), calls=%async_computation | async-start | bytes 131072 | tf_op jit(solution)/shard_map/all_to_all | solution.py:721
  14.9 11.5 %collective-permute-start.2 = (f32[4,32,768]{2,1,0:T(8,128)S(1)}, f32[4,32,768]{2,1,0:T(8,128)S(1)}, u32[]{:S(2)}, u32[]{:S(2)}) collective-permute-start(f32[4,32,768]{2,1,0:T(8,128)S(1)} %get-tuple-element.27), channel_id=1, source_target_pairs={{0,8},{8,16},{16,24},{1,9},{9,17},{17,25},{2,10},{10,18},{18,26},{... | collective-permute-start | bytes 1179656 | tf_op jit(solution)/shard_map/ppermute | solution.py:34
  18.4 9.1 %collective-permute-start.3 = (f32[4,32,768]{2,1,0:T(8,128)S(1)}, f32[4,32,768]{2,1,0:T(8,128)S(1)}, u32[]{:S(2)}, u32[]{:S(2)}) collective-permute-start(f32[4,32,768]{2,1,0:T(8,128)S(1)} %get-tuple-element.28), channel_id=1, source_target_pairs={{8,0},{16,8},{24,16},{9,1},{17,9},{25,17},{10,2},{18,10},{26,18},{... | collective-permute-start | bytes 1179656 | tf_op jit(solution)/shard_map/ppermute | solution.py:34
  35.5 5.6 %collective-permute-start.5 = (f32[14,8,128]{2,1,0:T(8,128)S(1)}, f32[14,8,128]{2,1,0:T(8,128)S(1)}, u32[]{:S(2)}, u32[]{:S(2)}) collective-permute-start(f32[14,8,128]{2,1,0:T(8,128)S(1)} %get-tuple-element.30.coarse), channel_id=1, source_target_pairs={{8,0},{16,8},{24,16},{9,1},{17,9},{25,17},{10,2},{18,10},{26,18},{... | collective-permute-start | bytes 172040 | tf_op jit(solution)/shard_map/ppermute | solution.py:34
  37.4 4.9 %collective-permute-start.4 = (f32[14,8,128]{2,1,0:T(8,128)S(1)}, f32[14,8,128]{2,1,0:T(8,128)S(1)}, u32[]{:S(2)}, u32[]{:S(2)}) collective-permute-start(f32[14,8,128]{2,1,0:T(8,128)S(1)} %get-tuple-element.30.coarse), channel_id=1, source_target_pairs={{0,8},{8,16},{16,24},{1,9},{9,17},{17,25},{2,10},{10,18},{18,26},{... | collective-permute-start | bytes 172040 | tf_op jit(solution)/shard_map/ppermute | solution.py:34

commit v4 on v3

--- a/solution.py
+++ b/solution.py
@@ -17,6 +17,8 @@
 HALO_ROWS = 32
 HALO_COLS = 128
 LANES = 128
+WIDE = 2 * LANES
+SPAN = WIDE // GROUP
 LISTS_AT_ONCE = 16
 VMEM_LIMIT = 30 * 1024 * 1024
 F32 = jnp.float32
@@ -61,26 +63,30 @@
 
 
 def factor_kernel(place, words, factor, tall_of, lane_of, codes, counts, *, rows, cols, gy):
-    word = words[...]
+    for at in range(words.shape[0]):
+        tall_of[at : at + 1, :] = words[at]
+    word = tall_of[...]
     cell_bits = log2(rows * cols)
     owner = word >> (cell_bits + 2)
     cell = (word >> 2) & (rows * cols - 1)
-    row = (owner >> log2(gy)) * rows + (cell >> log2(cols)) - place[0] * rows + HALO_ROWS
+    row = (owner >> log2(gy)) * rows + (cell >> log2(cols)) - place[0] * rows
     col = (owner & (gy - 1)) * cols + (cell & (cols - 1)) - place[1] * cols
     tall = rows + 2 * HALO_ROWS
-    inside = (row >= 0) & (row < tall) & (col >= -HALO_COLS) & (col < cols + HALO_COLS)
+    side = tall // GROUP
+    inside = (row >= -HALO_ROWS) & (row < rows + HALO_ROWS) & (col >= -HALO_COLS) & (col < cols + HALO_COLS)
     at = jnp.where(col < 0, col + cols + HALO_COLS, jnp.where(col >= cols, col + HALO_COLS, col))
-    tall_of[...] = jnp.where(inside, row + tall * (at >> log2(2 * LANES)), -1)
-    lane_of[...] = at & (2 * LANES - 1)
+    line = (row & (GROUP - 1)) * side + ((row >> LEVELS) & (side - 1))
+    tall_of[...] = jnp.where(inside, line + tall * (at >> log2(WIDE)), -1)
+    lane_of[...] = (at & (GROUP - 1)) * SPAN + ((at & (WIDE - 1)) >> LEVELS)
     codes[...] = (word & 3).astype(F32)
     counts[...] = jnp.zeros_like(counts)
-    length = words.shape[1]
+    length = words.shape[2]
     group = min(LISTS_AT_ONCE, words.shape[0])
 
     @pl.loop(0, words.shape[0] // group)
     def _(i):
         tall_id = lax.broadcasted_iota(jnp.int32, (counts.shape[0], length), 0)
-        lane_id = lax.broadcasted_iota(jnp.int32, (2 * LANES, length), 0)
+        lane_id = lax.broadcasted_iota(jnp.int32, (WIDE, length), 0)
         by_tall, by_lane = [], []
         for j in range(group):
             line = pl.ds(i * group + j, 1)
@@ -93,27 +99,31 @@
             preferred_element_type=F32,
         )
 
-    for tile in range(counts.shape[0] // tall * 2):
-        lines, lanes = tile // 2 * tall, tile % 2 * LANES
-        count = counts[lines : lines + tall, lanes : lanes + LANES]
-        factor[tile] = jnp.exp(count * math.log(YIELD_DROP))
+    for m in range(GROUP):
+        for k in range(GROUP):
+            half, slot = k * SPAN // LANES, k * SPAN % LANES
+            lanes = slice(half * LANES, (half + 1) * LANES)
+            lines = range(m * side, counts.shape[0], tall)
+            count = gather_lanes([counts[line : line + side, lanes] for line in lines], slot)
+            factor[m, k] = jnp.exp(count * math.log(YIELD_DROP))
 
 
 def yield_factor(place, words, rows, cols, gy):
     tall, wide = rows + 2 * HALO_ROWS, cols + 2 * HALO_COLS
+    lists = (words.shape[0], words.shape[2])
     return pl.pallas_call(
         functools.partial(factor_kernel, rows=rows, cols=cols, gy=gy),
-        out_shape=jax.ShapeDtypeStruct((wide // LANES, tall, LANES), F32),
+        out_shape=jax.ShapeDtypeStruct((GROUP, GROUP, tall // GROUP, LANES), F32),
         in_specs=[
             pl.BlockSpec(memory_space=pltpu.SMEM),
             pl.BlockSpec(memory_space=pltpu.VMEM),
         ],
         out_specs=pl.BlockSpec(memory_space=pltpu.VMEM),
         scratch_shapes=[
-            pltpu.VMEM(words.shape, jnp.int32),
-            pltpu.VMEM(words.shape, jnp.int32),
-            pltpu.VMEM(words.shape, F32),
-            pltpu.VMEM((tall * wide // (2 * LANES), 2 * LANES), F32),
+            pltpu.VMEM(lists, jnp.int32),
+            pltpu.VMEM(lists, jnp.int32),
+            pltpu.VMEM(lists, F32),
+            pltpu.VMEM((tall * wide // WIDE, WIDE), F32),
         ],
         compiler_params=pltpu.CompilerParams(vmem_limit_bytes=VMEM_LIMIT),
         cost_estimate=pl.CostEstimate(
@@ -125,7 +135,7 @@
 
 def pack_kernel(
     first_lame, shear_modulus, applied_load, owner, cell, code,
-    fields, first_cols, last_cols, words, lists, arrived,
+    fields, first_cols, last_cols, words, lists, copied, arrived,
     *, cells,
 ):
     copies = [
@@ -147,11 +157,14 @@
         copy.wait()
     word = (lists[0] * cells + lists[1]) * 4 + lists[2]
     for device in range(words.shape[0]):
-        words[device] = word
+        copied[device] = word
+    sent = pltpu.make_async_copy(copied, words, arrived.at[6])
+    sent.start()
     for copy in copies[3:]:
         copy.wait()
     first_cols[...] = fields[:, :, :HALO_COLS]
     last_cols[...] = fields[:, :, fields.shape[2] - HALO_COLS :]
+    sent.wait()
 
 
 def pack(first_lame, shear_modulus, applied_load, owner, cell, code, devices):
@@ -169,8 +182,12 @@
             jax.ShapeDtypeStruct((devices, 1, length), jnp.int32),
         ],
         in_specs=[hbm] * 6,
-        out_specs=[vmem] * 4,
-        scratch_shapes=[pltpu.VMEM((3, 1, length), jnp.int32), pltpu.SemaphoreType.DMA((6,))],
+        out_specs=[vmem] * 3 + [hbm],
+        scratch_shapes=[
+            pltpu.VMEM((3, 1, length), jnp.int32),
+            pltpu.VMEM((devices, 1, length), jnp.int32),
+            pltpu.SemaphoreType.DMA((7,)),
+        ],
         compiler_params=pltpu.CompilerParams(vmem_limit_bytes=8 * 1024 * 1024),
         name="pack",
     )(*[pltpu.with_memory_space_constraint(array, pltpu.HBM) for array in arrays])
@@ -203,9 +220,9 @@
         self.matrix, self.names_at, self.inverse, self.spill = matrix, names_at, inverse, spill
         self.count = matrix.shape[1]
 
-    def entry(self, name, m, k):
+    def entry(self, name, m, k, high):
         at = self.names_at.get(name)
-        return None if at is None else self.matrix[at, m, k]
+        return None if at is None else self.matrix[at, m, k, :high, :]
 
     def stress(self, m, k, modes):
         names = "123rc"
@@ -216,7 +233,7 @@
             for j in range(5):
                 name = names[min(i, j)] + names[max(i, j)]
                 if name not in known:
-                    known[name] = self.entry(name, m, k)
+                    known[name] = self.entry(name, m, k, modes[0].shape[0])
                 if known[name] is not None:
                     terms.append(known[name] * modes[j])
             result.append(plus(*terms))
@@ -227,7 +244,7 @@
             names = ("11", "33", "rr", "13", "1r", "3r")
         else:
             names = ("22", "33", "cc", "23", "3c", "2c")
-        first, second, third, cross, by_col, by_row = [self.entry(name, m, k) for name in names]
+        first, second, third, cross, by_col, by_row = [self.entry(name, m, k, self.matrix.shape[3]) for name in names]
         base = first + second + third
         by_row, by_col, cross = 2.0 * by_row, 2.0 * by_col, times(2.0, cross)
         if cross is None:
@@ -264,7 +281,7 @@
 
 class FineLevel(Level):
     def stress(self, m, k, modes):
-        lame, shear, mixed = self.matrix[0, m, k], self.matrix[1, m, k], self.matrix[2, m, k]
+        lame, shear, mixed = [self.matrix[at, m, k, : modes[0].shape[0], :] for at in range(3)]
         first, second, third, bend_row, bend_col = modes
         twice, mean = shear + shear, lame * (first + second)
         return [
@@ -302,8 +319,8 @@
                 self.inverse[0, m, k] = value
 
 
-def inverse_of(level, component, m, k):
-    return level.inverse[min(component, len(level.components()) - 1), m, k]
+def inverse_of(level, component, m, k, high):
+    return level.inverse[min(component, len(level.components()) - 1), m, k, :high, :]
 
 
 def close_columns(level, x):
@@ -319,7 +336,7 @@
     def column(k):
         for component in (0, 1):
             for m in range(count):
-                x[component, m, k] = source[component, m, k] * inverse_of(level, component, m, k)
+                x[component, m, k] = source[component, m, k] * inverse_of(level, component, m, k, x.shape[3])
 
     over_columns(count, column)
     close_columns(level, x)
@@ -333,53 +350,65 @@
             column(k)
 
 
-def apply(level, x, source, out, residual):
+def cut(value, height):
+    return value if value.shape[0] == height else value[:height]
+
+
+def apply(level, x, source, out, residual, tall_cells=None, tall_nodes=None):
     count, spill = level.count, level.spill
+    side = x.shape[3]
+    cells = [side if tall_cells is None or m in tall_cells else side // 2 for m in range(count)]
+    nodes = [side if tall_nodes is None or m in tall_nodes else side // 2 for m in range(count)]
+    held = [max(cells[m], cells[m - 1]) if m else side for m in range(count)]
     spill[...] = jnp.zeros_like(spill)
 
     def column(k):
         sums, steps = [], []
         for m in range(count):
-            here = [x[component, m, k] for component in (0, 1)]
-            after = [x[component, m, k + 1] for component in (0, 1)]
+            here = [x[component, m, k, : held[m], :] for component in (0, 1)]
+            after = [x[component, m, k + 1, : held[m], :] for component in (0, 1)]
             sums.append([here[c] + after[c] for c in (0, 1)])
             steps.append([after[c] - here[c] for c in (0, 1)])
         sums.append([from_after(value, 0) for value in sums[0]])
         steps.append([from_after(value, 0) for value in steps[0]])
         own, passed = [], []
         for m in range(count):
+            sum0, sum1 = [[cut(value, cells[m]) for value in sums[row]] for row in (m, m + 1)]
+            step0, step1 = [[cut(value, cells[m]) for value in steps[row]] for row in (m, m + 1)]
             modes = (
-                sums[m + 1][0] - sums[m][0],
-                steps[m][1] + steps[m + 1][1],
-                (steps[m][0] + steps[m + 1][0]) + (sums[m + 1][1] - sums[m][1]),
-                steps[m + 1][0] - steps[m][0],
-                steps[m + 1][1] - steps[m][1],
+                sum1[0] - sum0[0],
+                step0[1] + step1[1],
+                (step0[0] + step1[0]) + (sum1[1] - sum0[1]),
+                step1[0] - step0[0],
+                step1[1] - step0[1],
             )
             first, second, third, bend_row, bend_col = level.stress(m, k, modes)
             own.append((first, third - bend_row, third, second - bend_col))
             passed.append((first, third + bend_row, third, second + bend_col))
         for m in range(count):
+            high = nodes[m]
             above = passed[m - 1] if m else [from_before(value, 0) for value in passed[count - 1]]
             for component in (0, 1):
                 at = 2 * component
-                even = above[at] - own[m][at]
-                odd = above[at + 1] + own[m][at + 1]
-                left = spill[component, m]
-                spill[component, m] = even + odd
-                rest = source[component, m, k] - ((even - odd) + left)
+                even = cut(above[at], high) - cut(own[m][at], high)
+                odd = cut(above[at + 1], high) + cut(own[m][at + 1], high)
+                left = spill[component, m, :high, :]
+                spill[component, m, :high, :] = even + odd
+                rest = source[component, m, k, :high, :] - ((even - odd) + left)
                 if not residual:
-                    rest = x[component, m, k] + inverse_of(level, component, m, k) * rest
-                out[component, m, k] = rest
+                    rest = x[component, m, k, :high, :] + inverse_of(level, component, m, k, high) * rest
+                out[component, m, k, :high, :] = rest
 
     over_columns(count, column)
     for component in (0, 1):
         for m in range(count):
-            left = from_before(spill[component, m], 1)
+            high = nodes[m]
+            left = from_before(spill[component, m, :high, :], 1)
             if not residual:
-                left = left * inverse_of(level, component, m, 0)
-            out[component, m, 0] = out[component, m, 0] - left
-    if not residual:
-        close_columns(level, out)
+                left = left * inverse_of(level, component, m, 0, high)
+            out[component, m, 0, :high, :] = out[component, m, 0, :high, :] - left
+            if not residual:
+                out[component, m, count, :high, :] = from_after(out[component, m, 0, :high, :], 1)
 
 
 def restrict(residual, target, count):
@@ -512,9 +541,13 @@
                 write(FULL_AT[name], m, k, values[name])
 
 
-def edge_masks(place, shape, rows, cols, first_row, grid_rows, grid_cols):
-    row = lax.broadcasted_iota(jnp.int32, shape, 0) * GROUP + (place[0] * rows + first_row)
-    col = lax.broadcasted_iota(jnp.int32, shape, 1) * GROUP + (place[1] * cols - HALO_COLS)
+def edge_masks(place, shape, before, rows, cols, grid_rows, grid_cols):
+    def wrapped(axis, ahead):
+        at = lax.broadcasted_iota(jnp.int32, shape, axis)
+        return jnp.where(at < shape[axis] - ahead, at, at - shape[axis]) * GROUP
+
+    row = wrapped(0, before) + place[0] * rows
+    col = wrapped(1, HALO_COLS // GROUP) + place[1] * cols
     return (
         jnp.where(row < grid_rows, 1.0, 0.0).astype(F32),
         jnp.where(col < grid_cols, 1.0, 0.0).astype(F32),
@@ -529,58 +562,118 @@
     return high, middle, low
 
 
+def turned(value, by):
+    return pltpu.roll(value, by % LANES, 1) if by % LANES else value
+
+
+def gather_lanes(pieces, slot):
+    lane = lax.broadcasted_iota(jnp.int32, pieces[0].shape, 1)
+    halo = HALO_COLS // GROUP
+    own = (len(pieces) - 1) * SPAN
+    plane = jnp.where(lane >= LANES - halo, turned(pieces[-1], LANES - halo - slot), 0.0)
+    plane = jnp.where(lane < own + halo, turned(pieces[-1], own - halo - slot), plane)
+    for at in reversed(range(len(pieces) - 1)):
+        plane = jnp.where(lane < (at + 1) * SPAN, turned(pieces[at], at * SPAN - slot), plane)
+    return plane
+
+
+def make_spread(spread):
+    at = lax.broadcasted_iota(jnp.int32, (WIDE, WIDE), 0)
+    lane = lax.broadcasted_iota(jnp.int32, (WIDE, WIDE), 1)
+    spread[...] = jnp.where(lane == (at & (GROUP - 1)) * SPAN + (at >> LEVELS), 1.0, 0.0).astype(BF16)
+
+
+def spread_fields(load, write, tiles, stacked, spread):
+    fields, count, rows = tiles.shape[:3]
+    block = rows // GROUP
+    make_spread(spread)
+    for field in range(fields):
+        for tile in range(count):
+            load(field, tile)
+        for pair in range(GROUP // 2):
+            for tile in range(count):
+                lines = [tiles[field, tile, pl.ds(2 * pair + h, block, stride=GROUP), :] for h in (0, 1)]
+                for part, split in enumerate(three_parts(jnp.concatenate(lines, axis=0))):
+                    line = (field * 3 + part) * rows + pair * 2 * block
+                    stacked[line : line + 2 * block, tile * LANES : (tile + 1) * LANES] = split
+    for field in range(fields):
+        pieces = []
+        for piece in range(count * LANES // WIDE):
+            left = stacked[field * 3 * rows : (field + 1) * 3 * rows, piece * WIDE : (piece + 1) * WIDE]
+            product = jnp.dot(left, spread[...], preferred_element_type=F32)
+            pieces.append(product[:rows] + product[rows : 2 * rows] + product[2 * rows :])
+        for m in range(GROUP):
+            for k in range(GROUP):
+                half, slot = k * SPAN // LANES, k * SPAN % LANES
+                lanes = slice(half * LANES, (half + 1) * LANES)
+                lines = slice(m * block, (m + 1) * block)
+                write(field, m, k, gather_lanes([piece[lines, lanes] for piece in pieces], slot))
+
+
+def own_kernel(fields, left, right, planes, tiles, stacked, spread):
+    own_tiles = fields.shape[2] // LANES
+
+    def load(field, tile):
+        if tile < own_tiles:
+            tiles[field, tile] = fields[field, :, tile * LANES : (tile + 1) * LANES]
+        else:
+            tiles[field, tile] = (left if tile == own_tiles else right)[field]
+
+    def write(field, m, k, plane):
+        planes[field, m, k] = plane
+
+    spread_fields(load, write, tiles, stacked, spread)
+
+
+def spread_scratch(rows, wide):
+    return [
+        pltpu.VMEM((4, wide // LANES, rows, LANES), F32),
+        pltpu.VMEM((12 * rows, wide), BF16),
+        pltpu.VMEM((WIDE, WIDE), BF16),
+    ]
+
+
+def spread_own(fields, left, right):
+    rows, wide = fields.shape[1], fields.shape[2] + 2 * HALO_COLS
+    vmem = pl.BlockSpec(memory_space=pltpu.VMEM)
+    return pl.pallas_call(
+        own_kernel,
+        out_shape=jax.ShapeDtypeStruct((4, GROUP, GROUP, rows // GROUP, LANES), F32),
+        in_specs=[vmem] * 3,
+        out_specs=vmem,
+        scratch_shapes=spread_scratch(rows, wide),
+        compiler_params=pltpu.CompilerParams(vmem_limit_bytes=12 * 1024 * 1024),
+        cost_estimate=pl.CostEstimate(flops=24 * rows * wide * WIDE, bytes_accessed=0, transcendentals=0),
+        name="spread_own",
+    )(fields, left, right)
+
+
 def down_kernel(
-    place, fields, left, right, upper, lower, factor,
+    place, own, upper, lower, factor,
     matrix0, inverse0, source0, x0, matrix1, inverse1, source1, x1, matrix2, inverse2, source2, x2, coarsest,
     tiles, stacked, spread, other0, other1, other2, spill0, spill1, spill2, matrix3,
     *, rows, cols, gx, gy,
 ):
-    tall, wide = rows + 2 * HALO_ROWS, cols + 2 * HALO_COLS
-    side = tall // GROUP
-    row_ok, col_ok = edge_masks(place, (side, LANES), rows, cols, -HALO_ROWS, gx * rows, gy * cols)
-
-    for tile in range(wide // LANES):
-        at = lax.broadcasted_iota(jnp.int32, (LANES, GROUP * LANES), 0) + tile * LANES
-        if tile < cols // LANES:
-            at = at + HALO_COLS
-        elif tile == cols // LANES:
-            at = at - cols
-        target = (at & (GROUP - 1)) * LANES + (at >> LEVELS)
-        lane = lax.broadcasted_iota(jnp.int32, (LANES, GROUP * LANES), 1)
-        spread[tile * LANES : (tile + 1) * LANES, :] = jnp.where(lane == target, 1.0, 0.0).astype(BF16)
-
-    for field in range(4):
-        for tile in range(wide // LANES):
-            lanes = slice(tile * LANES, (tile + 1) * LANES)
-            if tile < cols // LANES:
-                middle = fields[field, :, lanes]
-            else:
-                middle = (left if tile == cols // LANES else right)[field]
-            parts = [
-                (slice(0, HALO_ROWS), upper[field, :, lanes]),
-                (slice(HALO_ROWS, HALO_ROWS + rows), middle),
-                (slice(HALO_ROWS + rows, tall), lower[field, :, lanes]),
-            ]
-            for span, value in parts:
-                if field < 2:
-                    value = value * (0.25 * factor[tile, span, :])
-                tiles[tile, span, :] = value
-        for m in range(GROUP):
-            for tile in range(wide // LANES):
-                lanes = slice(tile * LANES, (tile + 1) * LANES)
-                for part, value in enumerate(three_parts(tiles[tile, pl.ds(m, side, stride=GROUP), :])):
-                    stacked[part * tall + m * side : part * tall + (m + 1) * side, lanes] = value
-        for pair in range(GROUP // 2):
-            lanes = slice(pair * 2 * LANES, (pair + 1) * 2 * LANES)
-            product = jnp.dot(stacked[...], spread[:, lanes], preferred_element_type=F32)
-            product = product[:tall] + product[tall : 2 * tall] + product[2 * tall :]
-            for m in range(GROUP):
-                for half in (0, 1):
-                    plane = product[m * side : (m + 1) * side, half * LANES : (half + 1) * LANES]
-                    if field < 2:
-                        matrix0[field, m, 2 * pair + half] = plane
-                    else:
-                        source0[field - 2, m, 2 * pair + half] = plane
+    block = rows // GROUP
+    side = block + 2 * HALO_ROWS // GROUP
+    row_ok, col_ok = edge_masks(
+        place, (side, LANES), HALO_ROWS // GROUP, rows, cols, gx * rows, gy * cols
+    )
+
+    def load(field, tile):
+        lanes = slice(tile * LANES, (tile + 1) * LANES)
+        tiles[field, tile, :HALO_ROWS] = lower[field, :, lanes]
+        tiles[field, tile, HALO_ROWS:] = upper[field, :, lanes]
+
+    def write(field, m, k, plane):
+        if field < 2:
+            matrix0[field, m, k, :block, :] = own[field, m, k] * (0.25 * factor[m, k, :block, :])
+            matrix0[field, m, k, block:, :] = plane * (0.25 * factor[m, k, block:, :])
+        else:
+            source0[field - 2, m, k, :block, :] = own[field, m, k]
+            source0[field - 2, m, k, block:, :] = plane
+
+    spread_fields(load, write, tiles, stacked, spread)
 
     def mix(k):
         for m in range(GROUP):
@@ -620,9 +713,8 @@
             restrict(other, target, level.count)
         else:
             restrict_last(other, source3)
-    first = HALO_ROWS // GROUP
     for at in range(len(FULL) + 2):
-        coarsest[at] = matrix3[at, first : first + rows // GROUP, :]
+        coarsest[at] = matrix3[at, :block, :]
 
 
 def restrict_last(residual, target):
@@ -643,21 +735,19 @@
 ):
     block = rows // GROUP
     for at in range(len(FULL) + 2):
-        for piece, part in enumerate((coarse_before, coarse, coarse_after)):
+        for piece, part in enumerate((coarse, coarse_after, coarse_before)):
             if at < len(FULL):
                 matrix3[at, 0, 0, piece * block : (piece + 1) * block, :] = part[at]
             else:
                 source3[at - len(FULL), 0, 0, piece * block : (piece + 1) * block, :] = part[at]
     level3 = Level(matrix3, FULL_AT, inverse3, spill3)
-    level3.make_inverse(*edge_masks(place, (3 * block, LANES), rows, cols, -rows, gx * rows, gy * cols))
+    level3.make_inverse(*edge_masks(place, (3 * block, LANES), block, rows, cols, gx * rows, gy * cols))
     start(level3, x3, source3)
     now, then = x3, other3
     for _ in range(COARSE_SWEEPS - 1):
         apply(level3, now, source3, then, residual=False)
         now, then = then, now
-    offset = block - HALO_ROWS // GROUP
-    side = (rows + 2 * HALO_ROWS) // GROUP
-    coarse_plane = functools.partial(cut_plane, now, offset, side)
+    coarse_plane = functools.partial(cut_plane, now, block)
 
     level0 = FineLevel(matrix0, {}, inverse0, spill0)
     level1 = Level(matrix1, FIRST_AT, inverse1, spill1)
@@ -669,38 +759,63 @@
     ):
         prolong(coarse_plane, before, x, level.count)
         close_columns(level, x)
-        apply(level, x, source, other, residual=False)
-        apply(level, other, source, x, residual=False)
+        last = level.count - 1
+        if level is level0:
+            apply(level, x, source, other, False, {0, last - 1, last}, {0, last})
+            apply(level, other, source, x, False, {last}, set())
+        else:
+            apply(level, x, source, other, residual=False)
+            apply(level, other, source, x, residual=False)
         coarse_plane = functools.partial(whole_plane, x)
 
-    for tile in range(cols // LANES):
-        at = lax.broadcasted_iota(jnp.int32, (GROUP * LANES, LANES), 1) + tile * LANES + HALO_COLS
-        target = (at & (GROUP - 1)) * LANES + (at >> LEVELS)
-        line = lax.broadcasted_iota(jnp.int32, (GROUP * LANES, LANES), 0)
-        gathered[:, tile * LANES : (tile + 1) * LANES] = jnp.where(line == target, 1.0, 0.0).astype(BF16)
-    first = HALO_ROWS // GROUP
+    at = lax.broadcasted_iota(jnp.int32, (WIDE, WIDE), 1)
+    line = lax.broadcasted_iota(jnp.int32, (WIDE, WIDE), 0)
+    gathered[...] = jnp.where(line == (at & (GROUP - 1)) * SPAN + (at >> LEVELS), 1.0, 0.0).astype(BF16)
+    lane = lax.broadcasted_iota(jnp.int32, (2 * block, LANES), 1)
     for component in (0, 1):
         for pair in range(GROUP // 2):
-            for k in range(GROUP):
-                value = jnp.concatenate(
-                    [x0[component, 2 * pair + h, k, first : first + block, :] for h in (0, 1)], axis=0
+            values = [
+                jnp.concatenate(
+                    [x0[component, 2 * pair + h, k, :block, :] for h in (0, 1)], axis=0
                 )
-                for part, piece in enumerate(three_parts(value)):
-                    line = part * 2 * rows + component * rows + pair * 2 * block
-                    stacked[line : line + 2 * block, k * LANES : (k + 1) * LANES] = piece
-    product = jnp.dot(stacked[...], gathered[...], preferred_element_type=F32)
-    product = product[: 2 * rows] + product[2 * rows : 4 * rows] + product[4 * rows :]
+                for k in range(GROUP)
+            ]
+            for piece in range(cols // WIDE):
+                for half in range(WIDE // LANES):
+                    slots = LANES // SPAN
+                    value = None
+                    for slot in reversed(range(slots)):
+                        part = turned(values[half * slots + slot], (slot - piece) * SPAN)
+                        value = part if value is None else jnp.where(lane < (slot + 1) * SPAN, part, value)
+                    lanes = slice(piece * WIDE + half * LANES, piece * WIDE + (half + 1) * LANES)
+                    for part, split in enumerate(three_parts(value)):
+                        line = part * 2 * rows + component * rows + pair * 2 * block
+                        stacked[line : line + 2 * block, lanes] = split
+    pieces = []
+    for piece in range(cols // WIDE):
+        product = jnp.dot(
+            stacked[:, piece * WIDE : (piece + 1) * WIDE], gathered[...], preferred_element_type=F32
+        )
+        pieces.append(product[: 2 * rows] + product[2 * rows : 4 * rows] + product[4 * rows :])
     for component in (0, 1):
         for tile in range(cols // LANES):
             lanes = slice(tile * LANES, (tile + 1) * LANES)
             for m in range(GROUP):
                 line = component * rows + m * block
-                tiles[component, tile, pl.ds(m, block, stride=GROUP), :] = product[line : line + block, lanes]
+                tiles[component, tile, pl.ds(m, block, stride=GROUP), :] = pieces[tile * LANES // WIDE][
+                    line : line + block, tile * LANES % WIDE : tile * LANES % WIDE + LANES
+                ]
             displacement[component, :, lanes] = tiles[component, tile]
 
 
-def cut_plane(x, offset, side, component, m, k):
-    return x[component, 0, 0, offset : offset + side, :]
+def cut_plane(x, block, component, m, k):
+    line = lax.broadcasted_iota(jnp.int32, (block, LANES), 0)
+    halo = jnp.where(
+        line < HALO_ROWS // GROUP,
+        x[component, 0, 0, block : 2 * block, :],
+        x[component, 0, 0, 2 * block :, :],
+    )
+    return jnp.concatenate([x[component, 0, 0, :block, :], halo], axis=0)
 
 
 def whole_plane(x, component, m, k):
@@ -718,11 +833,13 @@
     )
     left = passed_along(last_cols, "gy", 1)
     right = passed_along(first_cols, "gy", -1)
-    words = lax.all_to_all(words, ("gx", "gy"), 0, 0, tiled=True).reshape(devices, -1)
+    words = lax.all_to_all(words, ("gx", "gy"), 0, 0, tiled=True)
 
     last_rows, first_rows = pack_rows(fields, left, right)
     upper = passed_along(last_rows, "gx", 1)
     lower = passed_along(first_rows, "gx", -1)
+    own = spread_own(fields, left, right)
+    words, own = lax.optimization_barrier((words, own))
     factor = yield_factor(place, words, rows, cols, gy)
 
     tall, wide = rows + 2 * HALO_ROWS, cols + 2 * HALO_COLS
@@ -741,19 +858,15 @@
         functools.partial(down_kernel, rows=rows, cols=cols, gx=gx, gy=gy),
         out_shape=[jax.ShapeDtypeStruct(shape, F32) for shape in state]
         + [jax.ShapeDtypeStruct((held, rows // GROUP, LANES), F32)],
-        in_specs=[smem] + [vmem] * 6,
+        in_specs=[smem] + [vmem] * 4,
         out_specs=[vmem] * (len(state) + 1),
-        scratch_shapes=[
-            pltpu.VMEM((wide // LANES, tall, LANES), F32),
-            pltpu.VMEM((3 * tall, wide), BF16),
-            pltpu.VMEM((wide, GROUP * LANES), BF16),
-        ]
+        scratch_shapes=spread_scratch(2 * HALO_ROWS, wide)
         + [pltpu.VMEM(planes(2, count, 1), F32) for count in counts]
         + [pltpu.VMEM((2, count, side, LANES), F32) for count in counts]
         + [pltpu.VMEM((held, side, LANES), F32)],
         compiler_params=pltpu.CompilerParams(vmem_limit_bytes=VMEM_LIMIT),
         name="descent",
-    )(place, fields, left, right, upper, lower, factor)
+    )(place, own, upper, lower, factor)
 
     coarse_before = passed_along(coarse, "gx", 1)
     coarse_after = passed_along(coarse, "gx", -1)
@@ -776,8 +889,8 @@
             pltpu.VMEM(planes(2, 1, 0, lines), F32),
             pltpu.VMEM(planes(2, 1, 1, lines), F32),
             pltpu.VMEM(planes(2, 1, 1, lines), F32),
-            pltpu.VMEM((6 * rows, GROUP * LANES), BF16),
-            pltpu.VMEM((GROUP * LANES, cols), BF16),
+            pltpu.VMEM((6 * rows, cols), BF16),
+            pltpu.VMEM((WIDE, WIDE), BF16),
             pltpu.VMEM((2, cols // LANES, rows, LANES), F32),
         ],
         compiler_params=pltpu.CompilerParams(vmem_limit_bytes=VMEM_LIMIT),

time: 49 us -> 45.9 us (0.937)
  waiting for transfers between devices: 3.91 us -> 2.27 us
  Pallas kernels: 20.6 us -> 19.2 us
    pallas_call x1, Pallas kernels: 7.95 us -> 6.18 us  [body(): pl.pallas_call(functools.partial(down_kernel, rows=rows, cols=cols, gx=gx...]
    all_to_all x1, waiting for transfers between devices: 1.5 us -> 0.37 us  [body(): words = lax.all_to_all(words, ('gx', 'gy'), 0, 0, tiled=True)]
    pallas_call x0 -> x1, Pallas kernels: none -> 1.11 us  [spread_own(): pl.pallas_call(own_kernel, out_shape=jax.ShapeDtypeStruct((4, GROUP, GROU...]
    pallas_call x1, Pallas kernels: 6.44 us -> 5.52 us  [body(): pl.pallas_call(functools.partial(up_kernel, rows=rows, cols=cols, gx=gx,...]
    pallas_call x1, Pallas kernels: 4.38 us -> 4.91 us  [yield_factor(): pl.pallas_call(functools.partial(factor_kernel, rows=rows, cols=cols, gy=...]
    ppermute x6, waiting for transfers between devices: 2.42 us -> 1.89 us  [passed_along(): return lax.ppermute(array, axis, pairs)]
  transfers between devices with their start and end apart: 7 -> 7, of which waited for: 3 -> 3; matrix products, arithmetic and copies ran while one was open for 0% -> 0% of each run, Pallas kernels for 9% -> 13%
where the time goes in v4:
time: 45.9 us; the launch traced here: 45.6 us
  starting transfers between devices  24 us (52%)
  Pallas kernels  19.2 us (42%)
  waiting for transfers between devices  2.27 us (5%)
    ppermute x6, starting transfers between devices, passed_along(): return lax.ppermute(array, axis, pairs)  16.3 us
    all_to_all x1, starting transfers between devices, body(): words = lax.all_to_all(words, ('gx', 'gy'), 0, 0, tiled=True)  7.7 us
    pallas_call x1, Pallas kernels, body(): pl.pallas_call(functools.partial(down_kernel, rows=rows, cols=cols, gx=gx...  6.18 us
    pallas_call x1, Pallas kernels, body(): pl.pallas_call(functools.partial(up_kernel, rows=rows, cols=cols, gx=gx,...  5.52 us
    pallas_call x1, Pallas kernels, yield_factor(): pl.pallas_call(functools.partial(factor_kernel, rows=rows, cols=cols, gy=...  4.91 us
    ppermute x6, waiting for transfers between devices, passed_along(): return lax.ppermute(array, axis, pairs)  1.89 us
    pallas_call x1, Pallas kernels, pack(): pl.pallas_call(functools.partial(pack_kernel, cells=rows * cols), out_sha...  1.41 us
    pallas_call x1, Pallas kernels, spread_own(): pl.pallas_call(own_kernel, out_shape=jax.ShapeDtypeStruct((4, GROUP, GROU...  1.11 us
  transfers between devices with their start and end apart: 7, of which 3 were waited for; matrix products, arithmetic and copies ran while one was open for 0% of the time, Pallas kernels for 13%

profile of v4, /device:TPU:1, one launch (start us, length us, event | category | flops | bytes accessed | tf_op | source)
XLA Modules:
  0.0 45.6 jit_solution(392760511978464423)
XLA Ops:
  0.0 1.4 %pack.1 = (f32[4,64,512]{2,1,0:T(8,128)S(1)}, f32[4,64,128]{2,1,0:T(8,128)S(1)}, f32[4,64,128]{2,1,0:T(8,128)S(1)}, s32[32,1,512]{2,1,0:T(1,128)}) custom-call(f32[64,512]{1,0:T(8,128)} %first_lame.1, f32[64,512]{1,0:T(8,128)} %shear_modulus.1, f32[2,64,512]{2,1,0:T(8,128)} %applied_load.1, s32[1,512]{1,0:T(1,128)} %bitcast.5, s32[1,512]{1,0:T(1,128)} %bitcast.6, ...), custom_call_target="tpu_custom_call" | custom-call | tf_op jit(solution)/shard_map/pack/pallas_call | solution.py:176
  1.4 4.0 %collective-permute-start = (f32[4,64,128]{2,1,0:T(8,128)S(1)}, f32[4,64,128]{2,1,0:T(8,128)S(1)}, u32[]{:S(2)}, u32[]{:S(2)}) collective-permute-start(f32[4,64,128]{2,1,0:T(8,128)S(1)} %get-tuple-element.28), channel_id=1, source_target_pairs={{0,1},{1,2},{2,3},{3,4},{4,5},{5,6},{6,7},{8,9},{9,10},{10,11},{11... | collective-permute-start | bytes 393224 | tf_op jit(solution)/shard_map/ppermute | solution.py:36
  5.4 1.3 %collective-permute-start.1 = (f32[4,64,128]{2,1,0:T(8,128)S(1)}, f32[4,64,128]{2,1,0:T(8,128)S(1)}, u32[]{:S(2)}, u32[]{:S(2)}) collective-permute-start(f32[4,64,128]{2,1,0:T(8,128)S(1)} %get-tuple-element.29), channel_id=1, source_target_pairs={{1,0},{2,1},{3,2},{4,3},{5,4},{6,5},{7,6},{9,8},{10,9},{11,10},{12... | collective-permute-start | bytes 393224 | tf_op jit(solution)/shard_map/ppermute | solution.py:36
  6.7 7.7 %all-to-all-start = ((s32[32,1,512]{2,1,0:T(1,128)}), s32[32,1,512]{2,1,0:T(1,128)S(1)}, u32[]{:S(2)}, u32[]{:S(2)}) async-start(s32[32,1,512]{2,1,0:T(1,128)} %get-tuple-element.26), calls=%async_computation | async-start | bytes 131072 | tf_op jit(solution)/shard_map/all_to_all | solution.py:836
  14.4 0.0 collective-permute-done.left
  14.4 0.0 collective-permute-done.1.right
  14.4 0.1 pack_rows.1
  14.5 3.5 %collective-permute-start.2 = (f32[4,32,768]{2,1,0:T(8,128)S(1)}, f32[4,32,768]{2,1,0:T(8,128)S(1)}, u32[]{:S(2)}, u32[]{:S(2)}) collective-permute-start(f32[4,32,768]{2,1,0:T(8,128)S(1)} %get-tuple-element.31), channel_id=1, source_target_pairs={{0,8},{8,16},{16,24},{1,9},{9,17},{17,25},{2,10},{10,18},{18,26},{... | collective-permute-start | bytes 1179656 | tf_op jit(solution)/shard_map/ppermute | solution.py:36
  18.0 1.9 %collective-permute-start.3 = (f32[4,32,768]{2,1,0:T(8,128)S(1)}, f32[4,32,768]{2,1,0:T(8,128)S(1)}, u32[]{:S(2)}, u32[]{:S(2)}) collective-permute-start(f32[4,32,768]{2,1,0:T(8,128)S(1)} %get-tuple-element.32), channel_id=1, source_target_pairs={{8,0},{16,8},{24,16},{9,1},{17,9},{25,17},{10,2},{18,10},{26,18},{... | collective-permute-start | bytes 1179656 | tf_op jit(solution)/shard_map/ppermute | solution.py:36
  20.0 0.1 pad_add_fusion.place
  20.0 1.1 %spread_own.1.own = f32[4,8,8,8,128]{4,3,2,1,0:T(8,128)S(1)} custom-call(f32[4,64,512]{2,1,0:T(8,128)S(1)} %get-tuple-element.27.fields, f32[4,64,128]{2,1,0:T(8,128)S(1)} %collective-permute-done.left, f32[4,64,128]{2,1,0:T(8,128)S(1)} %collective-permute-done.1.right), custom_call_target="tpu_custom_call" | custom-call | flops 301989888 | tf_op jit(solution)/shard_map/spread_own/pallas_call | solution.py:639
  21.2 0.4 all-to-all-done.words
  21.5 4.9 %yield_factor.1.factor = f32[8,8,16,128]{3,2,1,0:T(8,128)S(1)} custom-call(s32[2]{0:T(128)S(1)} %pad_add_fusion.place, s32[32,1,512]{2,1,0:T(1,128)S(1)} %all-to-all-done.words), custom_call_target="tpu_custom_call" | custom-call | flops 3221225472 | bytes 65536 | tf_op jit(solution)/shard_map/yield_factor/pallas_call | solution.py:114
  26.5 0.0 collective-permute-done.2.upper
  26.5 0.7 %collective-permute-done.3.lower = f32[4,32,768]{2,1,0:T(8,128)S(1)} collective-permute-done((f32[4,32,768]{2,1,0:T(8,128)S(1)}, f32[4,32,768]{2,1,0:T(8,128)S(1)}, u32[]{:S(2)}, u32[]{:S(2)}) %collective-permute-start.3) | collective-permute-done | bytes 393248 | tf_op jit(solution)/shard_map/ppermute | solution.py:36
  27.1 6.2 %descent.1 = (f32[3,8,8,16,128]{4,3,2,1,0:T(8,128)S(1)}, f32[1,8,8,16,128]{4,3,2,1,0:T(8,128)S(1)}, f32[2,8,8,16,128]{4,3,2,1,0:T(8,128)S(1)}, f32[2,8,9,16,128]...) custom-call(s32[2]{0:T(128)S(1)} %pad_add_fusion.place, ...), custom_call_target="tpu_custom_call" | custom-call | tf_op jit(solution)/shard_map/descent/pallas_call | solution.py:857
  33.3 1.9 %collective-permute-start.5 = (f32[14,8,128]{2,1,0:T(8,128)S(1)}, f32[14,8,128]{2,1,0:T(8,128)S(1)}, u32[]{:S(2)}, u32[]{:S(2)}) collective-permute-start(f32[14,8,128]{2,1,0:T(8,128)S(1)} %get-tuple-element.34.coarse), channel_id=1, source_target_pairs={{8,0},{16,8},{24,16},{9,1},{17,9},{25,17},{10,2},{18,10},{26,18},{... | collective-permute-start | bytes 172040 | tf_op jit(solution)/shard_map/ppermute | solution.py:36
  35.2 3.6 %collective-permute-start.4 = (f32[14,8,128]{2,1,0:T(8,128)S(1)}, f32[14,8,128]{2,1,0:T(8,128)S(1)}, u32[]{:S(2)}, u32[]{:S(2)}) collective-permute-start(f32[14,8,128]{2,1,0:T(8,128)S(1)} %get-tuple-element.34.coarse), channel_id=1, source_target_pairs={{0,8},{8,16},{16,24},{1,9},{9,17},{17,25},{2,10},{10,18},{18,26},{... | collective-permute-start | bytes 172040 | tf_op jit(solution)/shard_map/ppermute | solution.py:36
  38.9 0.0 collective-permute-done.5.coarse_after
  38.9 1.2 %collective-permute-done.4.coarse_before = f32[14,8,128]{2,1,0:T(8,128)S(1)} collective-permute-done((f32[14,8,128]{2,1,0:T(8,128)S(1)}, f32[14,8,128]{2,1,0:T(8,128)S(1)}, u32[]{:S(2)}, u32[]{:S(2)}) %collective-permute-start.4) | collective-permute-done | bytes 57376 | tf_op jit(solution)/shard_map/ppermute | solution.py:36
  40.1 5.5 %ascent.1 = f32[2,64,512]{2,1,0:T(8,128)} custom-call(s32[2]{0:T(128)S(1)} %pad_add_fusion.place, f32[14,8,128]{2,1,0:T(8,128)S(1)} %get-tuple-element.34.coarse, f32[14,8,128]{2,1,0:T(8,128)S(1)} %collective-permute-done.4.coarse_before, f32[14,8,128]{2,1,0:T(8,128)S(1)} %collective-permute-done.5.coarse_after, ...), custom_call_target="tpu_custom_call" | custom-call | tf_op jit(solution)/shard_map/ascent/pallas_call | solution.py:874
Async XLA Ops:
  1.4 13.0 %collective-permute-start = (f32[4,64,128]{2,1,0:T(8,128)S(1)}, f32[4,64,128]{2,1,0:T(8,128)S(1)}, u32[]{:S(2)}, u32[]{:S(2)}) collective-permute-start(f32[4,64,128]{2,1,0:T(8,128)S(1)} %get-tuple-element.28), channel_id=1, source_target_pairs={{0,1},{1,2},{2,3},{3,4},{4,5},{5,6},{6,7},{8,9},{9,10},{10,11},{11... | collective-permute-start | bytes 393224 | tf_op jit(solution)/shard_map/ppermute | solution.py:36
  5.4 9.0 %collective-permute-start.1 = (f32[4,64,128]{2,1,0:T(8,128)S(1)}, f32[4,64,128]{2,1,0:T(8,128)S(1)}, u32[]{:S(2)}, u32[]{:S(2)}) collective-permute-start(f32[4,64,128]{2,1,0:T(8,128)S(1)} %get-tuple-element.29), channel_id=1, source_target_pairs={{1,0},{2,1},{3,2},{4,3},{5,4},{6,5},{7,6},{9,8},{10,9},{11,10},{12... | collective-permute-start | bytes 393224 | tf_op jit(solution)/shard_map/ppermute | solution.py:36
  6.7 14.9 %all-to-all-start = ((s32[32,1,512]{2,1,0:T(1,128)}), s32[32,1,512]{2,1,0:T(1,128)S(1)}, u32[]{:S(2)}, u32[]{:S(2)}) async-start(s32[32,1,512]{2,1,0:T(1,128)} %get-tuple-element.26), calls=%async_computation | async-start | bytes 131072 | tf_op jit(solution)/shard_map/all_to_all | solution.py:836
  14.5 12.0 %collective-permute-start.2 = (f32[4,32,768]{2,1,0:T(8,128)S(1)}, f32[4,32,768]{2,1,0:T(8,128)S(1)}, u32[]{:S(2)}, u32[]{:S(2)}) collective-permute-start(f32[4,32,768]{2,1,0:T(8,128)S(1)} %get-tuple-element.31), channel_id=1, source_target_pairs={{0,8},{8,16},{16,24},{1,9},{9,17},{17,25},{2,10},{10,18},{18,26},{... | collective-permute-start | bytes 1179656 | tf_op jit(solution)/shard_map/ppermute | solution.py:36
  18.0 9.1 %collective-permute-start.3 = (f32[4,32,768]{2,1,0:T(8,128)S(1)}, f32[4,32,768]{2,1,0:T(8,128)S(1)}, u32[]{:S(2)}, u32[]{:S(2)}) collective-permute-start(f32[4,32,768]{2,1,0:T(8,128)S(1)} %get-tuple-element.32), channel_id=1, source_target_pairs={{8,0},{16,8},{24,16},{9,1},{17,9},{25,17},{10,2},{18,10},{26,18},{... | collective-permute-start | bytes 1179656 | tf_op jit(solution)/shard_map/ppermute | solution.py:36
  33.3 5.6 %collective-permute-start.5 = (f32[14,8,128]{2,1,0:T(8,128)S(1)}, f32[14,8,128]{2,1,0:T(8,128)S(1)}, u32[]{:S(2)}, u32[]{:S(2)}) collective-permute-start(f32[14,8,128]{2,1,0:T(8,128)S(1)} %get-tuple-element.34.coarse), channel_id=1, source_target_pairs={{8,0},{16,8},{24,16},{9,1},{17,9},{25,17},{10,2},{18,10},{26,18},{... | collective-permute-start | bytes 172040 | tf_op jit(solution)/shard_map/ppermute | solution.py:36
  35.2 4.9 %collective-permute-start.4 = (f32[14,8,128]{2,1,0:T(8,128)S(1)}, f32[14,8,128]{2,1,0:T(8,128)S(1)}, u32[]{:S(2)}, u32[]{:S(2)}) collective-permute-start(f32[14,8,128]{2,1,0:T(8,128)S(1)} %get-tuple-element.34.coarse), channel_id=1, source_target_pairs={{0,8},{8,16},{16,24},{1,9},{9,17},{17,25},{2,10},{10,18},{18,26},{... | collective-permute-start | bytes 172040 | tf_op jit(solution)/shard_map/ppermute | solution.py:36

commit v5 on v4

--- a/solution.py
+++ b/solution.py
@@ -30,9 +30,11 @@
 FULL_AT = {name: FULL.index(name) for name in FULL} | {"22": 0}
 
 
-def passed_along(array, axis, by):
+def swapped(array, axis, odd_pairs):
     devices = lax.axis_size(axis)
-    pairs = [(i, i + by) for i in range(devices) if 0 <= i + by < devices]
+    pairs = []
+    for i in range(odd_pairs, devices - 1, 2):
+        pairs += [(i, i + 1), (i + 1, i)]
     return lax.ppermute(array, axis, pairs)
 
 
@@ -62,15 +64,15 @@
     return None if term is None else weight * term
 
 
-def factor_kernel(place, words, factor, tall_of, lane_of, codes, counts, *, rows, cols, gy):
+def factor_kernel(words, factor, tall_of, lane_of, codes, counts, *, rows, cols, gy):
     for at in range(words.shape[0]):
         tall_of[at : at + 1, :] = words[at]
     word = tall_of[...]
     cell_bits = log2(rows * cols)
     owner = word >> (cell_bits + 2)
     cell = (word >> 2) & (rows * cols - 1)
-    row = (owner >> log2(gy)) * rows + (cell >> log2(cols)) - place[0] * rows
-    col = (owner & (gy - 1)) * cols + (cell & (cols - 1)) - place[1] * cols
+    row = (owner >> log2(gy)) * rows + (cell >> log2(cols)) - lax.axis_index("gx") * rows
+    col = (owner & (gy - 1)) * cols + (cell & (cols - 1)) - lax.axis_index("gy") * cols
     tall = rows + 2 * HALO_ROWS
     side = tall // GROUP
     inside = (row >= -HALO_ROWS) & (row < rows + HALO_ROWS) & (col >= -HALO_COLS) & (col < cols + HALO_COLS)
@@ -108,16 +110,13 @@
             factor[m, k] = jnp.exp(count * math.log(YIELD_DROP))
 
 
-def yield_factor(place, words, rows, cols, gy):
+def yield_factor(words, rows, cols, gy):
     tall, wide = rows + 2 * HALO_ROWS, cols + 2 * HALO_COLS
     lists = (words.shape[0], words.shape[2])
     return pl.pallas_call(
         functools.partial(factor_kernel, rows=rows, cols=cols, gy=gy),
         out_shape=jax.ShapeDtypeStruct((GROUP, GROUP, tall // GROUP, LANES), F32),
-        in_specs=[
-            pl.BlockSpec(memory_space=pltpu.SMEM),
-            pl.BlockSpec(memory_space=pltpu.VMEM),
-        ],
+        in_specs=[pl.BlockSpec(memory_space=pltpu.VMEM)],
         out_specs=pl.BlockSpec(memory_space=pltpu.VMEM),
         scratch_shapes=[
             pltpu.VMEM(lists, jnp.int32),
@@ -130,12 +129,12 @@
             flops=2 * tall * wide * words.size, bytes_accessed=4 * words.size, transcendentals=tall * wide
         ),
         name="yield_factor",
-    )(place, words)
+    )(words)
 
 
 def pack_kernel(
     first_lame, shear_modulus, applied_load, owner, cell, code,
-    fields, first_cols, last_cols, words, lists, copied, arrived,
+    fields, even_cols, odd_cols, words, lists, copied, arrived,
     *, cells,
 ):
     copies = [
@@ -162,8 +161,9 @@
     sent.start()
     for copy in copies[3:]:
         copy.wait()
-    first_cols[...] = fields[:, :, :HALO_COLS]
-    last_cols[...] = fields[:, :, fields.shape[2] - HALO_COLS :]
+    last, odd = fields.shape[2] - HALO_COLS, lax.axis_index("gy") & 1
+    even_cols[...] = fields[:, :, pl.ds(pl.multiple_of(last * (1 - odd), HALO_COLS), HALO_COLS)]
+    odd_cols[...] = fields[:, :, pl.ds(pl.multiple_of(last * odd, HALO_COLS), HALO_COLS)]
     sent.wait()
 
 
@@ -193,16 +193,18 @@
     )(*[pltpu.with_memory_space_constraint(array, pltpu.HBM) for array in arrays])
 
 
-def rows_kernel(fields, left, right, last_rows, first_rows):
-    cols = fields.shape[2]
-    for out, start in ((last_rows, fields.shape[1] - HALO_ROWS), (first_rows, 0)):
-        span = slice(start, start + HALO_ROWS)
+def rows_kernel(fields, even_side, odd_side, even_rows, odd_rows):
+    rows, cols = fields.shape[1:]
+    last, odd, odd_col = rows - HALO_ROWS, lax.axis_index("gx") & 1, lax.axis_index("gy") & 1
+    for out, side in ((even_rows, 1 - odd), (odd_rows, odd)):
+        span = pl.ds(pl.multiple_of(last * side, HALO_ROWS), HALO_ROWS)
         out[:, :, :cols] = fields[:, span, :]
-        out[:, :, cols : cols + HALO_COLS] = left[:, span, :]
-        out[:, :, cols + HALO_COLS :] = right[:, span, :]
-
-
-def pack_rows(fields, left, right):
+        for halo, after in ((even_side, 1 - odd_col), (odd_side, odd_col)):
+            at = pl.multiple_of(cols + HALO_COLS * after, HALO_COLS)
+            out[:, :, pl.ds(at, HALO_COLS)] = halo[:, span, :]
+
+
+def pack_rows(fields, even_side, odd_side):
     edge = jax.ShapeDtypeStruct((4, HALO_ROWS, fields.shape[2] + 2 * HALO_COLS), F32)
     vmem = pl.BlockSpec(memory_space=pltpu.VMEM)
     return pl.pallas_call(
@@ -212,7 +214,7 @@
         out_specs=[vmem] * 2,
         compiler_params=pltpu.CompilerParams(vmem_limit_bytes=8 * 1024 * 1024),
         name="pack_rows",
-    )(fields, left, right)
+    )(fields, even_side, odd_side)
 
 
 class Level:
@@ -541,13 +543,13 @@
                 write(FULL_AT[name], m, k, values[name])
 
 
-def edge_masks(place, shape, before, rows, cols, grid_rows, grid_cols):
+def edge_masks(shape, before, rows, cols, grid_rows, grid_cols):
     def wrapped(axis, ahead):
         at = lax.broadcasted_iota(jnp.int32, shape, axis)
         return jnp.where(at < shape[axis] - ahead, at, at - shape[axis]) * GROUP
 
-    row = wrapped(0, before) + place[0] * rows
-    col = wrapped(1, HALO_COLS // GROUP) + place[1] * cols
+    row = wrapped(0, before) + lax.axis_index("gx") * rows
+    col = wrapped(1, HALO_COLS // GROUP) + lax.axis_index("gy") * cols
     return (
         jnp.where(row < grid_rows, 1.0, 0.0).astype(F32),
         jnp.where(col < grid_cols, 1.0, 0.0).astype(F32),
@@ -610,14 +612,16 @@
                 write(field, m, k, gather_lanes([piece[lines, lanes] for piece in pieces], slot))
 
 
-def own_kernel(fields, left, right, planes, tiles, stacked, spread):
-    own_tiles = fields.shape[2] // LANES
+def own_kernel(fields, even_side, odd_side, planes, tiles, stacked, spread):
+    own_tiles, odd = fields.shape[2] // LANES, lax.axis_index("gy") & 1
 
     def load(field, tile):
         if tile < own_tiles:
             tiles[field, tile] = fields[field, :, tile * LANES : (tile + 1) * LANES]
+        elif tile == own_tiles:
+            tiles[field, tile + 1 - odd] = even_side[field]
         else:
-            tiles[field, tile] = (left if tile == own_tiles else right)[field]
+            tiles[field, own_tiles + odd] = odd_side[field]
 
     def write(field, m, k, plane):
         planes[field, m, k] = plane
@@ -633,7 +637,7 @@
     ]
 
 
-def spread_own(fields, left, right):
+def spread_own(fields, even_side, odd_side):
     rows, wide = fields.shape[1], fields.shape[2] + 2 * HALO_COLS
     vmem = pl.BlockSpec(memory_space=pltpu.VMEM)
     return pl.pallas_call(
@@ -645,11 +649,11 @@
         compiler_params=pltpu.CompilerParams(vmem_limit_bytes=12 * 1024 * 1024),
         cost_estimate=pl.CostEstimate(flops=24 * rows * wide * WIDE, bytes_accessed=0, transcendentals=0),
         name="spread_own",
-    )(fields, left, right)
+    )(fields, even_side, odd_side)
 
 
 def down_kernel(
-    place, own, upper, lower, factor,
+    own, even_rows, odd_rows, factor,
     matrix0, inverse0, source0, x0, matrix1, inverse1, source1, x1, matrix2, inverse2, source2, x2, coarsest,
     tiles, stacked, spread, other0, other1, other2, spill0, spill1, spill2, matrix3,
     *, rows, cols, gx, gy,
@@ -657,13 +661,16 @@
     block = rows // GROUP
     side = block + 2 * HALO_ROWS // GROUP
     row_ok, col_ok = edge_masks(
-        place, (side, LANES), HALO_ROWS // GROUP, rows, cols, gx * rows, gy * cols
+        (side, LANES), HALO_ROWS // GROUP, rows, cols, gx * rows, gy * cols
     )
+
+    odd = lax.axis_index("gx") & 1
 
     def load(field, tile):
         lanes = slice(tile * LANES, (tile + 1) * LANES)
-        tiles[field, tile, :HALO_ROWS] = lower[field, :, lanes]
-        tiles[field, tile, HALO_ROWS:] = upper[field, :, lanes]
+        for halo, before in ((even_rows, odd), (odd_rows, 1 - odd)):
+            span = pl.ds(pl.multiple_of(HALO_ROWS * before, HALO_ROWS), HALO_ROWS)
+            tiles[field, tile, span, :] = halo[field, :, lanes]
 
     def write(field, m, k, plane):
         if field < 2:
@@ -726,22 +733,23 @@
 
 
 def up_kernel(
-    place, coarse, coarse_before, coarse_after,
+    coarse, coarse_even, coarse_odd,
     matrix0, inverse0, source0, x0_in, matrix1, inverse1, source1, x1_in, matrix2, inverse2, source2, x2_in,
     displacement,
     x0, other0, x1, other1, x2, other2, spill0, spill1, spill2, spill3, matrix3, inverse3, source3, x3, other3,
     stacked, gathered, tiles,
     *, rows, cols, gx, gy,
 ):
-    block = rows // GROUP
+    block, odd = rows // GROUP, lax.axis_index("gx") & 1
     for at in range(len(FULL) + 2):
-        for piece, part in enumerate((coarse, coarse_after, coarse_before)):
+        for piece, part in ((0, coarse), (1 + odd, coarse_even), (2 - odd, coarse_odd)):
+            lines = pl.ds(pl.multiple_of(piece * block, block), block)
             if at < len(FULL):
-                matrix3[at, 0, 0, piece * block : (piece + 1) * block, :] = part[at]
+                matrix3[at, 0, 0, lines, :] = part[at]
             else:
-                source3[at - len(FULL), 0, 0, piece * block : (piece + 1) * block, :] = part[at]
+                source3[at - len(FULL), 0, 0, lines, :] = part[at]
     level3 = Level(matrix3, FULL_AT, inverse3, spill3)
-    level3.make_inverse(*edge_masks(place, (3 * block, LANES), block, rows, cols, gx * rows, gy * cols))
+    level3.make_inverse(*edge_masks((3 * block, LANES), block, rows, cols, gx * rows, gy * cols))
     start(level3, x3, source3)
     now, then = x3, other3
     for _ in range(COARSE_SWEEPS - 1):
@@ -826,25 +834,22 @@
     rows, cols = first_lame.shape
     gx, gy = lax.axis_size("gx"), lax.axis_size("gy")
     devices = gx * gy
-    place = jnp.stack([lax.axis_index("gx"), lax.axis_index("gy")]).astype(jnp.int32)
-
-    fields, first_cols, last_cols, words = pack(
+
+    fields, even_cols, odd_cols, words = pack(
         first_lame, shear_modulus, applied_load, plastic_owner, plastic_cell, plastic_code, devices
     )
-    left = passed_along(last_cols, "gy", 1)
-    right = passed_along(first_cols, "gy", -1)
+    even_side, odd_side = swapped(even_cols, "gy", 0), swapped(odd_cols, "gy", 1)
     words = lax.all_to_all(words, ("gx", "gy"), 0, 0, tiled=True)
 
-    last_rows, first_rows = pack_rows(fields, left, right)
-    upper = passed_along(last_rows, "gx", 1)
-    lower = passed_along(first_rows, "gx", -1)
-    own = spread_own(fields, left, right)
+    even_rows, odd_rows = pack_rows(fields, even_side, odd_side)
+    even_rows, odd_rows = swapped(even_rows, "gx", 0), swapped(odd_rows, "gx", 1)
+    own = spread_own(fields, even_side, odd_side)
     words, own = lax.optimization_barrier((words, own))
-    factor = yield_factor(place, words, rows, cols, gy)
+    factor = yield_factor(words, rows, cols, gy)
 
     tall, wide = rows + 2 * HALO_ROWS, cols + 2 * HALO_COLS
     side = tall // GROUP
-    vmem, smem = pl.BlockSpec(memory_space=pltpu.VMEM), pl.BlockSpec(memory_space=pltpu.SMEM)
+    vmem = pl.BlockSpec(memory_space=pltpu.VMEM)
 
     def planes(fields, count, extra=0, lines=side):
         return (fields, count, count + extra, lines, LANES)
@@ -858,7 +863,7 @@
         functools.partial(down_kernel, rows=rows, cols=cols, gx=gx, gy=gy),
         out_shape=[jax.ShapeDtypeStruct(shape, F32) for shape in state]
         + [jax.ShapeDtypeStruct((held, rows // GROUP, LANES), F32)],
-        in_specs=[smem] + [vmem] * 4,
+        in_specs=[vmem] * 4,
         out_specs=[vmem] * (len(state) + 1),
         scratch_shapes=spread_scratch(2 * HALO_ROWS, wide)
         + [pltpu.VMEM(planes(2, count, 1), F32) for count in counts]
@@ -866,15 +871,14 @@
         + [pltpu.VMEM((held, side, LANES), F32)],
         compiler_params=pltpu.CompilerParams(vmem_limit_bytes=VMEM_LIMIT),
         name="descent",
-    )(place, own, upper, lower, factor)
-
-    coarse_before = passed_along(coarse, "gx", 1)
-    coarse_after = passed_along(coarse, "gx", -1)
+    )(own, even_rows, odd_rows, factor)
+
+    coarse_even, coarse_odd = swapped(coarse, "gx", 0), swapped(coarse, "gx", 1)
     lines = 3 * (rows // GROUP)
     return pl.pallas_call(
         functools.partial(up_kernel, rows=rows, cols=cols, gx=gx, gy=gy),
         out_shape=jax.ShapeDtypeStruct((2, rows, cols), F32),
-        in_specs=[smem] + [vmem] * (3 + len(state)),
+        in_specs=[vmem] * (3 + len(state)),
         out_specs=vmem,
         scratch_shapes=[
             shape
@@ -895,7 +899,7 @@
         ],
         compiler_params=pltpu.CompilerParams(vmem_limit_bytes=VMEM_LIMIT),
         name="ascent",
-    )(place, coarse, coarse_before, coarse_after, *state)
+    )(coarse, coarse_even, coarse_odd, *state)
 
 
 def solution(mesh):

time: 45.9 us -> 40.4 us (0.88)
  starting transfers between devices: 24 us -> 17.5 us
  waiting for transfers between devices: 2.27 us -> 4.98 us
  Pallas kernels: 19.2 us -> 17.5 us
    ppermute x6, starting transfers between devices: 16.3 us -> 9.18 us  [swapped(): return lax.ppermute(array, axis, pairs)]
    all_to_all x1, waiting for transfers between devices: 0.37 us -> 2.16 us  [body(): words = lax.all_to_all(words, ('gx', 'gy'), 0, 0, tiled=True)]
    ppermute x6, waiting for transfers between devices: 1.89 us -> 2.82 us  [swapped(): return lax.ppermute(array, axis, pairs)]
    all_to_all x1, starting transfers between devices: 7.7 us -> 8.33 us  [body(): words = lax.all_to_all(words, ('gx', 'gy'), 0, 0, tiled=True)]
    pallas_call x1, Pallas kernels: 6.18 us -> 5.57 us  [body(): pl.pallas_call(functools.partial(down_kernel, rows=rows, cols=cols, gx=gx...]
    pallas_call x1, Pallas kernels: 4.91 us -> 4.37 us  [yield_factor(): pl.pallas_call(functools.partial(factor_kernel, rows=rows, cols=cols, gy=...]
    pallas_call x1, Pallas kernels: 5.52 us -> 4.98 us  [body(): pl.pallas_call(functools.partial(up_kernel, rows=rows, cols=cols, gx=gx,...]
  transfers between devices with their start and end apart: 7 -> 7, of which waited for: 3 -> 2; matrix products, arithmetic and copies ran while one was open for 0% -> 0% of each run, Pallas kernels for 13% -> 14%
where the time goes in v5:
time: 40.4 us; the launch traced here: 40.1 us
  Pallas kernels  17.5 us (43%)
  starting transfers between devices  17.5 us (43%)
  waiting for transfers between devices  4.98 us (12%)
    ppermute x6, starting transfers between devices, swapped(): return lax.ppermute(array, axis, pairs)  9.18 us
    all_to_all x1, starting transfers between devices, body(): words = lax.all_to_all(words, ('gx', 'gy'), 0, 0, tiled=True)  8.33 us
    pallas_call x1, Pallas kernels, body(): pl.pallas_call(functools.partial(down_kernel, rows=rows, cols=cols, gx=gx...  5.57 us
    pallas_call x1, Pallas kernels, body(): pl.pallas_call(functools.partial(up_kernel, rows=rows, cols=cols, gx=gx,...  4.98 us
    pallas_call x1, Pallas kernels, yield_factor(): pl.pallas_call(functools.partial(factor_kernel, rows=rows, cols=cols, gy=...  4.37 us
    ppermute x6, waiting for transfers between devices, swapped(): return lax.ppermute(array, axis, pairs)  2.82 us
    all_to_all x1, waiting for transfers between devices, body(): words = lax.all_to_all(words, ('gx', 'gy'), 0, 0, tiled=True)  2.16 us
    pallas_call x1, Pallas kernels, pack(): pl.pallas_call(functools.partial(pack_kernel, cells=rows * cols), out_sha...  1.41 us
  transfers between devices with their start and end apart: 7, of which 2 were waited for; matrix products, arithmetic and copies ran while one was open for 0% of the time, Pallas kernels for 14%

profile of v5, /device:TPU:1, one launch (start us, length us, event | category | flops | bytes accessed | tf_op | source)
XLA Modules:
  0.0 40.1 jit_solution(9291185890881758331)
XLA Ops:
  0.0 1.4 %pack.1 = (f32[4,64,512]{2,1,0:T(8,128)S(1)}, f32[4,64,128]{2,1,0:T(8,128)S(1)}, f32[4,64,128]{2,1,0:T(8,128)S(1)}, s32[32,1,512]{2,1,0:T(1,128)}) custom-call(f32[64,512]{1,0:T(8,128)} %first_lame.1, f32[64,512]{1,0:T(8,128)} %shear_modulus.1, f32[2,64,512]{2,1,0:T(8,128)} %applied_load.1, s32[1,512]{1,0:T(1,128)} %bitcast.3, s32[1,512]{1,0:T(1,128)} %bitcast.4, ...), custom_call_target="tpu_custom_call" | custom-call | tf_op jit(solution)/shard_map/pack/pallas_call | solution.py:176
  1.4 2.1 %collective-permute-start = (f32[4,64,128]{2,1,0:T(8,128)S(1)}, f32[4,64,128]{2,1,0:T(8,128)S(1)}, u32[]{:S(2)}, u32[]{:S(2)}) collective-permute-start(f32[4,64,128]{2,1,0:T(8,128)S(1)} %get-tuple-element.28), channel_id=1, source_target_pairs={{0,1},{1,0},{2,3},{3,2},{4,5},{5,4},{6,7},{7,6},{8,9},{9,8},{10,11... | collective-permute-start | bytes 393224 | tf_op jit(solution)/shard_map/ppermute | solution.py:38
  3.5 0.7 %collective-permute-start.1 = (f32[4,64,128]{2,1,0:T(8,128)S(1)}, f32[4,64,128]{2,1,0:T(8,128)S(1)}, u32[]{:S(2)}, u32[]{:S(2)}) collective-permute-start(f32[4,64,128]{2,1,0:T(8,128)S(1)} %get-tuple-element.29), channel_id=1, source_target_pairs={{1,2},{2,1},{3,4},{4,3},{5,6},{6,5},{9,10},{10,9},{11,12},{12,11},... | collective-permute-start | bytes 393224 | tf_op jit(solution)/shard_map/ppermute | solution.py:38
  4.2 8.3 %all-to-all-start = ((s32[32,1,512]{2,1,0:T(1,128)}), s32[32,1,512]{2,1,0:T(1,128)S(1)}, u32[]{:S(2)}, u32[]{:S(2)}) async-start(s32[32,1,512]{2,1,0:T(1,128)} %get-tuple-element.26), calls=%async_computation | async-start | bytes 131072 | tf_op jit(solution)/shard_map/all_to_all | solution.py:842
  12.5 0.0 collective-permute-done.even_side
  12.5 0.0 collective-permute-done.1.odd_side
  12.5 0.1 pack_rows.1
  12.6 0.3 collective-permute-start.2
  12.9 3.4 %collective-permute-start.3 = (f32[4,32,768]{2,1,0:T(8,128)S(1)}, f32[4,32,768]{2,1,0:T(8,128)S(1)}, u32[]{:S(2)}, u32[]{:S(2)}) collective-permute-start(f32[4,32,768]{2,1,0:T(8,128)S(1)} %get-tuple-element.32), channel_id=1, source_target_pairs={{8,16},{16,8},{9,17},{17,9},{10,18},{18,10},{11,19},{19,11},{12,20... | collective-permute-start | bytes 1179656 | tf_op jit(solution)/shard_map/ppermute | solution.py:38
  16.4 1.1 %spread_own.1.own = f32[4,8,8,8,128]{4,3,2,1,0:T(8,128)S(1)} custom-call(f32[4,64,512]{2,1,0:T(8,128)S(1)} %get-tuple-element.27.fields, f32[4,64,128]{2,1,0:T(8,128)S(1)} %collective-permute-done.even_side, f32[4,64,128]{2,1,0:T(8,128)S(1)} %collective-permute-done.1.odd_side), custom_call_target="tpu_custom_call" | custom-call | flops 301989888 | tf_op jit(solution)/shard_map/spread_own/pallas_call | solution.py:643
  17.5 2.2 %all-to-all-done.words = s32[32,1,512]{2,1,0:T(1,128)S(1)} async-done(((s32[32,1,512]{2,1,0:T(1,128)}), s32[32,1,512]{2,1,0:T(1,128)S(1)}, u32[]{:S(2)}, u32[]{:S(2)}) %all-to-all-start) | async-done | bytes 65568 | tf_op jit(solution)/shard_map/all_to_all | solution.py:842
  19.7 4.4 %yield_factor.1.factor = f32[8,8,16,128]{3,2,1,0:T(8,128)S(1)} custom-call(s32[32,1,512]{2,1,0:T(1,128)S(1)} %all-to-all-done.words), custom_call_target="tpu_custom_call" | custom-call | flops 3221225472 | bytes 65536 | tf_op jit(solution)/shard_map/yield_factor/pallas_call | solution.py:116
  24.0 0.0 collective-permute-done.2.even_rows
  24.1 0.0 collective-permute-done.3.odd_rows
  24.1 5.6 %descent.1 = (f32[3,8,8,16,128]{4,3,2,1,0:T(8,128)S(1)}, f32[1,8,8,16,128]{4,3,2,1,0:T(8,128)S(1)}, f32[2,8,8,16,128]{4,3,2,1,0:T(8,128)S(1)}, f32[2,8,9,16,128]...) custom-call(f32[4,8,8,8,128]{4,3,2,1,0:T(8,128)S(1)} %spread_own.1.o, ...), custom_call_target="tpu_custom_call" | custom-call | tf_op jit(solution)/shard_map/descent/pallas_call | solution.py:862
  29.7 2.6 %collective-permute-start.5 = (f32[14,8,128]{2,1,0:T(8,128)S(1)}, f32[14,8,128]{2,1,0:T(8,128)S(1)}, u32[]{:S(2)}, u32[]{:S(2)}) collective-permute-start(f32[14,8,128]{2,1,0:T(8,128)S(1)} %get-tuple-element.34.coarse), channel_id=1, source_target_pairs={{8,16},{16,8},{9,17},{17,9},{10,18},{18,10},{11,19},{19,11},{12,20... | collective-permute-start | bytes 172040 | tf_op jit(solution)/shard_map/ppermute | solution.py:38
  32.3 0.1 collective-permute-start.4
  32.3 2.8 %collective-permute-done.5.coarse_odd = f32[14,8,128]{2,1,0:T(8,128)S(1)} collective-permute-done((f32[14,8,128]{2,1,0:T(8,128)S(1)}, f32[14,8,128]{2,1,0:T(8,128)S(1)}, u32[]{:S(2)}, u32[]{:S(2)}) %collective-permute-start.5) | collective-permute-done | bytes 57376 | tf_op jit(solution)/shard_map/ppermute | solution.py:38
  35.1 0.0 collective-permute-done.4.coarse_even
  35.2 5.0 %ascent.1 = f32[2,64,512]{2,1,0:T(8,128)} custom-call(f32[14,8,128]{2,1,0:T(8,128)S(1)} %get-tuple-element.34.coarse, f32[14,8,128]{2,1,0:T(8,128)S(1)} %collective-permute-done.4.coarse_even, f32[14,8,128]{2,1,0:T(8,128)S(1)} %collective-permute-done.5.coarse_odd, f32[3,8,8,16,128]{4,3,2,1,0:T(8,128)S(1)} %get-tuple-element.35.matrix0, ...), custom_call_target="tpu_custom_call" | custom-call | tf_op jit(solution)/shard_map/ascent/pallas_call | solution.py:878
Async XLA Ops:
  1.4 11.1 %collective-permute-start = (f32[4,64,128]{2,1,0:T(8,128)S(1)}, f32[4,64,128]{2,1,0:T(8,128)S(1)}, u32[]{:S(2)}, u32[]{:S(2)}) collective-permute-start(f32[4,64,128]{2,1,0:T(8,128)S(1)} %get-tuple-element.28), channel_id=1, source_target_pairs={{0,1},{1,0},{2,3},{3,2},{4,5},{5,4},{6,7},{7,6},{8,9},{9,8},{10,11... | collective-permute-start | bytes 393224 | tf_op jit(solution)/shard_map/ppermute | solution.py:38
  3.5 9.0 %collective-permute-start.1 = (f32[4,64,128]{2,1,0:T(8,128)S(1)}, f32[4,64,128]{2,1,0:T(8,128)S(1)}, u32[]{:S(2)}, u32[]{:S(2)}) collective-permute-start(f32[4,64,128]{2,1,0:T(8,128)S(1)} %get-tuple-element.29), channel_id=1, source_target_pairs={{1,2},{2,1},{3,4},{4,3},{5,6},{6,5},{9,10},{10,9},{11,12},{12,11},... | collective-permute-start | bytes 393224 | tf_op jit(solution)/shard_map/ppermute | solution.py:38
  4.2 15.5 %all-to-all-start = ((s32[32,1,512]{2,1,0:T(1,128)}), s32[32,1,512]{2,1,0:T(1,128)S(1)}, u32[]{:S(2)}, u32[]{:S(2)}) async-start(s32[32,1,512]{2,1,0:T(1,128)} %get-tuple-element.26), calls=%async_computation | async-start | bytes 131072 | tf_op jit(solution)/shard_map/all_to_all | solution.py:842
  12.6 11.4 %collective-permute-start.2 = (f32[4,32,768]{2,1,0:T(8,128)S(1)}, f32[4,32,768]{2,1,0:T(8,128)S(1)}, u32[]{:S(2)}, u32[]{:S(2)}) collective-permute-start(f32[4,32,768]{2,1,0:T(8,128)S(1)} %get-tuple-element.31), channel_id=1, source_target_pairs={{0,8},{8,0},{16,24},{24,16},{1,9},{9,1},{17,25},{25,17},{2,10},{10... | collective-permute-start | bytes 1179656 | tf_op jit(solution)/shard_map/ppermute | solution.py:38
  12.9 11.1 %collective-permute-start.3 = (f32[4,32,768]{2,1,0:T(8,128)S(1)}, f32[4,32,768]{2,1,0:T(8,128)S(1)}, u32[]{:S(2)}, u32[]{:S(2)}) collective-permute-start(f32[4,32,768]{2,1,0:T(8,128)S(1)} %get-tuple-element.32), channel_id=1, source_target_pairs={{8,16},{16,8},{9,17},{17,9},{10,18},{18,10},{11,19},{19,11},{12,20... | collective-permute-start | bytes 1179656 | tf_op jit(solution)/shard_map/ppermute | solution.py:38
  29.7 5.5 %collective-permute-start.5 = (f32[14,8,128]{2,1,0:T(8,128)S(1)}, f32[14,8,128]{2,1,0:T(8,128)S(1)}, u32[]{:S(2)}, u32[]{:S(2)}) collective-permute-start(f32[14,8,128]{2,1,0:T(8,128)S(1)} %get-tuple-element.34.coarse), channel_id=1, source_target_pairs={{8,16},{16,8},{9,17},{17,9},{10,18},{18,10},{11,19},{19,11},{12,20... | collective-permute-start | bytes 172040 | tf_op jit(solution)/shard_map/ppermute | solution.py:38
  32.3 2.9 %collective-permute-start.4 = (f32[14,8,128]{2,1,0:T(8,128)S(1)}, f32[14,8,128]{2,1,0:T(8,128)S(1)}, u32[]{:S(2)}, u32[]{:S(2)}) collective-permute-start(f32[14,8,128]{2,1,0:T(8,128)S(1)} %get-tuple-element.34.coarse), channel_id=1, source_target_pairs={{0,8},{8,0},{16,24},{24,16},{1,9},{9,1},{17,25},{25,17},{2,10},{10... | collective-permute-start | bytes 172040 | tf_op jit(solution)/shard_map/ppermute | solution.py:38

commit v6 on v5

--- a/solution.py
+++ b/solution.py
@@ -218,8 +218,8 @@
 
 
 class Level:
-    def __init__(self, matrix, names_at, inverse, spill):
-        self.matrix, self.names_at, self.inverse, self.spill = matrix, names_at, inverse, spill
+    def __init__(self, matrix, names_at, inverse):
+        self.matrix, self.names_at, self.inverse = matrix, names_at, inverse
         self.count = matrix.shape[1]
 
     def entry(self, name, m, k, high):
@@ -345,11 +345,8 @@
 
 
 def over_columns(count, column):
-    if count > 2:
-        pl.loop(0, count)(column)
-    else:
-        for k in range(count):
-            column(k)
+    for k in range(count):
+        column(k)
 
 
 def cut(value, height):
@@ -357,12 +354,12 @@
 
 
 def apply(level, x, source, out, residual, tall_cells=None, tall_nodes=None):
-    count, spill = level.count, level.spill
+    count = level.count
     side = x.shape[3]
     cells = [side if tall_cells is None or m in tall_cells else side // 2 for m in range(count)]
     nodes = [side if tall_nodes is None or m in tall_nodes else side // 2 for m in range(count)]
     held = [max(cells[m], cells[m - 1]) if m else side for m in range(count)]
-    spill[...] = jnp.zeros_like(spill)
+    passed_right = {}
 
     def column(k):
         sums, steps = [], []
@@ -394,9 +391,11 @@
                 at = 2 * component
                 even = cut(above[at], high) - cut(own[m][at], high)
                 odd = cut(above[at + 1], high) + cut(own[m][at + 1], high)
-                left = spill[component, m, :high, :]
-                spill[component, m, :high, :] = even + odd
-                rest = source[component, m, k, :high, :] - ((even - odd) + left)
+                force = even - odd
+                if k:
+                    force = force + passed_right[component, m]
+                passed_right[component, m] = even + odd
+                rest = source[component, m, k, :high, :] - force
                 if not residual:
                     rest = x[component, m, k, :high, :] + inverse_of(level, component, m, k, high) * rest
                 out[component, m, k, :high, :] = rest
@@ -405,7 +404,7 @@
     for component in (0, 1):
         for m in range(count):
             high = nodes[m]
-            left = from_before(spill[component, m, :high, :], 1)
+            left = from_before(passed_right[component, m], 1)
             if not residual:
                 left = left * inverse_of(level, component, m, 0, high)
             out[component, m, 0, :high, :] = out[component, m, 0, :high, :] - left
@@ -430,7 +429,13 @@
                 target[component, m, k] = lines[2 * m] + 0.5 * (lines[2 * m + 1] + before)
 
 
-def prolong(coarse, before, x, count):
+def prolong(coarse, before, x, count, tall=None):
+    side = x.shape[3]
+
+    def add(component, m, k, value):
+        high = side if tall is None or m in tall else side // 2
+        x[component, m, k, :high, :] = before[component, m, k, :high, :] + cut(value, high)
+
     half = count // 2
     for component in (0, 1):
         planes = {(m, k): coarse(component, m, k) for m in range(half) for k in range(half)}
@@ -441,10 +446,10 @@
         for m in range(half):
             for k in range(half):
                 a, b, c, d = planes[m, k], planes[m + 1, k], planes[m, k + 1], planes[m + 1, k + 1]
-                x[component, 2 * m, 2 * k] = before[component, 2 * m, 2 * k] + a
-                x[component, 2 * m + 1, 2 * k] = before[component, 2 * m + 1, 2 * k] + 0.5 * (a + b)
-                x[component, 2 * m, 2 * k + 1] = before[component, 2 * m, 2 * k + 1] + 0.5 * (a + c)
-                x[component, 2 * m + 1, 2 * k + 1] = before[component, 2 * m + 1, 2 * k + 1] + 0.25 * ((a + b) + (c + d))
+                add(component, 2 * m, 2 * k, a)
+                add(component, 2 * m + 1, 2 * k, 0.5 * (a + b))
+                add(component, 2 * m, 2 * k + 1, 0.5 * (a + c))
+                add(component, 2 * m + 1, 2 * k + 1, 0.25 * ((a + b) + (c + d)))
 
 
 def haar(level, names_at, m, k):
@@ -556,12 +561,9 @@
     )
 
 
-def three_parts(value):
+def two_parts(value):
     high = value.astype(BF16)
-    rest = value - high.astype(F32)
-    middle = rest.astype(BF16)
-    low = (rest - middle.astype(F32)).astype(BF16)
-    return high, middle, low
+    return high, (value - high.astype(F32)).astype(BF16)
 
 
 def turned(value, by):
@@ -595,15 +597,15 @@
         for pair in range(GROUP // 2):
             for tile in range(count):
                 lines = [tiles[field, tile, pl.ds(2 * pair + h, block, stride=GROUP), :] for h in (0, 1)]
-                for part, split in enumerate(three_parts(jnp.concatenate(lines, axis=0))):
-                    line = (field * 3 + part) * rows + pair * 2 * block
+                for part, split in enumerate(two_parts(jnp.concatenate(lines, axis=0))):
+                    line = (field * 2 + part) * rows + pair * 2 * block
                     stacked[line : line + 2 * block, tile * LANES : (tile + 1) * LANES] = split
     for field in range(fields):
         pieces = []
         for piece in range(count * LANES // WIDE):
-            left = stacked[field * 3 * rows : (field + 1) * 3 * rows, piece * WIDE : (piece + 1) * WIDE]
+            left = stacked[field * 2 * rows : (field + 1) * 2 * rows, piece * WIDE : (piece + 1) * WIDE]
             product = jnp.dot(left, spread[...], preferred_element_type=F32)
-            pieces.append(product[:rows] + product[rows : 2 * rows] + product[2 * rows :])
+            pieces.append(product[:rows] + product[rows:])
         for m in range(GROUP):
             for k in range(GROUP):
                 half, slot = k * SPAN // LANES, k * SPAN % LANES
@@ -632,7 +634,7 @@
 def spread_scratch(rows, wide):
     return [
         pltpu.VMEM((4, wide // LANES, rows, LANES), F32),
-        pltpu.VMEM((12 * rows, wide), BF16),
+        pltpu.VMEM((8 * rows, wide), BF16),
         pltpu.VMEM((WIDE, WIDE), BF16),
     ]
 
@@ -647,7 +649,7 @@
         out_specs=vmem,
         scratch_shapes=spread_scratch(rows, wide),
         compiler_params=pltpu.CompilerParams(vmem_limit_bytes=12 * 1024 * 1024),
-        cost_estimate=pl.CostEstimate(flops=24 * rows * wide * WIDE, bytes_accessed=0, transcendentals=0),
+        cost_estimate=pl.CostEstimate(flops=16 * rows * wide * WIDE, bytes_accessed=0, transcendentals=0),
         name="spread_own",
     )(fields, even_side, odd_side)
 
@@ -655,7 +657,7 @@
 def down_kernel(
     own, even_rows, odd_rows, factor,
     matrix0, inverse0, source0, x0, matrix1, inverse1, source1, x1, matrix2, inverse2, source2, x2, coarsest,
-    tiles, stacked, spread, other0, other1, other2, spill0, spill1, spill2, matrix3,
+    tiles, stacked, spread, other0, other1, other2, matrix3,
     *, rows, cols, gx, gy,
 ):
     block = rows // GROUP
@@ -674,23 +676,21 @@
 
     def write(field, m, k, plane):
         if field < 2:
-            matrix0[field, m, k, :block, :] = own[field, m, k] * (0.25 * factor[m, k, :block, :])
-            matrix0[field, m, k, block:, :] = plane * (0.25 * factor[m, k, block:, :])
+            spans = (slice(0, block), slice(block, side))
+            for span, value in zip(spans, (own[field, m, k], plane)):
+                value = value * (0.25 * factor[m, k, span, :])
+                matrix0[field, m, k, span, :] = value
+                if field == 1:
+                    matrix0[2, m, k, span, :] = matrix0[0, m, k, span, :] * (1.0 / 3.0) + value
         else:
             source0[field - 2, m, k, :block, :] = own[field, m, k]
             source0[field - 2, m, k, block:, :] = plane
 
     spread_fields(load, write, tiles, stacked, spread)
 
-    def mix(k):
-        for m in range(GROUP):
-            matrix0[2, m, k] = matrix0[0, m, k] * (1.0 / 3.0) + matrix0[1, m, k]
-
-    over_columns(GROUP, mix)
-
-    level0 = FineLevel(matrix0, {}, inverse0, spill0)
-    level1 = Level(matrix1, FIRST_AT, inverse1, spill1)
-    level2 = Level(matrix2, FULL_AT, inverse2, spill2)
+    level0 = FineLevel(matrix0, {}, inverse0)
+    level1 = Level(matrix1, FIRST_AT, inverse1)
+    level2 = Level(matrix2, FULL_AT, inverse2)
 
     coarsen_fine(level0, level1)
 
@@ -736,7 +736,7 @@
     coarse, coarse_even, coarse_odd,
     matrix0, inverse0, source0, x0_in, matrix1, inverse1, source1, x1_in, matrix2, inverse2, source2, x2_in,
     displacement,
-    x0, other0, x1, other1, x2, other2, spill0, spill1, spill2, spill3, matrix3, inverse3, source3, x3, other3,
+    x0, other0, x1, other1, x2, other2, matrix3, inverse3, source3, x3,
     stacked, gathered, tiles,
     *, rows, cols, gx, gy,
 ):
@@ -748,26 +748,23 @@
                 matrix3[at, 0, 0, lines, :] = part[at]
             else:
                 source3[at - len(FULL), 0, 0, lines, :] = part[at]
-    level3 = Level(matrix3, FULL_AT, inverse3, spill3)
+    level3 = Level(matrix3, FULL_AT, inverse3)
     level3.make_inverse(*edge_masks((3 * block, LANES), block, rows, cols, gx * rows, gy * cols))
-    start(level3, x3, source3)
-    now, then = x3, other3
-    for _ in range(COARSE_SWEEPS - 1):
-        apply(level3, now, source3, then, residual=False)
-        now, then = then, now
+    relax(level3, source3, x3)
+    now = x3
     coarse_plane = functools.partial(cut_plane, now, block)
 
-    level0 = FineLevel(matrix0, {}, inverse0, spill0)
-    level1 = Level(matrix1, FIRST_AT, inverse1, spill1)
-    level2 = Level(matrix2, FULL_AT, inverse2, spill2)
+    level0 = FineLevel(matrix0, {}, inverse0)
+    level1 = Level(matrix1, FIRST_AT, inverse1)
+    level2 = Level(matrix2, FULL_AT, inverse2)
     for level, source, before, x, other in (
         (level2, source2, x2_in, x2, other2),
         (level1, source1, x1_in, x1, other1),
         (level0, source0, x0_in, x0, other0),
     ):
-        prolong(coarse_plane, before, x, level.count)
+        last = level.count - 1
+        prolong(coarse_plane, before, x, level.count, {0, 1, last - 1, last} if level is level0 else None)
         close_columns(level, x)
-        last = level.count - 1
         if level is level0:
             apply(level, x, source, other, False, {0, last - 1, last}, {0, last})
             apply(level, other, source, x, False, {last}, set())
@@ -796,7 +793,7 @@
                         part = turned(values[half * slots + slot], (slot - piece) * SPAN)
                         value = part if value is None else jnp.where(lane < (slot + 1) * SPAN, part, value)
                     lanes = slice(piece * WIDE + half * LANES, piece * WIDE + (half + 1) * LANES)
-                    for part, split in enumerate(three_parts(value)):
+                    for part, split in enumerate(two_parts(value)):
                         line = part * 2 * rows + component * rows + pair * 2 * block
                         stacked[line : line + 2 * block, lanes] = split
     pieces = []
@@ -804,7 +801,7 @@
         product = jnp.dot(
             stacked[:, piece * WIDE : (piece + 1) * WIDE], gathered[...], preferred_element_type=F32
         )
-        pieces.append(product[: 2 * rows] + product[2 * rows : 4 * rows] + product[4 * rows :])
+        pieces.append(product[: 2 * rows] + product[2 * rows :])
     for component in (0, 1):
         for tile in range(cols // LANES):
             lanes = slice(tile * LANES, (tile + 1) * LANES)
@@ -814,6 +811,33 @@
                     line : line + block, tile * LANES % WIDE : tile * LANES % WIDE + LANES
                 ]
             displacement[component, :, lanes] = tiles[component, tile]
+
+
+def relax(level, source, out):
+    right = [source[component, 0, 0] for component in (0, 1)]
+    inverse = [inverse_of(level, component, 0, 0, out.shape[3]) for component in (0, 1)]
+    x = [right[c] * inverse[c] for c in (0, 1)]
+    for _ in range(COARSE_SWEEPS - 1):
+        after = [from_after(value, 1) for value in x]
+        sums = [x[c] + after[c] for c in (0, 1)]
+        steps = [after[c] - x[c] for c in (0, 1)]
+        sum1, step1 = [[from_after(value, 0) for value in pair] for pair in (sums, steps)]
+        modes = (
+            sum1[0] - sums[0],
+            steps[1] + step1[1],
+            (steps[0] + step1[0]) + (sum1[1] - sums[1]),
+            step1[0] - steps[0],
+            step1[1] - steps[1],
+        )
+        first, second, third, bend_row, bend_col = level.stress(0, 0, modes)
+        own = (first, third - bend_row, third, second - bend_col)
+        above = [from_before(v, 0) for v in (first, third + bend_row, third, second + bend_col)]
+        for c in (0, 1):
+            even, odd = above[2 * c] - own[2 * c], above[2 * c + 1] + own[2 * c + 1]
+            rest = right[c] - ((even - odd) + from_before(even + odd, 1))
+            x[c] = x[c] + inverse[c] * rest
+    for component in (0, 1):
+        out[component, 0, 0] = x[component]
 
 
 def cut_plane(x, block, component, m, k):
@@ -867,7 +891,6 @@
         out_specs=[vmem] * (len(state) + 1),
         scratch_shapes=spread_scratch(2 * HALO_ROWS, wide)
         + [pltpu.VMEM(planes(2, count, 1), F32) for count in counts]
-        + [pltpu.VMEM((2, count, side, LANES), F32) for count in counts]
         + [pltpu.VMEM((held, side, LANES), F32)],
         compiler_params=pltpu.CompilerParams(vmem_limit_bytes=VMEM_LIMIT),
         name="descent",
@@ -885,15 +908,12 @@
             for count in counts
             for shape in (pltpu.VMEM(planes(2, count, 1), F32),) * 2
         ]
-        + [pltpu.VMEM((2, count, side, LANES), F32) for count in counts]
         + [
-            pltpu.VMEM((2, 1, lines, LANES), F32),
             pltpu.VMEM(planes(len(FULL), 1, 0, lines), F32),
             pltpu.VMEM(planes(2, 1, 0, lines), F32),
             pltpu.VMEM(planes(2, 1, 0, lines), F32),
-            pltpu.VMEM(planes(2, 1, 1, lines), F32),
-            pltpu.VMEM(planes(2, 1, 1, lines), F32),
-            pltpu.VMEM((6 * rows, cols), BF16),
+            pltpu.VMEM(planes(2, 1, 0, lines), F32),
+            pltpu.VMEM((4 * rows, cols), BF16),
             pltpu.VMEM((WIDE, WIDE), BF16),
             pltpu.VMEM((2, cols // LANES, rows, LANES), F32),
         ],

time: 40.4 us -> 39.1 us (0.968)
  Pallas kernels: 17.5 us -> 16.2 us
    pallas_call x1, Pallas kernels: 5.57 us -> 4.92 us  [body(): pl.pallas_call(functools.partial(down_kernel, rows=rows, cols=cols, gx=gx...]
    pallas_call x1, Pallas kernels: 4.98 us -> 4.38 us  [body(): pl.pallas_call(functools.partial(up_kernel, rows=rows, cols=cols, gx=gx,...]
where the time goes in v6:
time: 39.1 us; the launch traced here: 38.9 us
  starting transfers between devices  17.5 us (45%)
  Pallas kernels  16.2 us (41%)
  waiting for transfers between devices  5.07 us (13%)
    ppermute x6, starting transfers between devices, swapped(): return lax.ppermute(array, axis, pairs)  9.18 us
    all_to_all x1, starting transfers between devices, body(): words = lax.all_to_all(words, ('gx', 'gy'), 0, 0, tiled=True)  8.33 us
    pallas_call x1, Pallas kernels, body(): pl.pallas_call(functools.partial(down_kernel, rows=rows, cols=cols, gx=gx...  4.92 us
    pallas_call x1, Pallas kernels, body(): pl.pallas_call(functools.partial(up_kernel, rows=rows, cols=cols, gx=gx,...  4.38 us
    pallas_call x1, Pallas kernels, yield_factor(): pl.pallas_call(functools.partial(factor_kernel, rows=rows, cols=cols, gy=...  4.37 us
    ppermute x6, waiting for transfers between devices, swapped(): return lax.ppermute(array, axis, pairs)  2.82 us
    all_to_all x1, waiting for transfers between devices, body(): words = lax.all_to_all(words, ('gx', 'gy'), 0, 0, tiled=True)  2.25 us
    pallas_call x1, Pallas kernels, pack(): pl.pallas_call(functools.partial(pack_kernel, cells=rows * cols), out_sha...  1.41 us
  transfers between devices with their start and end apart: 7, of which 2 were waited for; matrix products, arithmetic and copies ran while one was open for 0% of the time, Pallas kernels for 14%

profile of v6, /device:TPU:1, one launch (start us, length us, event | category | flops | bytes accessed | tf_op | source)
XLA Modules:
  0.0 38.9 jit_solution(6166718377862583689)
XLA Ops:
  0.0 1.4 %pack.1 = (f32[4,64,512]{2,1,0:T(8,128)S(1)}, f32[4,64,128]{2,1,0:T(8,128)S(1)}, f32[4,64,128]{2,1,0:T(8,128)S(1)}, s32[32,1,512]{2,1,0:T(1,128)}) custom-call(f32[64,512]{1,0:T(8,128)} %first_lame.1, f32[64,512]{1,0:T(8,128)} %shear_modulus.1, f32[2,64,512]{2,1,0:T(8,128)} %applied_load.1, s32[1,512]{1,0:T(1,128)} %bitcast.3, s32[1,512]{1,0:T(1,128)} %bitcast.4, ...), custom_call_target="tpu_custom_call" | custom-call | tf_op jit(solution)/shard_map/pack/pallas_call | solution.py:176
  1.4 2.1 %collective-permute-start = (f32[4,64,128]{2,1,0:T(8,128)S(1)}, f32[4,64,128]{2,1,0:T(8,128)S(1)}, u32[]{:S(2)}, u32[]{:S(2)}) collective-permute-start(f32[4,64,128]{2,1,0:T(8,128)S(1)} %get-tuple-element.28), channel_id=1, source_target_pairs={{0,1},{1,0},{2,3},{3,2},{4,5},{5,4},{6,7},{7,6},{8,9},{9,8},{10,11... | collective-permute-start | bytes 393224 | tf_op jit(solution)/shard_map/ppermute | solution.py:38
  3.5 0.7 %collective-permute-start.1 = (f32[4,64,128]{2,1,0:T(8,128)S(1)}, f32[4,64,128]{2,1,0:T(8,128)S(1)}, u32[]{:S(2)}, u32[]{:S(2)}) collective-permute-start(f32[4,64,128]{2,1,0:T(8,128)S(1)} %get-tuple-element.29), channel_id=1, source_target_pairs={{1,2},{2,1},{3,4},{4,3},{5,6},{6,5},{9,10},{10,9},{11,12},{12,11},... | collective-permute-start | bytes 393224 | tf_op jit(solution)/shard_map/ppermute | solution.py:38
  4.2 8.3 %all-to-all-start = ((s32[32,1,512]{2,1,0:T(1,128)}), s32[32,1,512]{2,1,0:T(1,128)S(1)}, u32[]{:S(2)}, u32[]{:S(2)}) async-start(s32[32,1,512]{2,1,0:T(1,128)} %get-tuple-element.26), calls=%async_computation | async-start | bytes 131072 | tf_op jit(solution)/shard_map/all_to_all | solution.py:866
  12.5 0.0 collective-permute-done.even_side
  12.5 0.0 collective-permute-done.1.odd_side
  12.5 0.1 pack_rows.1
  12.6 0.3 collective-permute-start.2
  12.9 3.4 %collective-permute-start.3 = (f32[4,32,768]{2,1,0:T(8,128)S(1)}, f32[4,32,768]{2,1,0:T(8,128)S(1)}, u32[]{:S(2)}, u32[]{:S(2)}) collective-permute-start(f32[4,32,768]{2,1,0:T(8,128)S(1)} %get-tuple-element.32), channel_id=1, source_target_pairs={{8,16},{16,8},{9,17},{17,9},{10,18},{18,10},{11,19},{19,11},{12,20... | collective-permute-start | bytes 1179656 | tf_op jit(solution)/shard_map/ppermute | solution.py:38
  16.4 1.0 %spread_own.1.own = f32[4,8,8,8,128]{4,3,2,1,0:T(8,128)S(1)} custom-call(f32[4,64,512]{2,1,0:T(8,128)S(1)} %get-tuple-element.27.fields, f32[4,64,128]{2,1,0:T(8,128)S(1)} %collective-permute-done.even_side, f32[4,64,128]{2,1,0:T(8,128)S(1)} %collective-permute-done.1.odd_side), custom_call_target="tpu_custom_call" | custom-call | flops 201326592 | tf_op jit(solution)/shard_map/spread_own/pallas_call | solution.py:645
  17.4 2.2 %all-to-all-done.words = s32[32,1,512]{2,1,0:T(1,128)S(1)} async-done(((s32[32,1,512]{2,1,0:T(1,128)}), s32[32,1,512]{2,1,0:T(1,128)S(1)}, u32[]{:S(2)}, u32[]{:S(2)}) %all-to-all-start) | async-done | bytes 65568 | tf_op jit(solution)/shard_map/all_to_all | solution.py:866
  19.7 4.4 %yield_factor.1.factor = f32[8,8,16,128]{3,2,1,0:T(8,128)S(1)} custom-call(s32[32,1,512]{2,1,0:T(1,128)S(1)} %all-to-all-done.words), custom_call_target="tpu_custom_call" | custom-call | flops 3221225472 | bytes 65536 | tf_op jit(solution)/shard_map/yield_factor/pallas_call | solution.py:116
  24.0 0.0 collective-permute-done.2.even_rows
  24.1 0.0 collective-permute-done.3.odd_rows
  24.1 4.9 %descent.1 = (f32[3,8,8,16,128]{4,3,2,1,0:T(8,128)S(1)}, f32[1,8,8,16,128]{4,3,2,1,0:T(8,128)S(1)}, f32[2,8,8,16,128]{4,3,2,1,0:T(8,128)S(1)}, f32[2,8,9,16,128]...) custom-call(f32[4,8,8,8,128]{4,3,2,1,0:T(8,128)S(1)} %spread_own.1.o, ...), custom_call_target="tpu_custom_call" | custom-call | tf_op jit(solution)/shard_map/descent/pallas_call | solution.py:886
  29.0 2.6 %collective-permute-start.5 = (f32[14,8,128]{2,1,0:T(8,128)S(1)}, f32[14,8,128]{2,1,0:T(8,128)S(1)}, u32[]{:S(2)}, u32[]{:S(2)}) collective-permute-start(f32[14,8,128]{2,1,0:T(8,128)S(1)} %get-tuple-element.34.coarse), channel_id=1, source_target_pairs={{8,16},{16,8},{9,17},{17,9},{10,18},{18,10},{11,19},{19,11},{12,20... | collective-permute-start | bytes 172040 | tf_op jit(solution)/shard_map/ppermute | solution.py:38
  31.6 0.1 collective-permute-start.4
  31.7 2.8 %collective-permute-done.5.coarse_odd = f32[14,8,128]{2,1,0:T(8,128)S(1)} collective-permute-done((f32[14,8,128]{2,1,0:T(8,128)S(1)}, f32[14,8,128]{2,1,0:T(8,128)S(1)}, u32[]{:S(2)}, u32[]{:S(2)}) %collective-permute-start.5) | collective-permute-done | bytes 57376 | tf_op jit(solution)/shard_map/ppermute | solution.py:38
  34.5 0.0 collective-permute-done.4.coarse_even
  34.5 4.4 %ascent.1 = f32[2,64,512]{2,1,0:T(8,128)} custom-call(f32[14,8,128]{2,1,0:T(8,128)S(1)} %get-tuple-element.34.coarse, f32[14,8,128]{2,1,0:T(8,128)S(1)} %collective-permute-done.4.coarse_even, f32[14,8,128]{2,1,0:T(8,128)S(1)} %collective-permute-done.5.coarse_odd, f32[3,8,8,16,128]{4,3,2,1,0:T(8,128)S(1)} %get-tuple-element.35.matrix0, ...), custom_call_target="tpu_custom_call" | custom-call | tf_op jit(solution)/shard_map/ascent/pallas_call | solution.py:901
Async XLA Ops:
  1.4 11.1 %collective-permute-start = (f32[4,64,128]{2,1,0:T(8,128)S(1)}, f32[4,64,128]{2,1,0:T(8,128)S(1)}, u32[]{:S(2)}, u32[]{:S(2)}) collective-permute-start(f32[4,64,128]{2,1,0:T(8,128)S(1)} %get-tuple-element.28), channel_id=1, source_target_pairs={{0,1},{1,0},{2,3},{3,2},{4,5},{5,4},{6,7},{7,6},{8,9},{9,8},{10,11... | collective-permute-start | bytes 393224 | tf_op jit(solution)/shard_map/ppermute | solution.py:38
  3.5 9.0 %collective-permute-start.1 = (f32[4,64,128]{2,1,0:T(8,128)S(1)}, f32[4,64,128]{2,1,0:T(8,128)S(1)}, u32[]{:S(2)}, u32[]{:S(2)}) collective-permute-start(f32[4,64,128]{2,1,0:T(8,128)S(1)} %get-tuple-element.29), channel_id=1, source_target_pairs={{1,2},{2,1},{3,4},{4,3},{5,6},{6,5},{9,10},{10,9},{11,12},{12,11},... | collective-permute-start | bytes 393224 | tf_op jit(solution)/shard_map/ppermute | solution.py:38
  4.2 15.5 %all-to-all-start = ((s32[32,1,512]{2,1,0:T(1,128)}), s32[32,1,512]{2,1,0:T(1,128)S(1)}, u32[]{:S(2)}, u32[]{:S(2)}) async-start(s32[32,1,512]{2,1,0:T(1,128)} %get-tuple-element.26), calls=%async_computation | async-start | bytes 131072 | tf_op jit(solution)/shard_map/all_to_all | solution.py:866
  12.6 11.4 %collective-permute-start.2 = (f32[4,32,768]{2,1,0:T(8,128)S(1)}, f32[4,32,768]{2,1,0:T(8,128)S(1)}, u32[]{:S(2)}, u32[]{:S(2)}) collective-permute-start(f32[4,32,768]{2,1,0:T(8,128)S(1)} %get-tuple-element.31), channel_id=1, source_target_pairs={{0,8},{8,0},{16,24},{24,16},{1,9},{9,1},{17,25},{25,17},{2,10},{10... | collective-permute-start | bytes 1179656 | tf_op jit(solution)/shard_map/ppermute | solution.py:38
  12.9 11.1 %collective-permute-start.3 = (f32[4,32,768]{2,1,0:T(8,128)S(1)}, f32[4,32,768]{2,1,0:T(8,128)S(1)}, u32[]{:S(2)}, u32[]{:S(2)}) collective-permute-start(f32[4,32,768]{2,1,0:T(8,128)S(1)} %get-tuple-element.32), channel_id=1, source_target_pairs={{8,16},{16,8},{9,17},{17,9},{10,18},{18,10},{11,19},{19,11},{12,20... | collective-permute-start | bytes 1179656 | tf_op jit(solution)/shard_map/ppermute | solution.py:38
  29.0 5.5 %collective-permute-start.5 = (f32[14,8,128]{2,1,0:T(8,128)S(1)}, f32[14,8,128]{2,1,0:T(8,128)S(1)}, u32[]{:S(2)}, u32[]{:S(2)}) collective-permute-start(f32[14,8,128]{2,1,0:T(8,128)S(1)} %get-tuple-element.34.coarse), channel_id=1, source_target_pairs={{8,16},{16,8},{9,17},{17,9},{10,18},{18,10},{11,19},{19,11},{12,20... | collective-permute-start | bytes 172040 | tf_op jit(solution)/shard_map/ppermute | solution.py:38
  31.6 2.9 %collective-permute-start.4 = (f32[14,8,128]{2,1,0:T(8,128)S(1)}, f32[14,8,128]{2,1,0:T(8,128)S(1)}, u32[]{:S(2)}, u32[]{:S(2)}) collective-permute-start(f32[14,8,128]{2,1,0:T(8,128)S(1)} %get-tuple-element.34.coarse), channel_id=1, source_target_pairs={{0,8},{8,0},{16,24},{24,16},{1,9},{9,1},{17,25},{25,17},{2,10},{10... | collective-permute-start | bytes 172040 | tf_op jit(solution)/shard_map/ppermute | solution.py:38

commit v7 on v6

--- a/solution.py
+++ b/solution.py
@@ -300,25 +300,22 @@
     def make_inverse(self, row_ok, col_ok):
         count = self.count
 
-        @pl.loop(0, count)
-        def _(k):
+        def pair_sums(k):
             parts = [self.matrix[2, m, k] for m in range(count)]
+            return [parts[m] + (parts[m - 1] if m else from_before(parts[count - 1], 0)) for m in range(count)]
+
+        left = [from_before(value, 1) for value in pair_sums(count - 1)]
+        for k in range(count):
+            here = pair_sums(k)
             for m in range(count):
-                above = parts[m - 1] if m else from_before(parts[count - 1], 0)
-                self.inverse[0, m, k] = parts[m] + above
-
-        for m in range(count):
-            left = from_before(self.inverse[0, m, count - 1], 1)
-            for k in range(count):
-                here = self.inverse[0, m, k]
-                diagonal = 4.0 * (here + left)
-                left = here
+                diagonal = 4.0 * (here[m] + left[m])
                 value = jnp.where(diagonal > 0.0, 0.5 / diagonal, 0.0)
                 if m == 0:
                     value = value * row_ok
                 if k == 0:
                     value = value * col_ok
                 self.inverse[0, m, k] = value
+            left = here
 
 
 def inverse_of(level, component, m, k, high):

time: 39.1 us -> 38.8 us (level)
  no operation moved by 1% of the time
where the time goes in v7:
time: 38.8 us; the launch traced here: 38.6 us
  starting transfers between devices  17.5 us (45%)
  Pallas kernels  15.9 us (41%)
  waiting for transfers between devices  5.07 us (13%)
    ppermute x6, starting transfers between devices, swapped(): return lax.ppermute(array, axis, pairs)  9.18 us
    all_to_all x1, starting transfers between devices, body(): words = lax.all_to_all(words, ('gx', 'gy'), 0, 0, tiled=True)  8.33 us
    pallas_call x1, Pallas kernels, body(): pl.pallas_call(functools.partial(down_kernel, rows=rows, cols=cols, gx=gx...  4.63 us
    pallas_call x1, Pallas kernels, body(): pl.pallas_call(functools.partial(up_kernel, rows=rows, cols=cols, gx=gx,...  4.38 us
    pallas_call x1, Pallas kernels, yield_factor(): pl.pallas_call(functools.partial(factor_kernel, rows=rows, cols=cols, gy=...  4.37 us
    ppermute x6, waiting for transfers between devices, swapped(): return lax.ppermute(array, axis, pairs)  2.82 us
    all_to_all x1, waiting for transfers between devices, body(): words = lax.all_to_all(words, ('gx', 'gy'), 0, 0, tiled=True)  2.25 us
    pallas_call x1, Pallas kernels, pack(): pl.pallas_call(functools.partial(pack_kernel, cells=rows * cols), out_sha...  1.41 us
  transfers between devices with their start and end apart: 7, of which 2 were waited for; matrix products, arithmetic and copies ran while one was open for 0% of the time, Pallas kernels for 14%

profile of v7, /device:TPU:1, one launch (start us, length us, event | category | flops | bytes accessed | tf_op | source)
XLA Modules:
  0.0 38.6 jit_solution(4014747065392517721)
XLA Ops:
  0.0 1.4 %pack.1 = (f32[4,64,512]{2,1,0:T(8,128)S(1)}, f32[4,64,128]{2,1,0:T(8,128)S(1)}, f32[4,64,128]{2,1,0:T(8,128)S(1)}, s32[32,1,512]{2,1,0:T(1,128)}) custom-call(f32[64,512]{1,0:T(8,128)} %first_lame.1, f32[64,512]{1,0:T(8,128)} %shear_modulus.1, f32[2,64,512]{2,1,0:T(8,128)} %applied_load.1, s32[1,512]{1,0:T(1,128)} %bitcast.3, s32[1,512]{1,0:T(1,128)} %bitcast.4, ...), custom_call_target="tpu_custom_call" | custom-call | tf_op jit(solution)/shard_map/pack/pallas_call | solution.py:176
  1.4 2.1 %collective-permute-start = (f32[4,64,128]{2,1,0:T(8,128)S(1)}, f32[4,64,128]{2,1,0:T(8,128)S(1)}, u32[]{:S(2)}, u32[]{:S(2)}) collective-permute-start(f32[4,64,128]{2,1,0:T(8,128)S(1)} %get-tuple-element.28), channel_id=1, source_target_pairs={{0,1},{1,0},{2,3},{3,2},{4,5},{5,4},{6,7},{7,6},{8,9},{9,8},{10,11... | collective-permute-start | bytes 393224 | tf_op jit(solution)/shard_map/ppermute | solution.py:38
  3.5 0.7 %collective-permute-start.1 = (f32[4,64,128]{2,1,0:T(8,128)S(1)}, f32[4,64,128]{2,1,0:T(8,128)S(1)}, u32[]{:S(2)}, u32[]{:S(2)}) collective-permute-start(f32[4,64,128]{2,1,0:T(8,128)S(1)} %get-tuple-element.29), channel_id=1, source_target_pairs={{1,2},{2,1},{3,4},{4,3},{5,6},{6,5},{9,10},{10,9},{11,12},{12,11},... | collective-permute-start | bytes 393224 | tf_op jit(solution)/shard_map/ppermute | solution.py:38
  4.2 8.3 %all-to-all-start = ((s32[32,1,512]{2,1,0:T(1,128)}), s32[32,1,512]{2,1,0:T(1,128)S(1)}, u32[]{:S(2)}, u32[]{:S(2)}) async-start(s32[32,1,512]{2,1,0:T(1,128)} %get-tuple-element.26), calls=%async_computation | async-start | bytes 131072 | tf_op jit(solution)/shard_map/all_to_all | solution.py:863
  12.5 0.0 collective-permute-done.even_side
  12.5 0.0 collective-permute-done.1.odd_side
  12.5 0.1 pack_rows.1
  12.6 0.3 collective-permute-start.2
  12.9 3.4 %collective-permute-start.3 = (f32[4,32,768]{2,1,0:T(8,128)S(1)}, f32[4,32,768]{2,1,0:T(8,128)S(1)}, u32[]{:S(2)}, u32[]{:S(2)}) collective-permute-start(f32[4,32,768]{2,1,0:T(8,128)S(1)} %get-tuple-element.32), channel_id=1, source_target_pairs={{8,16},{16,8},{9,17},{17,9},{10,18},{18,10},{11,19},{19,11},{12,20... | collective-permute-start | bytes 1179656 | tf_op jit(solution)/shard_map/ppermute | solution.py:38
  16.4 1.0 %spread_own.1.own = f32[4,8,8,8,128]{4,3,2,1,0:T(8,128)S(1)} custom-call(f32[4,64,512]{2,1,0:T(8,128)S(1)} %get-tuple-element.27.fields, f32[4,64,128]{2,1,0:T(8,128)S(1)} %collective-permute-done.even_side, f32[4,64,128]{2,1,0:T(8,128)S(1)} %collective-permute-done.1.odd_side), custom_call_target="tpu_custom_call" | custom-call | flops 201326592 | tf_op jit(solution)/shard_map/spread_own/pallas_call | solution.py:642
  17.4 2.2 %all-to-all-done.words = s32[32,1,512]{2,1,0:T(1,128)S(1)} async-done(((s32[32,1,512]{2,1,0:T(1,128)}), s32[32,1,512]{2,1,0:T(1,128)S(1)}, u32[]{:S(2)}, u32[]{:S(2)}) %all-to-all-start) | async-done | bytes 65568 | tf_op jit(solution)/shard_map/all_to_all | solution.py:863
  19.7 4.4 %yield_factor.1.factor = f32[8,8,16,128]{3,2,1,0:T(8,128)S(1)} custom-call(s32[32,1,512]{2,1,0:T(1,128)S(1)} %all-to-all-done.words), custom_call_target="tpu_custom_call" | custom-call | flops 3221225472 | bytes 65536 | tf_op jit(solution)/shard_map/yield_factor/pallas_call | solution.py:116
  24.0 0.0 collective-permute-done.2.even_rows
  24.1 0.0 collective-permute-done.3.odd_rows
  24.1 4.6 %descent.1 = (f32[3,8,8,16,128]{4,3,2,1,0:T(8,128)S(1)}, f32[1,8,8,16,128]{4,3,2,1,0:T(8,128)S(1)}, f32[2,8,8,16,128]{4,3,2,1,0:T(8,128)S(1)}, f32[2,8,9,16,128]...) custom-call(f32[4,8,8,8,128]{4,3,2,1,0:T(8,128)S(1)} %spread_own.1.o, ...), custom_call_target="tpu_custom_call" | custom-call | tf_op jit(solution)/shard_map/descent/pallas_call | solution.py:883
  28.7 2.6 %collective-permute-start.5 = (f32[14,8,128]{2,1,0:T(8,128)S(1)}, f32[14,8,128]{2,1,0:T(8,128)S(1)}, u32[]{:S(2)}, u32[]{:S(2)}) collective-permute-start(f32[14,8,128]{2,1,0:T(8,128)S(1)} %get-tuple-element.34.coarse), channel_id=1, source_target_pairs={{8,16},{16,8},{9,17},{17,9},{10,18},{18,10},{11,19},{19,11},{12,20... | collective-permute-start | bytes 172040 | tf_op jit(solution)/shard_map/ppermute | solution.py:38
  31.3 0.1 collective-permute-start.4
  31.4 2.8 %collective-permute-done.5.coarse_odd = f32[14,8,128]{2,1,0:T(8,128)S(1)} collective-permute-done((f32[14,8,128]{2,1,0:T(8,128)S(1)}, f32[14,8,128]{2,1,0:T(8,128)S(1)}, u32[]{:S(2)}, u32[]{:S(2)}) %collective-permute-start.5) | collective-permute-done | bytes 57376 | tf_op jit(solution)/shard_map/ppermute | solution.py:38
  34.2 0.0 collective-permute-done.4.coarse_even
  34.2 4.4 %ascent.1 = f32[2,64,512]{2,1,0:T(8,128)} custom-call(f32[14,8,128]{2,1,0:T(8,128)S(1)} %get-tuple-element.34.coarse, f32[14,8,128]{2,1,0:T(8,128)S(1)} %collective-permute-done.4.coarse_even, f32[14,8,128]{2,1,0:T(8,128)S(1)} %collective-permute-done.5.coarse_odd, f32[3,8,8,16,128]{4,3,2,1,0:T(8,128)S(1)} %get-tuple-element.35.matrix0, ...), custom_call_target="tpu_custom_call" | custom-call | tf_op jit(solution)/shard_map/ascent/pallas_call | solution.py:898
Async XLA Ops:
  1.4 11.1 %collective-permute-start = (f32[4,64,128]{2,1,0:T(8,128)S(1)}, f32[4,64,128]{2,1,0:T(8,128)S(1)}, u32[]{:S(2)}, u32[]{:S(2)}) collective-permute-start(f32[4,64,128]{2,1,0:T(8,128)S(1)} %get-tuple-element.28), channel_id=1, source_target_pairs={{0,1},{1,0},{2,3},{3,2},{4,5},{5,4},{6,7},{7,6},{8,9},{9,8},{10,11... | collective-permute-start | bytes 393224 | tf_op jit(solution)/shard_map/ppermute | solution.py:38
  3.5 9.0 %collective-permute-start.1 = (f32[4,64,128]{2,1,0:T(8,128)S(1)}, f32[4,64,128]{2,1,0:T(8,128)S(1)}, u32[]{:S(2)}, u32[]{:S(2)}) collective-permute-start(f32[4,64,128]{2,1,0:T(8,128)S(1)} %get-tuple-element.29), channel_id=1, source_target_pairs={{1,2},{2,1},{3,4},{4,3},{5,6},{6,5},{9,10},{10,9},{11,12},{12,11},... | collective-permute-start | bytes 393224 | tf_op jit(solution)/shard_map/ppermute | solution.py:38
  4.2 15.5 %all-to-all-start = ((s32[32,1,512]{2,1,0:T(1,128)}), s32[32,1,512]{2,1,0:T(1,128)S(1)}, u32[]{:S(2)}, u32[]{:S(2)}) async-start(s32[32,1,512]{2,1,0:T(1,128)} %get-tuple-element.26), calls=%async_computation | async-start | bytes 131072 | tf_op jit(solution)/shard_map/all_to_all | solution.py:863
  12.6 11.4 %collective-permute-start.2 = (f32[4,32,768]{2,1,0:T(8,128)S(1)}, f32[4,32,768]{2,1,0:T(8,128)S(1)}, u32[]{:S(2)}, u32[]{:S(2)}) collective-permute-start(f32[4,32,768]{2,1,0:T(8,128)S(1)} %get-tuple-element.31), channel_id=1, source_target_pairs={{0,8},{8,0},{16,24},{24,16},{1,9},{9,1},{17,25},{25,17},{2,10},{10... | collective-permute-start | bytes 1179656 | tf_op jit(solution)/shard_map/ppermute | solution.py:38
  12.9 11.1 %collective-permute-start.3 = (f32[4,32,768]{2,1,0:T(8,128)S(1)}, f32[4,32,768]{2,1,0:T(8,128)S(1)}, u32[]{:S(2)}, u32[]{:S(2)}) collective-permute-start(f32[4,32,768]{2,1,0:T(8,128)S(1)} %get-tuple-element.32), channel_id=1, source_target_pairs={{8,16},{16,8},{9,17},{17,9},{10,18},{18,10},{11,19},{19,11},{12,20... | collective-permute-start | bytes 1179656 | tf_op jit(solution)/shard_map/ppermute | solution.py:38
  28.7 5.5 %collective-permute-start.5 = (f32[14,8,128]{2,1,0:T(8,128)S(1)}, f32[14,8,128]{2,1,0:T(8,128)S(1)}, u32[]{:S(2)}, u32[]{:S(2)}) collective-permute-start(f32[14,8,128]{2,1,0:T(8,128)S(1)} %get-tuple-element.34.coarse), channel_id=1, source_target_pairs={{8,16},{16,8},{9,17},{17,9},{10,18},{18,10},{11,19},{19,11},{12,20... | collective-permute-start | bytes 172040 | tf_op jit(solution)/shard_map/ppermute | solution.py:38
  31.3 2.9 %collective-permute-start.4 = (f32[14,8,128]{2,1,0:T(8,128)S(1)}, f32[14,8,128]{2,1,0:T(8,128)S(1)}, u32[]{:S(2)}, u32[]{:S(2)}) collective-permute-start(f32[14,8,128]{2,1,0:T(8,128)S(1)} %get-tuple-element.34.coarse), channel_id=1, source_target_pairs={{0,8},{8,0},{16,24},{24,16},{1,9},{9,1},{17,25},{25,17},{2,10},{10... | collective-permute-start | bytes 172040 | tf_op jit(solution)/shard_map/ppermute | solution.py:38

commit v8 on v7

--- a/solution.py
+++ b/solution.py
@@ -297,7 +297,7 @@
     def components(self):
         return (0,)
 
-    def make_inverse(self, row_ok, col_ok):
+    def make_inverse(self, row_ok, col_ok, source, x):
         count = self.count
 
         def pair_sums(k):
@@ -315,7 +315,10 @@
                 if k == 0:
                     value = value * col_ok
                 self.inverse[0, m, k] = value
+                for component in (0, 1):
+                    x[component, m, k] = source[component, m, k] * value
             left = here
+        close_columns(self, x)
 
 
 def inverse_of(level, component, m, k, high):
@@ -700,7 +703,8 @@
         matrix3[at] = value
 
     coarsen(level2, write3, 1)
-    for level in (level0, level1, level2):
+    level0.make_inverse(row_ok, col_ok, source0, other0)
+    for level in (level1, level2):
         level.make_inverse(row_ok, col_ok)
 
     source3 = matrix3.at[pl.ds(len(FULL), 2)]
@@ -710,7 +714,8 @@
         (level2, source2, x2, other2, None),
     )
     for level, source, x, other, target in chain:
-        start(level, other, source)
+        if level is not level0:
+            start(level, other, source)
         apply(level, other, source, x, residual=False)
         apply(level, x, source, other, residual=True)
         if target is not None:

time: 38.8 us -> 38.8 us (level)
  no operation moved by 1% of the time
where the time goes in v8:
time: 38.8 us; the launch traced here: 38.6 us
  starting transfers between devices  17.5 us (45%)
  Pallas kernels  15.9 us (41%)
  waiting for transfers between devices  5.07 us (13%)
    ppermute x6, starting transfers between devices, swapped(): return lax.ppermute(array, axis, pairs)  9.18 us
    all_to_all x1, starting transfers between devices, body(): words = lax.all_to_all(words, ('gx', 'gy'), 0, 0, tiled=True)  8.33 us
    pallas_call x1, Pallas kernels, body(): pl.pallas_call(functools.partial(down_kernel, rows=rows, cols=cols, gx=gx...  4.61 us
    pallas_call x1, Pallas kernels, body(): pl.pallas_call(functools.partial(up_kernel, rows=rows, cols=cols, gx=gx,...  4.38 us
    pallas_call x1, Pallas kernels, yield_factor(): pl.pallas_call(functools.partial(factor_kernel, rows=rows, cols=cols, gy=...  4.37 us
    ppermute x6, waiting for transfers between devices, swapped(): return lax.ppermute(array, axis, pairs)  2.82 us
    all_to_all x1, waiting for transfers between devices, body(): words = lax.all_to_all(words, ('gx', 'gy'), 0, 0, tiled=True)  2.25 us
    pallas_call x1, Pallas kernels, pack(): pl.pallas_call(functools.partial(pack_kernel, cells=rows * cols), out_sha...  1.41 us
  transfers between devices with their start and end apart: 7, of which 2 were waited for; matrix products, arithmetic and copies ran while one was open for 0% of the time, Pallas kernels for 14%

profile of v8, /device:TPU:1, one launch (start us, length us, event | category | flops | bytes accessed | tf_op | source)
XLA Modules:
  0.0 38.6 jit_solution(11759077372997092007)
XLA Ops:
  0.0 1.4 %pack.1 = (f32[4,64,512]{2,1,0:T(8,128)S(1)}, f32[4,64,128]{2,1,0:T(8,128)S(1)}, f32[4,64,128]{2,1,0:T(8,128)S(1)}, s32[32,1,512]{2,1,0:T(1,128)}) custom-call(f32[64,512]{1,0:T(8,128)} %first_lame.1, f32[64,512]{1,0:T(8,128)} %shear_modulus.1, f32[2,64,512]{2,1,0:T(8,128)} %applied_load.1, s32[1,512]{1,0:T(1,128)} %bitcast.3, s32[1,512]{1,0:T(1,128)} %bitcast.4, ...), custom_call_target="tpu_custom_call" | custom-call | tf_op jit(solution)/shard_map/pack/pallas_call | solution.py:176
  1.4 2.1 %collective-permute-start = (f32[4,64,128]{2,1,0:T(8,128)S(1)}, f32[4,64,128]{2,1,0:T(8,128)S(1)}, u32[]{:S(2)}, u32[]{:S(2)}) collective-permute-start(f32[4,64,128]{2,1,0:T(8,128)S(1)} %get-tuple-element.28), channel_id=1, source_target_pairs={{0,1},{1,0},{2,3},{3,2},{4,5},{5,4},{6,7},{7,6},{8,9},{9,8},{10,11... | collective-permute-start | bytes 393224 | tf_op jit(solution)/shard_map/ppermute | solution.py:38
  3.5 0.7 %collective-permute-start.1 = (f32[4,64,128]{2,1,0:T(8,128)S(1)}, f32[4,64,128]{2,1,0:T(8,128)S(1)}, u32[]{:S(2)}, u32[]{:S(2)}) collective-permute-start(f32[4,64,128]{2,1,0:T(8,128)S(1)} %get-tuple-element.29), channel_id=1, source_target_pairs={{1,2},{2,1},{3,4},{4,3},{5,6},{6,5},{9,10},{10,9},{11,12},{12,11},... | collective-permute-start | bytes 393224 | tf_op jit(solution)/shard_map/ppermute | solution.py:38
  4.2 8.3 %all-to-all-start = ((s32[32,1,512]{2,1,0:T(1,128)}), s32[32,1,512]{2,1,0:T(1,128)S(1)}, u32[]{:S(2)}, u32[]{:S(2)}) async-start(s32[32,1,512]{2,1,0:T(1,128)} %get-tuple-element.26), calls=%async_computation | async-start | bytes 131072 | tf_op jit(solution)/shard_map/all_to_all | solution.py:868
  12.5 0.0 collective-permute-done.even_side
  12.5 0.0 collective-permute-done.1.odd_side
  12.5 0.1 pack_rows.1
  12.6 0.3 collective-permute-start.2
  12.9 3.4 %collective-permute-start.3 = (f32[4,32,768]{2,1,0:T(8,128)S(1)}, f32[4,32,768]{2,1,0:T(8,128)S(1)}, u32[]{:S(2)}, u32[]{:S(2)}) collective-permute-start(f32[4,32,768]{2,1,0:T(8,128)S(1)} %get-tuple-element.32), channel_id=1, source_target_pairs={{8,16},{16,8},{9,17},{17,9},{10,18},{18,10},{11,19},{19,11},{12,20... | collective-permute-start | bytes 1179656 | tf_op jit(solution)/shard_map/ppermute | solution.py:38
  16.4 1.0 %spread_own.1.own = f32[4,8,8,8,128]{4,3,2,1,0:T(8,128)S(1)} custom-call(f32[4,64,512]{2,1,0:T(8,128)S(1)} %get-tuple-element.27.fields, f32[4,64,128]{2,1,0:T(8,128)S(1)} %collective-permute-done.even_side, f32[4,64,128]{2,1,0:T(8,128)S(1)} %collective-permute-done.1.odd_side), custom_call_target="tpu_custom_call" | custom-call | flops 201326592 | tf_op jit(solution)/shard_map/spread_own/pallas_call | solution.py:645
  17.4 2.2 %all-to-all-done.words = s32[32,1,512]{2,1,0:T(1,128)S(1)} async-done(((s32[32,1,512]{2,1,0:T(1,128)}), s32[32,1,512]{2,1,0:T(1,128)S(1)}, u32[]{:S(2)}, u32[]{:S(2)}) %all-to-all-start) | async-done | bytes 65568 | tf_op jit(solution)/shard_map/all_to_all | solution.py:868
  19.7 4.4 %yield_factor.1.factor = f32[8,8,16,128]{3,2,1,0:T(8,128)S(1)} custom-call(s32[32,1,512]{2,1,0:T(1,128)S(1)} %all-to-all-done.words), custom_call_target="tpu_custom_call" | custom-call | flops 3221225472 | bytes 65536 | tf_op jit(solution)/shard_map/yield_factor/pallas_call | solution.py:116
  24.0 0.0 collective-permute-done.2.even_rows
  24.1 0.0 collective-permute-done.3.odd_rows
  24.1 4.6 %descent.1 = (f32[3,8,8,16,128]{4,3,2,1,0:T(8,128)S(1)}, f32[1,8,8,16,128]{4,3,2,1,0:T(8,128)S(1)}, f32[2,8,8,16,128]{4,3,2,1,0:T(8,128)S(1)}, f32[2,8,9,16,128]...) custom-call(f32[4,8,8,8,128]{4,3,2,1,0:T(8,128)S(1)} %spread_own.1.o, ...), custom_call_target="tpu_custom_call" | custom-call | tf_op jit(solution)/shard_map/descent/pallas_call | solution.py:888
  28.7 2.6 %collective-permute-start.5 = (f32[14,8,128]{2,1,0:T(8,128)S(1)}, f32[14,8,128]{2,1,0:T(8,128)S(1)}, u32[]{:S(2)}, u32[]{:S(2)}) collective-permute-start(f32[14,8,128]{2,1,0:T(8,128)S(1)} %get-tuple-element.34.coarse), channel_id=1, source_target_pairs={{8,16},{16,8},{9,17},{17,9},{10,18},{18,10},{11,19},{19,11},{12,20... | collective-permute-start | bytes 172040 | tf_op jit(solution)/shard_map/ppermute | solution.py:38
  31.3 0.1 collective-permute-start.4
  31.4 2.8 %collective-permute-done.5.coarse_odd = f32[14,8,128]{2,1,0:T(8,128)S(1)} collective-permute-done((f32[14,8,128]{2,1,0:T(8,128)S(1)}, f32[14,8,128]{2,1,0:T(8,128)S(1)}, u32[]{:S(2)}, u32[]{:S(2)}) %collective-permute-start.5) | collective-permute-done | bytes 57376 | tf_op jit(solution)/shard_map/ppermute | solution.py:38
  34.2 0.0 collective-permute-done.4.coarse_even
  34.2 4.4 %ascent.1 = f32[2,64,512]{2,1,0:T(8,128)} custom-call(f32[14,8,128]{2,1,0:T(8,128)S(1)} %get-tuple-element.34.coarse, f32[14,8,128]{2,1,0:T(8,128)S(1)} %collective-permute-done.4.coarse_even, f32[14,8,128]{2,1,0:T(8,128)S(1)} %collective-permute-done.5.coarse_odd, f32[3,8,8,16,128]{4,3,2,1,0:T(8,128)S(1)} %get-tuple-element.35.matrix0, ...), custom_call_target="tpu_custom_call" | custom-call | tf_op jit(solution)/shard_map/ascent/pallas_call | solution.py:903
Async XLA Ops:
  1.4 11.1 %collective-permute-start = (f32[4,64,128]{2,1,0:T(8,128)S(1)}, f32[4,64,128]{2,1,0:T(8,128)S(1)}, u32[]{:S(2)}, u32[]{:S(2)}) collective-permute-start(f32[4,64,128]{2,1,0:T(8,128)S(1)} %get-tuple-element.28), channel_id=1, source_target_pairs={{0,1},{1,0},{2,3},{3,2},{4,5},{5,4},{6,7},{7,6},{8,9},{9,8},{10,11... | collective-permute-start | bytes 393224 | tf_op jit(solution)/shard_map/ppermute | solution.py:38
  3.5 9.0 %collective-permute-start.1 = (f32[4,64,128]{2,1,0:T(8,128)S(1)}, f32[4,64,128]{2,1,0:T(8,128)S(1)}, u32[]{:S(2)}, u32[]{:S(2)}) collective-permute-start(f32[4,64,128]{2,1,0:T(8,128)S(1)} %get-tuple-element.29), channel_id=1, source_target_pairs={{1,2},{2,1},{3,4},{4,3},{5,6},{6,5},{9,10},{10,9},{11,12},{12,11},... | collective-permute-start | bytes 393224 | tf_op jit(solution)/shard_map/ppermute | solution.py:38
  4.2 15.5 %all-to-all-start = ((s32[32,1,512]{2,1,0:T(1,128)}), s32[32,1,512]{2,1,0:T(1,128)S(1)}, u32[]{:S(2)}, u32[]{:S(2)}) async-start(s32[32,1,512]{2,1,0:T(1,128)} %get-tuple-element.26), calls=%async_computation | async-start | bytes 131072 | tf_op jit(solution)/shard_map/all_to_all | solution.py:868
  12.6 11.4 %collective-permute-start.2 = (f32[4,32,768]{2,1,0:T(8,128)S(1)}, f32[4,32,768]{2,1,0:T(8,128)S(1)}, u32[]{:S(2)}, u32[]{:S(2)}) collective-permute-start(f32[4,32,768]{2,1,0:T(8,128)S(1)} %get-tuple-element.31), channel_id=1, source_target_pairs={{0,8},{8,0},{16,24},{24,16},{1,9},{9,1},{17,25},{25,17},{2,10},{10... | collective-permute-start | bytes 1179656 | tf_op jit(solution)/shard_map/ppermute | solution.py:38
  12.9 11.1 %collective-permute-start.3 = (f32[4,32,768]{2,1,0:T(8,128)S(1)}, f32[4,32,768]{2,1,0:T(8,128)S(1)}, u32[]{:S(2)}, u32[]{:S(2)}) collective-permute-start(f32[4,32,768]{2,1,0:T(8,128)S(1)} %get-tuple-element.32), channel_id=1, source_target_pairs={{8,16},{16,8},{9,17},{17,9},{10,18},{18,10},{11,19},{19,11},{12,20... | collective-permute-start | bytes 1179656 | tf_op jit(solution)/shard_map/ppermute | solution.py:38
  28.7 5.5 %collective-permute-start.5 = (f32[14,8,128]{2,1,0:T(8,128)S(1)}, f32[14,8,128]{2,1,0:T(8,128)S(1)}, u32[]{:S(2)}, u32[]{:S(2)}) collective-permute-start(f32[14,8,128]{2,1,0:T(8,128)S(1)} %get-tuple-element.34.coarse), channel_id=1, source_target_pairs={{8,16},{16,8},{9,17},{17,9},{10,18},{18,10},{11,19},{19,11},{12,20... | collective-permute-start | bytes 172040 | tf_op jit(solution)/shard_map/ppermute | solution.py:38
  31.3 2.9 %collective-permute-start.4 = (f32[14,8,128]{2,1,0:T(8,128)S(1)}, f32[14,8,128]{2,1,0:T(8,128)S(1)}, u32[]{:S(2)}, u32[]{:S(2)}) collective-permute-start(f32[14,8,128]{2,1,0:T(8,128)S(1)} %get-tuple-element.34.coarse), channel_id=1, source_target_pairs={{0,8},{8,0},{16,24},{24,16},{1,9},{9,1},{17,25},{25,17},{2,10},{10... | collective-permute-start | bytes 172040 | tf_op jit(solution)/shard_map/ppermute | solution.py:38
